TPU v7x, 128 devices: a whole 4x4x4 slice. The times are simulated.
128 devices in a mesh: row: 16 (over z, y_lo, core), col: 8 (over x, y_hi).
Axes of the slice: x: 4, y: 4 (y_hi: 2, y_lo: 2; y = y_hi * 2 + y_lo), z: 4, core: 2. Of those that a mesh axis runs over, the one named last changes fastest.
Arguments:
- atom_feats: bfloat16 [32768, 128], P(('row', 'col')), may hold values from -6 to 6
- atom_gain: float32 [128], replicated, may hold values from 0.1 to 1.9
- atom_project: bfloat16 [128, 384], replicated, may hold values from -2 to 2
- atom_merge: bfloat16 [128, 128], replicated, may hold values from -0.5 to 0.5
- atom_up: bfloat16 [128, 768], replicated, may hold values from -0.5 to 0.5
- token_counts: int32 [128, 16], P(('row', 'col')), may hold values from 1 to 24, 256 in all within a row
- token_single: bfloat16 [2048, 768], P(('row', 'col')), may hold values from -6 to 6
- token_gain: float32 [768], replicated, may hold values from 0.1 to 1.9
- token_project: bfloat16 [768, 2304], replicated, may hold values from -0.21875 to 0.21875
- token_merge: bfloat16 [768, 768], replicated, may hold values from -0.21875 to 0.21875
- pair_state: bfloat16 [2048, 2048, 128], P('row', 'col'), may hold values from -6 to 6
- pair_gain: float32 [128], replicated, may hold values from 0.1 to 1.9
- bias_weight: bfloat16 [128, 16], replicated, may hold values from -5 to 5
- atom_down: bfloat16 [768, 128], replicated, may hold values from -0.21875 to 0.21875
- position_weight: bfloat16 [3, 128], replicated, may hold values from -0.5 to 0.5
- position_cotangent: float32 [3, 32768], P(None, ('row', 'col')), may hold values from -6 to 6
Outputs:
- positions: float32 [3, 32768], P(None, ('row', 'col'))
- token_update: bfloat16 [2048, 768], P(('row', 'col'))
- pair_grad: bfloat16 [2048, 2048, 128], P('row', 'col')
Inputs may be any that keep to these rules, and one draw needn't show every extreme that they name: `token_counts`: each row sums to 256, and each row holds the value 24.
All inputs are finite; a program needn't handle non-finite values.
Results may differ from a plain program's by a relative error of at most 0.013.
The roundings to bfloat16 on the way count: a program that leaves them out, or rounds other values in their place, can miss the bound.
Values may be sent and summed in bfloat16 or wider, within the bound.
No kernel may reach another device: no remote copies, remote signals or barrier semaphores. Data moves between devices by JAX's collectives and lax.ppermute only.
A program may use at most 128 MiB of HBM per device.

v0:
```python
import math

import jax
import jax.numpy as jnp
from jax import lax
from jax.sharding import PartitionSpec as P

ATOM_HEADS = 4


EPS = 1e-05
ROWS_DIMS = (((0,), (0,)), ((), ()))
COLS_DIMS = (((1,), (1,)), ((), ()))


def shifted(block, axis, distance):
    devices = range(lax.axis_size(axis))
    route = [(i - distance, i) for i in devices if i - distance in devices]
    return lax.ppermute(block, axis, route)


def combined_all(value, axis, join):
    pieces = jax.tree.map(lambda part: lax.all_gather(part, axis), value)
    head = jax.tree.map(lambda part: part[0], pieces)
    tail = jax.tree.map(lambda part: part[1:], pieces)
    so_far, _ = lax.scan(lambda so_far, share: (join(so_far, share), None), head, tail)
    return so_far


def layer_norm(values, gain):
    center = values - jnp.mean(values, axis=-1, keepdims=True)
    spread = lax.rsqrt(jnp.mean(center * center, axis=-1, keepdims=True) + EPS)
    standard = center * spread
    return (standard * gain, standard, spread)


def window_attend(queries, key_ext, value_ext, first_row, atom_total):
    blocks = queries.shape[0] // 32
    feature_width = queries.shape[1]
    head_size = feature_width // ATOM_HEADS

    def windows(extended):
        tile_rows = extended.reshape(blocks + 4, 32, feature_width)
        joined = jnp.concatenate(
            [tile_rows[offset : offset + blocks] for offset in range(4)], axis=1
        )
        return joined.reshape(blocks, 128, ATOM_HEADS, head_size)

    query_heads = queries.reshape(blocks, 32, ATOM_HEADS, head_size)
    scores = jnp.einsum(
        "bqhd,bkhd->bhqk", query_heads, windows(key_ext), preferred_element_type=jnp.float32
    ) / math.sqrt(head_size)
    position = (
        first_row
        - 48
        + 32 * jnp.arange(blocks, dtype=jnp.int32)[:, None]
        + jnp.arange(128, dtype=jnp.int32)[None, :]
    )
    inside = (position >= 0) & (position < atom_total)
    scores = jnp.where(inside[:, None, None, :], scores, -1e30)
    row_max = jnp.max(scores, axis=-1, keepdims=True)
    weights = jnp.exp(scores - row_max)
    row_total = jnp.sum(weights, axis=-1)
    mixture = jnp.einsum(
        "bhqk,bkhd->bqhd",
        weights.astype(jnp.bfloat16),
        windows(value_ext),
        preferred_element_type=jnp.float32,
    )
    mixture = mixture / jnp.transpose(row_total, (0, 2, 1))[:, :, :, None]
    return mixture.reshape(blocks * 32, feature_width).astype(jnp.bfloat16)


def merge_parts(first_part, second_part):
    max_first, total_first, acc_first = first_part
    max_second, total_second, acc_second = second_part
    joint_max = jnp.maximum(max_first, max_second)
    scale_first = jnp.exp(max_first - joint_max)
    scale_second = jnp.exp(max_second - joint_max)
    row_count, feature_width = acc_first.shape
    head_count = joint_max.shape[0]
    joint_acc = (
        acc_first.reshape(row_count, head_count, -1) * scale_first.T[:, :, None]
        + acc_second.reshape(row_count, head_count, -1) * scale_second.T[:, :, None]
    )
    return (
        joint_max,
        total_first * scale_first + total_second * scale_second,
        joint_acc.reshape(row_count, feature_width),
    )


def project_rows(normed_rows, weights):
    return jnp.dot(normed_rows, weights, preferred_element_type=jnp.float32).astype(jnp.bfloat16)


def per_device(
    atom_feats,
    atom_gain,
    atom_project,
    atom_merge,
    atom_up,
    token_counts,
    token_single,
    token_gain,
    token_project,
    token_merge,
    pair_state,
    pair_gain,
    bias_weight,
    atom_down,
    position_weight,
    position_cotangent,
):
    atom_rows, feature_width = atom_feats.shape
    device = lax.axis_index(("row", "col"))
    atom_total = atom_rows * lax.axis_size(("row", "col"))
    normed = layer_norm(atom_feats.astype(jnp.float32), atom_gain)[0].astype(jnp.bfloat16)
    projected = jnp.dot(normed, atom_project, preferred_element_type=jnp.float32).astype(
        jnp.bfloat16
    )
    queries = projected[:, :feature_width]
    key_cols = projected[:, feature_width : 2 * feature_width]
    value_cols = projected[:, 2 * feature_width :]
    left_keys, left_values = shifted(
        (key_cols[atom_rows - 48 :], value_cols[atom_rows - 48 :]), ("row", "col"), 1
    )
    right_keys, right_values = shifted((key_cols[:80], value_cols[:80]), ("row", "col"), -1)
    key_ext = jnp.concatenate([left_keys, key_cols, right_keys], axis=0)
    value_ext = jnp.concatenate([left_values, value_cols, right_values], axis=0)
    attended = window_attend(queries, key_ext, value_ext, device * atom_rows, atom_total)
    hidden = (
        atom_feats.astype(jnp.float32)
        + jnp.dot(attended, atom_merge, preferred_element_type=jnp.float32)
    ).astype(jnp.bfloat16)
    counts = token_counts[0]
    segment_count = counts.shape[0]
    ends = jnp.cumsum(counts)
    owner_local = jnp.sum(
        (jnp.arange(atom_rows, dtype=jnp.int32)[:, None] >= ends[None, :]).astype(jnp.int32), axis=1
    )
    membership = (
        owner_local[:, None] == jnp.arange(segment_count, dtype=jnp.int32)[None, :]
    ).astype(jnp.bfloat16)
    lifted = jnp.maximum(jnp.dot(hidden, atom_up, preferred_element_type=jnp.float32), 0.0).astype(
        jnp.bfloat16
    )
    sums = lax.dot_general(membership, lifted, ROWS_DIMS, preferred_element_type=jnp.float32)
    token_state = sums / counts[:, None].astype(jnp.float32) + token_single.astype(jnp.float32)
    token_normed = layer_norm(token_state, token_gain)[0].astype(jnp.bfloat16)
    token_width = token_project.shape[0]
    column = lax.axis_index("col")
    row_index = lax.axis_index("row")
    token_proj = project_rows(token_normed, token_project)
    own_query = token_proj[:, :token_width]
    own_key = token_proj[:, token_width : 2 * token_width]
    own_value = token_proj[:, 2 * token_width :]
    all_query, all_key, all_value = (
        lax.all_gather(own_query, ("row", "col"), axis=0, tiled=True),
        lax.all_gather(own_key, ("row", "col"), axis=0, tiled=True),
        lax.all_gather(own_value, ("row", "col"), axis=0, tiled=True),
    )
    query_count = segment_count * lax.axis_size("col")
    key_count = segment_count * lax.axis_size("row")
    block_query = lax.dynamic_slice_in_dim(all_query, row_index * query_count, query_count, 0)
    block_key = lax.dynamic_slice_in_dim(all_key, column * key_count, key_count, 0)
    block_value = lax.dynamic_slice_in_dim(all_value, column * key_count, key_count, 0)
    query_count = block_query.shape[0]
    key_count = block_key.shape[0]
    head_count = bias_weight.shape[1]
    head_size = token_width // head_count
    normed_pair, standard, inv_spread = layer_norm(pair_state.astype(jnp.float32), pair_gain)
    bias = jnp.einsum(
        "ijc,ch->hij",
        normed_pair.astype(jnp.bfloat16),
        bias_weight,
        preferred_element_type=jnp.float32,
    )
    query_heads = block_query.reshape(query_count, head_count, head_size)
    key_heads = block_key.reshape(key_count, head_count, head_size)
    value_heads = block_value.reshape(key_count, head_count, head_size)
    scores = (
        jnp.einsum("ihd,jhd->hij", query_heads, key_heads, preferred_element_type=jnp.float32)
        / math.sqrt(head_size)
        + bias
    )
    local_max = jnp.max(scores, axis=-1)
    weights = jnp.exp(scores - local_max[:, :, None])
    local_total = jnp.sum(weights, axis=-1)
    local_acc = jnp.einsum(
        "hij,jhd->ihd",
        weights.astype(jnp.bfloat16),
        value_heads,
        preferred_element_type=jnp.float32,
    ).reshape(query_count, token_width)
    score_max, score_total, joint_acc = combined_all(
        (local_max, local_total, local_acc), "col", merge_parts
    )
    attention = joint_acc.reshape(query_count, head_count, head_size) / score_total.T[:, :, None]
    own_attention = lax.dynamic_slice_in_dim(
        attention.reshape(query_count, token_width), column * segment_count, segment_count, 0
    )
    token_update = (
        token_state
        + jnp.dot(
            own_attention.astype(jnp.bfloat16), token_merge, preferred_element_type=jnp.float32
        )
    ).astype(jnp.bfloat16)
    lowered = jnp.dot(token_update, atom_down, preferred_element_type=jnp.float32).astype(
        jnp.bfloat16
    )
    hidden_next = (
        hidden.astype(jnp.float32)
        + jnp.dot(membership, lowered, preferred_element_type=jnp.float32)
    ).astype(jnp.bfloat16)
    positions = lax.dot_general(
        position_weight, hidden_next, COLS_DIMS, preferred_element_type=jnp.float32
    )
    grad_hidden = lax.dot_general(
        position_cotangent,
        position_weight.astype(jnp.float32),
        ROWS_DIMS,
        precision=lax.Precision.HIGHEST,
    ).astype(jnp.bfloat16)
    grad_tokens = lax.dot_general(
        membership, grad_hidden, ROWS_DIMS, preferred_element_type=jnp.float32
    ).astype(jnp.bfloat16)
    grad_update = lax.dot_general(
        grad_tokens, atom_down, COLS_DIMS, preferred_element_type=jnp.float32
    ).astype(jnp.bfloat16)
    grad_mix = lax.dot_general(
        grad_update, token_merge, COLS_DIMS, preferred_element_type=jnp.float32
    ).astype(jnp.bfloat16)
    mix_rows = lax.all_gather(grad_mix, "col", axis=0, tiled=True).reshape(
        query_count, head_count, head_size
    )
    probs = jnp.exp(scores - score_max[:, :, None]) / score_total[:, :, None]
    grad_probs = jnp.einsum(
        "ihd,jhd->hij", mix_rows, value_heads, preferred_element_type=jnp.float32
    )
    inner = jnp.einsum(
        "ihd,ihd->hi", mix_rows.astype(jnp.float32), attention, precision=lax.Precision.HIGHEST
    )
    grad_scores = probs * (grad_probs - inner[:, :, None])
    grad_normed = jnp.einsum(
        "hij,ch->ijc", grad_scores, bias_weight.astype(jnp.float32), precision=lax.Precision.HIGHEST
    )
    scaled = grad_normed * pair_gain
    first_mean = jnp.mean(scaled, axis=-1, keepdims=True)
    second_mean = jnp.mean(scaled * standard, axis=-1, keepdims=True)
    pair_grad = (inv_spread * (scaled - first_mean - standard * second_mean)).astype(jnp.bfloat16)
    return (positions, token_update, pair_grad)


def solution(mesh):
    placed = (
        P(("row", "col"), None),
        P(),
        P(),
        P(),
        P(),
        P(("row", "col"), None),
        P(("row", "col"), None),
        P(),
        P(),
        P(),
        P("row", "col", None),
        P(),
        P(),
        P(),
        P(),
        P(None, ("row", "col")),
    )
    return jax.shard_map(
        per_device,
        mesh=mesh,
        in_specs=placed,
        out_specs=(P(None, ("row", "col")), P(("row", "col"), None), P("row", "col", None)),
        check_vma=False,
    )
```

profile of v0, /device:TPU:0, one launch (start us, length us, event | category | flops | bytes accessed | tf_op | source)
XLA Modules:
  0.0 1186.9 jit_solution(15299389109649732175)
XLA Ops:
  7.2 1.1 convert_reduce_fusion.1
  8.3 1.0 fusion.65
  9.4 1.2 convolution_convert_fusion.1
  11.2 5.8 collective-permute-start
  17.0 3.2 collective-permute-start.2
  20.8 1.3 collective-permute-start.1
  22.1 1.3 collective-permute-start.3
  24.7 1.2 convert_bitcast_fusion
  26.9 1.7 reshape.181
  28.6 1.6 collective-permute-done.3
  30.2 1.9 fusion.69
  32.1 1.7 concatenate.50
  33.8 1.8 copy.85
  35.6 1.7 concatenate.51
  37.3 1.8 copy.86
  39.1 1.7 concatenate.54
  40.8 1.8 copy.88
  42.6 1.7 concatenate.53
  44.3 1.8 copy.87
  46.1 1.7 concatenate.46
  47.8 1.8 copy.83
  49.6 1.7 concatenate.47
  51.3 1.8 copy.84
  53.1 1.7 concatenate.44
  54.8 1.8 copy.82
  56.6 1.7 concatenate.43
  58.3 1.8 copy.81
  60.1 1.9 fusion.97
  62.4 1.7 fusion.29
  65.1 1.8 convert_element_type.96
  66.9 1.7 fusion.30
  68.6 2.0 fusion.98
  71.6 1.4 convolution_convert_fusion
  75.4 11.9 %copy.94 = bf16[128,256,128]{1,2,0:T(8,128)(2,1)} copy(bf16[128,256,128]{2,1,0:T(8,128)(2,1)} %param.28) | data formatting | bytes 16777216 | tf_op args[10]
  87.3 6.1 convert_reduce_fusion
  93.5 3.9 fusion.15
  97.4 3.9 fusion.16
  101.3 281.3 %all-gather.11.cloned.1.call-done = bf16[2048,768]{1,0:T(8,128)(2,1)} async-done(((bf16[16,768]{1,0:T(8,128)(2,1)}), bf16[2048,768]{1,0:T(8,128)(2,1)}) %all-gather.11.cloned.1.call-update) | async-done | bytes 3145744 | tf_op jit(solution)/shard_map/all_gather | solution.py:161
  382.6 1.0 constant_dynamic-slice_fusion.1
  383.8 306.7 %all-gather.9.cloned.1.call-done = bf16[2048,768]{1,0:T(8,128)(2,1)} async-done(((bf16[16,768]{1,0:T(8,128)(2,1)}), bf16[2048,768]{1,0:T(8,128)(2,1)}) %all-gather.9.cloned.1.call-update) | async-done | bytes 3145744 | tf_op jit(solution)/shard_map/all_gather | solution.py:160
  690.5 1.0 constant_dynamic-slice_fusion.2
  691.7 306.4 %all-gather.7.cloned.1.call-done = bf16[2048,768]{1,0:T(8,128)(2,1)} async-done(((bf16[16,768]{1,0:T(8,128)(2,1)}), bf16[2048,768]{1,0:T(8,128)(2,1)}) %all-gather.7.cloned.1.call-update) | async-done | bytes 3145744 | tf_op jit(solution)/shard_map/all_gather | solution.py:159
  999.3 3.2 fusion.99
  1005.0 1.8 convolution_convert_fusion.3
  1006.8 34.4 %all_gather.35 = bf16[128,768]{1,0:T(8,128)(2,1)S(1)} all-gather(bf16[16,768]{1,0:T(8,128)(2,1)S(1)} %convolution_convert_fusion.3), channel_id=1, replica_groups=mesh['row'=16,'col'=8] {'col'}, dimensions={0}, use_global_device_ids=true | all-gather | bytes 221184 | tf_op jit(solution)/shard_map/all_gather | solution.py:234
  1042.7 34.2 %all-gather.1 = f32[128,128]{1,0:T(8,128)S(1)} all-gather(f32[16,128]{1,0:T(8,128)S(1)} %fusion.24), channel_id=3, replica_groups=mesh['row'=16,'col'=8] {'col'}, dimensions={0}, use_global_device_ids=true | all-gather | bytes 73728 | tf_op jit(solution)/shard_map/all_gather | solution.py:23
  1077.5 34.2 %all-gather = f32[128,128]{1,0:T(8,128)S(1)} all-gather(f32[16,128]{1,0:T(8,128)S(1)} %get-tuple-element.117), channel_id=2, replica_groups=mesh['row'=16,'col'=8] {'col'}, dimensions={0}, use_global_device_ids=true | all-gather | bytes 73728 | tf_op jit(solution)/shard_map/all_gather | solution.py:23
  1111.7 1.0 slice_bitcast_fusion
  1112.9 3.6 slice.143
  1116.5 14.8 %while.14 = (s32[]{:T(128)}, f32[16,128]{1,0:T(8,128)S(1)}, f32[16,128]{1,0:T(8,128)S(1)}, f32[128,768]{0,1:T(8,128)S(1)}, f32[7,16,128]{2,1,0:T(8,128)S(1)}, /*...) while((s32[]{:T(128)}, f32[16,128]{1,0:T(8,128)S(1)}, f32[16,128]{1,0:T(8,128)S(1)}, ...), condition=%wide.region_13.14_spmd, body=%wide.region_12.13_spmd.sunk | while | flops 309250 | bytes 2875497 | solution.py:26
  1117.3 1.0 constant_dynamic-slice_fusion.5
  1119.4 1.0 constant_dynamic-slice_fusion.5
  1121.5 1.0 constant_dynamic-slice_fusion.5
  1123.6 1.0 constant_dynamic-slice_fusion.5
  1125.7 1.0 constant_dynamic-slice_fusion.5
  1127.9 1.0 constant_dynamic-slice_fusion.5
  1130.0 1.0 constant_dynamic-slice_fusion.5
  1131.4 1.9 fusion.35
  1133.3 1.1 convolution_convert_fusion.6
  1134.4 1.8 fusion.36
  1137.2 2.3 subtract_multiply_fusion
  1139.6 17.2 %multiply_reduce_fusion = (f32[128,256]{1,0:T(8,128)S(1)}, f32[128,256]{1,0:T(8,128)S(1)}, f32[128,256,128]{1,2,0:T(8,128)}) fusion(f32[128]{0:T(128)S(1)} %copy-done.12, f32[128,256]{1,0:T(8,128)S(1)} %copy-done.6, f32[128,256]{1,0:T(8,128)S(1)} %broadcast_multiply_fusion.2, bf16[128,256,128]{1,2,0:T(8,128)(2,1)} %copy.94, ...), kind=kOutput, calls=%fused_computation.25 | convolution fusion | flops 834600960 | bytes 27791872 | tf_op jit(solution)/shard_map/hij,ch->ijc/dot_general | solution.py:245
  1156.8 11.5 fusion.14
  1168.3 12.1 %copy.103 = bf16[128,256,128]{2,1,0:T(8,128)(2,1)} copy(bf16[128,256,128]{1,2,0:T(8,128)(2,1)} %fusion.14) | data formatting | bytes 16777216
  (120 shorter events, 22.8 us)
Async XLA Ops:
  7.2 64.5 %copy-start = (bf16[768,2304]{1,0:T(8,128)(2,1)S(1)}, bf16[768,2304]{1,0:T(8,128)(2,1)}, u32[]{:S(2)}) copy-start(bf16[768,2304]{1,0:T(8,128)(2,1)} %param.26) | copy-start | bytes 10616836
  7.2 375.4 %all-gather.11.cloned.1.call-start = ((), (), s32[]{:S(2)}) async-start(), calls=%async_computation.2 | async-start | bytes 3170304 | tf_op jit(solution)/shard_map/all_gather | solution.py:161
  11.2 17.4 %collective-permute-start = (bf16[48,128]{1,0:T(8,128)(2,1)}, bf16[48,128]{1,0:T(8,128)(2,1)}, u32[]{:S(2)}, u32[]{:S(2)}) collective-permute-start(bf16[48,128]{1,0:T(8,128)(2,1)} %get-tuple-element.91), channel_id=1, source_target_pairs={{0,1},{1,2},{2,3},{3,4},{4,5},{5,6},{6,7},{7,8},{8,9},{9,10},{10,1... | collective-permute-start | bytes 36872 | tf_op jit(solution)/shard_map/ppermute | solution.py:19
  17.0 11.6 collective-permute-start.2
  20.8 7.8 collective-permute-start.1
  22.1 8.1 collective-permute-start.3
  32.1 28.0 %copy-start.11 = (pred[8,128]{1,0:T(8,128)(4,1)S(1)}, pred[8,128]{1,0:T(8,128)(4,1)}, u32[]{:S(2)}) copy-start(pred[8,128]{1,0:T(8,128)(4,1)} %fusion.88) | copy-start | bytes 3076
  58.3 10.2 copy-start.14
  60.1 11.5 copy-start.8
  73.7 616.8 %all-gather.9.cloned.1.call-start = ((), (), s32[]{:S(2)}) async-start(), calls=%async_computation.1 | async-start | bytes 3170304 | tf_op jit(solution)/shard_map/all_gather | solution.py:160
  74.5 923.6 %all-gather.7.cloned.1.call-start = ((), (), s32[]{:S(2)}) async-start(), calls=%async_computation | async-start | bytes 3170304 | tf_op jit(solution)/shard_map/all_gather | solution.py:159
  75.2 1036.5 %all-gather.13.cloned.1.call-start = ((), (), s32[]{:S(2)}) async-start(), calls=%async_computation.3 | async-start | bytes 3538944 | tf_op jit(solution)/shard_map/all_gather | solution.py:23
  87.3 6.1 copy-start.2
  93.4 3.9 copy-start.12
  93.5 3.9 copy-start.13
  97.4 3.9 copy-start.5
  383.8 618.7 %copy-start.3 = (bf16[256,768]{0,1:T(8,128)(2,1)}, bf16[256,768]{0,1:T(8,128)(2,1)S(1)}, u32[]{:S(2)}) copy-start(bf16[256,768]{0,1:T(8,128)(2,1)S(1)} %copy.97) | copy-start | bytes 1179652
  999.2 5.2 copy-start.9
  999.2 5.2 copy-start.10
  999.2 5.7 copy-start.4
  1133.3 6.3 copy-start.7
  1137.2 2.4 copy-start.6
  1137.2 19.6 %slice-start = ((s8[8388608]{0:T(1024)(128)(4,1)}), s8[4194304]{0:T(1024)(128)(4,1)S(1)}, s32[]{:S(2)}) async-start(s8[8388608]{0:T(1024)(128)(4,1)} %bitcast.107), calls=%async_computation.4 | async-start | bytes 8388608
  1139.5 17.2 %slice-start.1 = ((s8[8388608]{0:T(1024)(128)(4,1)}), s8[4194304]{0:T(1024)(128)(4,1)S(1)}, s32[]{:S(2)}) async-start(s8[8388608]{0:T(1024)(128)(4,1)} %bitcast.107), calls=%async_computation.5 | async-start | bytes 8388608
  1168.3 12.1 %copy-start.1 = (bf16[768,2304]{1,0:T(8,128)(2,1)S(1)}, bf16[768,2304]{1,0:T(8,128)(2,1)}, u32[]{:S(2)}) copy-start(bf16[768,2304]{1,0:T(8,128)(2,1)} %param.26) | copy-start | bytes 10616836
Sparse Core Ops, SparseCore 0:
  73.8 308.6 all-gather.10
  384.2 306.1 all-gather.8
  692.2 305.8 all-gather.6
  1004.5 65.6 all-gather.12
where the time goes:
time: 1190 us
  waiting for transfers between devices  897 us (75%)
  blocking collectives  103 us (9%)
  local copies, waits for them, and re-layouts  78.7 us (7%)
  matrix products  44.7 us (4%)
  other arithmetic  37 us (3%)
  between operations  14.2 us (1%)
  starting transfers between devices  11.9 us (1%)
    all_gather x1, waiting for transfers between devices, per_device(): lax.all_gather(own_key, ('row', 'col'), axis=0, tiled=True)  307 us
    all_gather x1, waiting for transfers between devices, per_device(): lax.all_gather(own_query, ('row', 'col'), axis=0, tiled=True)  306 us
    all_gather x1, waiting for transfers between devices, per_device(): lax.all_gather(own_value, ('row', 'col'), axis=0, tiled=True)  281 us
    all_gather x2, blocking collectives, combined_all(): pieces = jax.tree.map(lambda part: lax.all_gather(part, axis), value)  68.4 us
    all_gather x1, blocking collectives, per_device(): lax.all_gather(grad_mix, 'col', axis=0, tiled=True)  34.4 us
    concatenate x16, local copies, waits for them, and re-layouts, windows(): jnp.concatenate([tile_rows[offset:offset + blocks] for offset in range(4)...  28 us
    unnamed x36, local copies, waits for them, and re-layouts  24.1 us
  transfers between devices with their start and end apart: 8, of which 4 were waited for; matrix products, arithmetic and copies ran while one was open for 3% of the time, Pallas kernels for 0%

commit v1 on v0

v1 whole, which is shorter than its diff:
```python
import math

import jax
import jax.numpy as jnp
from jax import lax
from jax.experimental import pallas as pl
from jax.experimental.pallas import tpu as pltpu
from jax.sharding import PartitionSpec as P

ATOM_HEADS = 4
EPS = 1e-05
NEGATIVE = -1e30
LEFT, RIGHT = 48, 80
WINDOW = 32
KEYS = 128
LANES = 128
GROUP = 8
F32 = jnp.float32
BF16 = jnp.bfloat16
NT = (((1,), (1,)), ((), ()))
TN = (((0,), (0,)), ((), ()))
MIB = 1 << 20


def iota(shape, axis):
    return lax.broadcasted_iota(jnp.int32, shape, axis)


def dot(a, b):
    return jnp.dot(a, b, preferred_element_type=F32)


def dot_nt(a, b):
    return lax.dot_general(a, b, NT, preferred_element_type=F32)


def dot_tn(a, b):
    return lax.dot_general(a, b, TN, preferred_element_type=F32)


def split(value):
    high = value.astype(BF16)
    return high, (value - high.astype(F32)).astype(BF16)


def normalize(values, gain):
    center = values - jnp.mean(values, axis=-1, keepdims=True)
    spread = lax.rsqrt(jnp.mean(center * center, axis=-1, keepdims=True) + EPS)
    return center * spread * gain


def head_mask(rows, width, heads):
    size = width // heads
    head = iota((rows, width), 0) % heads
    column = iota((rows, width), 1)
    return ((column >= head * size) & (column < (head + 1) * size)).astype(F32)


def pair_kernel(x_ref, gain_ref, weight_ref, *rest):
    bias_ref, spread_ref, standard_ref, block_ref, ones_ref = rest[-5:]
    heads = weight_ref.shape[1]
    width = x_ref.shape[2]

    @pl.when(pl.program_id(0) == 0)
    def _():
        lane = iota((heads, LANES), 1)
        repeat = (lane % heads == iota((heads, LANES), 0)).astype(BF16)
        tiled = dot(weight_ref[...], repeat)
        owner = iota((width, LANES), 1) // heads
        for i in range(GROUP):
            block_ref[i * width : (i + 1) * width, :] = jnp.where(owner == i, tiled, 0.0).astype(BF16)
        same = (iota((2 * width, 2 * width), 0) // width) == (iota((2 * width, 2 * width), 1) // width)
        ones_ref[...] = jnp.where(same, 1.0 / width, 0.0).astype(BF16)

    gain = jnp.concatenate([gain_ref[...], gain_ref[...]], axis=1)
    ones = ones_ref[...]
    keys = x_ref.shape[1]
    owner = iota((keys, LANES), 1) // heads
    bias = jnp.zeros((keys, LANES), F32)
    spread_all = jnp.zeros((keys, LANES), F32)
    for i in range(0, GROUP, 2):
        x = jnp.concatenate([x_ref[i], x_ref[i + 1]], axis=1)
        center = x.astype(F32) - dot(x, ones)
        high, low = split(center * center)
        spread = lax.rsqrt(dot(high, ones) + dot(low, ones) + EPS)
        standard = center * spread
        rounded = standard.astype(BF16)
        standard_ref[i] = rounded[:, :width]
        standard_ref[i + 1] = rounded[:, width:]
        normed = (standard * gain).astype(BF16)
        bias = bias + dot(normed, block_ref[i * width : (i + 2) * width, :])
        spread_all = jnp.where(owner == i, spread[:, :width], spread_all)
        spread_all = jnp.where(owner == i + 1, spread[:, width:], spread_all)
    bias_ref[...] = bias
    spread_ref[...] = spread_all


def pair_forward(pair, gain, weight, first, count, previous=None):
    rows, keys, width = pair.shape
    heads = weight.shape[1]
    lanes = rows * heads
    outs = (
        jax.ShapeDtypeStruct((keys, lanes), F32),
        jax.ShapeDtypeStruct((keys, lanes), F32),
        jax.ShapeDtypeStruct(pair.shape, BF16),
    )
    before = () if previous is None else tuple(previous)
    return pl.pallas_call(
        pair_kernel,
        grid=(count,),
        in_specs=[
            pl.BlockSpec((GROUP, keys, width), lambda g: (g + first, 0, 0)),
            pl.BlockSpec((1, width), lambda g: (0, 0)),
            pl.BlockSpec((width, heads), lambda g: (0, 0)),
        ]
        + [pl.BlockSpec(memory_space=pl.ANY)] * len(before),
        out_specs=(
            pl.BlockSpec((keys, LANES), lambda g: (0, g + first)),
            pl.BlockSpec((keys, LANES), lambda g: (0, g + first)),
            pl.BlockSpec((GROUP, keys, width), lambda g: (g + first, 0, 0)),
        ),
        out_shape=outs,
        scratch_shapes=[
            pltpu.VMEM((GROUP * width, LANES), BF16),
            pltpu.VMEM((2 * width, 2 * width), BF16),
        ],
        input_output_aliases={3 + i: i for i in range(len(before))},
        compiler_params=pltpu.CompilerParams(vmem_limit_bytes=24 * MIB),
        cost_estimate=pl.CostEstimate(
            flops=count * GROUP * keys * width * 800, bytes_accessed=count * GROUP * keys * width * 5, transcendentals=0
        ),
        name="pair_forward",
    )(pair, gain, weight, *before)


def atom_kernel(
    first_ref, left_ref, own_ref, right_ref, gain_ref, project_ref, merge_ref, up_ref,
    counts_ref, single_ref, token_gain_ref, weight_ref, cotangent_ref,
    hidden_ref, state_ref, send_ref, key_ref, value_ref, query_ref, attended_ref,
):
    atoms, width = own_ref.shape
    tokens = single_ref.shape[0]
    first = first_ref[0]
    feats = jnp.concatenate(
        [left_ref[atoms - LEFT :, :], own_ref[...], right_ref[:RIGHT, :]], axis=0
    )
    normed = normalize(feats.astype(F32), gain_ref[...]).astype(BF16)
    projected = dot(normed, project_ref[...]).astype(BF16)
    query_ref[...] = projected[LEFT : LEFT + atoms, :width]
    key_ref[...] = projected[:, width : 2 * width]
    value_ref[...] = projected[:, 2 * width :]
    size = width // ATOM_HEADS
    rows = ATOM_HEADS * WINDOW
    lane_head = iota((rows, width), 1) // size
    row_head = iota((rows, width), 0) // WINDOW
    mask = lane_head == row_head
    key_index = iota((rows, KEYS), 1)
    total = jnp.int32(atoms) * first_ref[1]
    for b in range(atoms // WINDOW):
        at = b * WINDOW
        queries = jnp.concatenate([query_ref[at : at + WINDOW, :]] * ATOM_HEADS, axis=0)
        queries = jnp.where(mask, queries.astype(F32), 0.0).astype(BF16)
        scores = dot_nt(queries, key_ref[at : at + KEYS, :]) / math.sqrt(size)
        position = first - LEFT + at + key_index
        scores = jnp.where((position >= 0) & (position < total), scores, NEGATIVE)
        weights = jnp.exp(scores - jnp.max(scores, axis=1, keepdims=True))
        row_total = jnp.sum(weights, axis=1, keepdims=True)
        mixture = dot(weights.astype(BF16), value_ref[at : at + KEYS, :]) / row_total
        mixture = jnp.where(mask, mixture, 0.0)
        joined = mixture[:WINDOW]
        for h in range(1, ATOM_HEADS):
            joined = joined + mixture[h * WINDOW : (h + 1) * WINDOW]
        attended_ref[at : at + WINDOW, :] = joined.astype(BF16)
    hidden = (own_ref[...].astype(F32) + dot(attended_ref[...], merge_ref[...])).astype(BF16)
    hidden_ref[...] = hidden
    lifted = jnp.maximum(dot(hidden, up_ref[...]), 0.0).astype(BF16)
    counts_row = counts_ref[...].astype(F32)
    square = jnp.broadcast_to(counts_row, (tokens, tokens))
    above = iota((tokens, tokens), 0)
    below = iota((tokens, tokens), 1)
    counts_col = jnp.sum(jnp.where(above == below, square, 0.0), axis=1, keepdims=True)
    ends = jnp.sum(jnp.where(below <= above, square, 0.0), axis=1, keepdims=True)
    atom = iota((tokens, atoms), 1).astype(F32)
    member = ((atom < ends) & (atom >= ends - counts_col)).astype(F32).astype(BF16)
    state = dot(member, lifted) / counts_col + single_ref[...].astype(F32)
    state_ref[...] = state
    token_normed = normalize(state, token_gain_ref[...]).astype(BF16)
    turned = jnp.transpose(
        jnp.concatenate([cotangent_ref[...], jnp.zeros((LANES - 3, atoms), F32)], axis=0)
    )
    position_weight = weight_ref[...].astype(F32)
    grad_hidden = turned[:, 0:1] * position_weight[0:1, :]
    for k in range(1, 3):
        grad_hidden = grad_hidden + turned[:, k : k + 1] * position_weight[k : k + 1, :]
    grad_tokens = dot(member, grad_hidden.astype(BF16)).astype(BF16)
    packed = jnp.concatenate([token_normed, grad_tokens], axis=1)
    for c in range(send_ref.shape[0]):
        send_ref[c] = packed


def whole(array):
    zeros = (0,) * array.ndim
    return pl.BlockSpec(array.shape, lambda *_: zeros)


def atom_stage(first, left, own, right, gain, project, merge, up, counts, single, token_gain, weight, cotangent, copies):
    atoms, width = own.shape
    tokens, token_width = single.shape
    arrays = (left, own, right, gain, project, merge, up, counts, single, token_gain, weight, cotangent)
    outs = (
        jax.ShapeDtypeStruct((atoms, width), BF16),
        jax.ShapeDtypeStruct((tokens, token_width), F32),
        jax.ShapeDtypeStruct((copies, tokens, token_width + width), BF16),
    )
    return pl.pallas_call(
        atom_kernel,
        grid=(1,),
        in_specs=[pl.BlockSpec(memory_space=pltpu.SMEM)] + [whole(a) for a in arrays],
        out_specs=tuple(whole(a) for a in outs),
        out_shape=outs,
        scratch_shapes=[
            pltpu.VMEM((LEFT + atoms + RIGHT, width), BF16),
            pltpu.VMEM((LEFT + atoms + RIGHT, width), BF16),
            pltpu.VMEM((atoms, width), BF16),
            pltpu.VMEM((atoms, width), BF16),
        ],
        compiler_params=pltpu.CompilerParams(vmem_limit_bytes=16 * MIB),
        cost_estimate=pl.CostEstimate(flops=400 * MIB, bytes_accessed=2 * MIB, transcendentals=0),
        name="atom_stage",
    )(first, *arrays)


def query_kernel(rows_ref, project_ref, down_ref, merge_ref, query_ref, mix_ref):
    width = project_ref.shape[0]
    rows = rows_ref[...]
    query_ref[...] = dot(rows[:, :width], project_ref[...]).astype(BF16)
    update = dot_nt(rows[:, width:], down_ref[...]).astype(BF16)
    mix_ref[...] = dot_nt(update, merge_ref[...]).astype(BF16)


def query_stage(rows, project, down, merge):
    count = rows.shape[0]
    width = project.shape[0]
    out = jax.ShapeDtypeStruct((count, width), BF16)
    return pl.pallas_call(
        query_kernel,
        grid=(1,),
        in_specs=[whole(rows), pl.BlockSpec((width, width), lambda g: (0, 0)), whole(down), whole(merge)],
        out_specs=(whole(out), whole(out)),
        out_shape=(out, out),
        compiler_params=pltpu.CompilerParams(vmem_limit_bytes=16 * MIB),
        cost_estimate=pl.CostEstimate(flops=400 * MIB, bytes_accessed=4 * MIB, transcendentals=0),
        name="query_stage",
    )(rows, project, down, merge)


def attend_kernel(
    half_ref, first_ref, second_ref, key_project_ref, value_project_ref, query_ref, mix_ref,
    bias_ref, spread_ref,
    weight_ref, grad_ref, small_ref, send_ref, key_ref, value_ref,
):
    step = pl.program_id(0)
    width = key_project_ref.shape[0]
    heads = 16
    stat_rows = 2 * 8

    @pl.when(step == 0)
    def _():
        count = first_ref.shape[0]
        swap = half_ref[0] == 1
        first = first_ref[:, :width]
        second = second_ref[:, :width]
        low = jnp.where(swap, second, first)
        high = jnp.where(swap, first, second)
        for at, rows in ((0, low), (count, high)):
            key_ref[at : at + count, :] = dot(rows, key_project_ref[...]).astype(BF16)
            value_ref[at : at + count, :] = dot(rows, value_project_ref[...]).astype(BF16)

    mask = head_mask(heads, width, heads)
    rows = query_ref.shape[0]

    def expanded(ref):
        spread_out = ref[...].astype(F32)[:, None, :] * mask[None]
        return spread_out.reshape(rows * heads, width).astype(BF16)

    keys = key_ref[...]
    values = value_ref[...]
    scores = dot_nt(keys, expanded(query_ref)) / math.sqrt(width // heads) + bias_ref[...]
    grad_probs = dot_nt(values, expanded(mix_ref))
    row_max = jnp.max(scores, axis=0, keepdims=True)
    weights = jnp.exp(scores - row_max)
    row_total = jnp.sum(weights, axis=0, keepdims=True)
    rounded = weights.astype(BF16)
    inner = jnp.sum(rounded.astype(F32) * grad_probs, axis=0, keepdims=True)
    weight_ref[...] = weights * spread_ref[...]
    grad_ref[...] = grad_probs
    small_ref[...] = (bias_ref[...] * (1.0 / LANES)).astype(BF16)
    per = rows * heads // LANES
    for k, stat in enumerate((row_max, row_total, inner)):
        for p in range(per):
            send_ref[0, pl.ds(k * stat_rows + step * per + p, 1), :] = stat[:, p * LANES : (p + 1) * LANES]
    mixture = dot_tn(rounded, values).reshape(rows, heads, width) * mask[None]
    part = jnp.sum(mixture, axis=1)
    for t in range(width // LANES):
        at = 3 * stat_rows + t * rows
        send_ref[step, at : at + rows, :] = part[:, t * LANES : (t + 1) * LANES]

    @pl.when(step == pl.num_programs(0) - 1)
    def _():
        stats = send_ref[0, : 3 * stat_rows, :]
        for c in range(1, send_ref.shape[0]):
            send_ref[c, : 3 * stat_rows, :] = stats


def attend_stage(half, first, second, project, query, mix, bias, spread, owners):
    keys, lanes = bias.shape
    count, width = query.shape
    rows = count // owners
    chunk = lanes // owners
    stat_rows = 3 * lanes // LANES
    payload = jax.ShapeDtypeStruct((owners, stat_rows + rows * width // LANES, LANES), F32)
    tile = pl.BlockSpec((keys, chunk), lambda g: (0, g))
    return pl.pallas_call(
        attend_kernel,
        grid=(owners,),
        in_specs=[
            pl.BlockSpec(memory_space=pltpu.SMEM),
            whole(first),
            whole(second),
            pl.BlockSpec((width, width), lambda g: (0, 1)),
            pl.BlockSpec((width, width), lambda g: (0, 2)),
            pl.BlockSpec((rows, width), lambda g: (g, 0)),
            pl.BlockSpec((rows, width), lambda g: (g, 0)),
            tile,
            tile,
        ],
        out_specs=(tile, tile, tile, whole(payload)),
        out_shape=(
            jax.ShapeDtypeStruct((keys, lanes), F32),
            jax.ShapeDtypeStruct((keys, lanes), F32),
            jax.ShapeDtypeStruct((keys, lanes), BF16),
            payload,
        ),
        scratch_shapes=[pltpu.VMEM((keys, width), BF16), pltpu.VMEM((keys, width), BF16)],
        compiler_params=pltpu.CompilerParams(vmem_limit_bytes=32 * MIB),
        cost_estimate=pl.CostEstimate(flops=3000 * MIB, bytes_accessed=12 * MIB, transcendentals=0),
        name="attend_stage",
    )(half, first, second, project, project, query, mix, bias, spread)


def gradient_kernel(
    weight_ref, grad_ref, small_ref, standard_ref, received_ref, own_ref, gain_ref, bias_weight_ref,
    out_ref, block_ref, ones_ref, factor_ref, inner_ref,
):
    step = pl.program_id(0)
    width, heads = bias_weight_ref.shape
    rows = factor_ref.shape[0]

    @pl.when(step == 0)
    def _():
        lane = iota((heads, LANES), 1)
        repeat = (lane % heads == iota((heads, LANES), 0)).astype(BF16)
        tiled = jnp.transpose(dot(bias_weight_ref[...], repeat)) * gain_ref[...]
        tiled = tiled - jnp.mean(tiled, axis=1, keepdims=True)
        high, low = split(tiled)
        owner = iota((LANES, width), 0) // heads
        for i in range(GROUP):
            mine = owner == i
            at = slice(i * width, (i + 1) * width)
            block_ref[:LANES, at] = jnp.where(mine, high.astype(F32), 0.0).astype(BF16)
            block_ref[LANES:, at] = jnp.where(mine, low.astype(F32), 0.0).astype(BF16)
            ones = jnp.where(mine, 1.0, 0.0).astype(BF16)
            ones_ref[:LANES, at] = ones
            ones_ref[LANES:, at] = ones
        parts = received_ref.shape[0]
        top = received_ref[0, :rows, :]
        for s in range(1, parts):
            top = jnp.maximum(top, received_ref[s, :rows, :])
        total = jnp.zeros_like(top)
        inner = jnp.zeros_like(top)
        for s in range(parts):
            scale = jnp.exp(received_ref[s, :rows, :] - top)
            total = total + scale * received_ref[s, rows : 2 * rows, :]
            inner = inner + scale * received_ref[s, 2 * rows : 3 * rows, :]
        factor_ref[...] = jnp.exp(own_ref[0, :rows, :] - top) / total
        inner_ref[...] = inner / total

    factor = factor_ref[pl.ds(step, 1), :]
    inner = inner_ref[pl.ds(step, 1), :]
    grad = weight_ref[...] * factor * (grad_ref[...] - inner)
    rounded = grad.astype(BF16)
    left = jnp.concatenate([rounded, rounded], axis=1)
    high, low = split(grad * small_ref[...].astype(F32))
    right = jnp.concatenate([high, low], axis=1)
    for i in range(0, GROUP, 2):
        at = slice(i * width, (i + 2) * width)
        direct = dot(left, block_ref[:, at])
        along = dot(right, ones_ref[:, at])
        for k in range(2):
            part = slice(k * width, (k + 1) * width)
            out_ref[i + k] = (direct[:, part] - standard_ref[i + k].astype(F32) * along[:, part]).astype(BF16)


def gradient_stage(weights, grad, small, standard, received, own, gain, bias_weight):
    rows, keys, width = standard.shape
    tile = pl.BlockSpec((keys, LANES), lambda g: (0, g))
    block = pl.BlockSpec((GROUP, keys, width), lambda g: (g, 0, 0))
    return pl.pallas_call(
        gradient_kernel,
        grid=(rows // GROUP,),
        in_specs=[tile, tile, tile, block, whole(received), whole(own), whole(gain), whole(bias_weight)],
        out_specs=block,
        out_shape=jax.ShapeDtypeStruct(standard.shape, BF16),
        scratch_shapes=[
            pltpu.VMEM((2 * LANES, GROUP * width), BF16),
            pltpu.VMEM((2 * LANES, GROUP * width), BF16),
            pltpu.VMEM((rows // GROUP, LANES), F32),
            pltpu.VMEM((rows // GROUP, LANES), F32),
        ],
        compiler_params=pltpu.CompilerParams(vmem_limit_bytes=24 * MIB),
        cost_estimate=pl.CostEstimate(flops=16000 * MIB, bytes_accessed=22 * MIB, transcendentals=0),
        name="gradient_stage",
    )(weights, grad, small, standard, received, own, gain, bias_weight)


def update_kernel(
    column_ref, received_ref, state_ref, hidden_ref, counts_ref, merge_ref, down_ref, weight_ref,
    positions_ref, update_ref,
):
    column = column_ref[0]
    tokens, width = state_ref.shape
    heads = 16
    parts = received_ref.shape[0]
    stat_rows = (received_ref.shape[1] - tokens * width // LANES) // 3
    halves = tokens // GROUP

    def stats(kind, part):
        at = kind * stat_rows + column * halves
        return [received_ref[part, pl.ds(at + p, 1), :] for p in range(halves)]

    maxima = [stats(0, s) for s in range(parts)]
    totals = [stats(1, s) for s in range(parts)]
    sub = iota((tokens, LANES), 0)
    lane = iota((tokens, LANES), 1)
    scales = [[] for _ in range(parts)]
    for p in range(halves):
        top = maxima[0][p]
        for s in range(1, parts):
            top = jnp.maximum(top, maxima[s][p])
        exps = [jnp.exp(maxima[s][p] - top) for s in range(parts)]
        total = exps[0] * totals[0][p]
        for s in range(1, parts):
            total = total + exps[s] * totals[s][p]
        for s in range(parts):
            scales[s].append(exps[s] / total)
    mine = lane // heads == sub % GROUP
    rows = []
    for s in range(parts):
        picked = jnp.zeros((tokens, LANES), F32)
        for p in range(halves):
            picked = jnp.where(sub // GROUP == p, jnp.broadcast_to(scales[s][p], (tokens, LANES)), picked)
        rows.append(jnp.where(mine, picked, 0.0))
    stacked = jnp.concatenate(rows, axis=0)
    spread_out = head_mask(LANES, width, heads).astype(BF16)
    high, low = split(stacked)
    rest = stacked - high.astype(F32) - low.astype(F32)
    scale = dot(high, spread_out) + dot(low, spread_out) + dot(rest.astype(BF16), spread_out)
    pieces = []
    for t in range(width // LANES):
        at = 3 * stat_rows + t * tokens
        piece = jnp.zeros((tokens, LANES), F32)
        for s in range(parts):
            factor = scale[s * tokens : (s + 1) * tokens, t * LANES : (t + 1) * LANES]
            piece = piece + factor * received_ref[s, at : at + tokens, :]
        pieces.append(piece.astype(BF16))
    attention = jnp.concatenate(pieces, axis=1)
    update = (state_ref[...] + dot(attention, merge_ref[...])).astype(BF16)
    update_ref[...] = update
    lowered = dot(update, down_ref[...]).astype(BF16)
    atoms = hidden_ref.shape[0]
    counts_row = counts_ref[...].astype(F32)
    square = jnp.broadcast_to(counts_row, (tokens, tokens))
    above = iota((tokens, tokens), 0)
    below = iota((tokens, tokens), 1)
    counts_col = jnp.sum(jnp.where(above == below, square, 0.0), axis=1, keepdims=True)
    ends = jnp.sum(jnp.where(below <= above, square, 0.0), axis=1, keepdims=True)
    atom = iota((tokens, atoms), 1).astype(F32)
    member = ((atom < ends) & (atom >= ends - counts_col)).astype(F32).astype(BF16)
    hidden_next = (hidden_ref[...].astype(F32) + dot_tn(member, lowered)).astype(BF16)
    positions_ref[...] = dot_nt(weight_ref[...], hidden_next)


def update_stage(column, received, state, hidden, counts, merge, down, weight):
    tokens, width = state.shape
    arrays = (received, state, hidden, counts, merge, down, weight)
    outs = (
        jax.ShapeDtypeStruct((weight.shape[0], hidden.shape[0]), F32),
        jax.ShapeDtypeStruct((tokens, width), BF16),
    )
    return pl.pallas_call(
        update_kernel,
        grid=(1,),
        in_specs=[pl.BlockSpec(memory_space=pltpu.SMEM)] + [whole(a) for a in arrays],
        out_specs=tuple(whole(a) for a in outs),
        out_shape=outs,
        compiler_params=pltpu.CompilerParams(vmem_limit_bytes=16 * MIB),
        cost_estimate=pl.CostEstimate(flops=100 * MIB, bytes_accessed=3 * MIB, transcendentals=0),
        name="update_stage",
    )(column, *arrays)


def per_device(
    atom_feats, atom_gain, atom_project, atom_merge, atom_up, token_counts, token_single, token_gain,
    token_project, token_merge, pair_state, pair_gain, bias_weight, atom_down, position_weight,
    position_cotangent,
):
    both = ("row", "col")
    rows, columns = lax.axis_size("row"), lax.axis_size("col")
    devices = rows * columns
    row, column = lax.axis_index("row"), lax.axis_index("col")
    device = row * columns + column
    atoms = atom_feats.shape[0]
    left = lax.ppermute(atom_feats, both, [(i, i + 1) for i in range(devices - 1)])
    right = lax.ppermute(atom_feats, both, [(i + 1, i) for i in range(devices - 1)])
    gain = pair_gain.reshape(1, -1)
    groups = pair_state.shape[0] // GROUP
    cut = groups // 2
    pair_first = pair_forward(pair_state, gain, bias_weight, 0, cut)
    first_atom = jnp.stack([device * atoms, devices]).astype(jnp.int32)
    hidden, state, send = atom_stage(
        first_atom, left, atom_feats, right, atom_gain.reshape(1, -1), atom_project, atom_merge, atom_up,
        token_counts, token_single, token_gain.reshape(1, -1), position_weight, position_cotangent, columns,
    )
    gathered = lax.all_to_all(send, "col", 0, 0)
    gathered = gathered.reshape(-1, gathered.shape[-1])
    per_column = rows // columns
    routes = []
    for shift in range(per_column):
        route = []
        for c in range(columns):
            for k in range(per_column):
                for m in range(columns):
                    target = m + columns * ((k + shift) % per_column)
                    route.append(((per_column * c + k) * columns + m, target * columns + c))
        routes.append(route)
    first, second = [lax.ppermute(gathered, both, route) for route in routes]
    query, mix = query_stage(gathered, token_project, atom_down, token_merge)
    bias, spread, standard = pair_forward(pair_state, gain, bias_weight, cut, groups - cut, pair_first)
    half = (row // columns).astype(jnp.int32).reshape(1)
    weights, grad, small, payload = attend_stage(
        half, first, second, token_project, query, mix, bias, spread, columns
    )
    received = lax.all_to_all(payload, "col", 0, 0)
    positions, token_update = update_stage(
        column.astype(jnp.int32).reshape(1), received, state, hidden, token_counts, token_merge, atom_down,
        position_weight,
    )
    pair_grad = gradient_stage(weights, grad, small, standard, received, payload, gain, bias_weight)
    return (positions, token_update, pair_grad)


def solution(mesh):
    placed = (
        P(("row", "col"), None), P(), P(), P(), P(), P(("row", "col"), None), P(("row", "col"), None), P(),
        P(), P(), P("row", "col", None), P(), P(), P(), P(), P(None, ("row", "col")),
    )
    return jax.shard_map(
        per_device,
        mesh=mesh,
        in_specs=placed,
        out_specs=(P(None, ("row", "col")), P(("row", "col"), None), P("row", "col", None)),
        check_vma=False,
    )
```

time: 1190 us -> 130 us (0.11)
  waiting for transfers between devices: 897 us -> 13.3 us
  blocking collectives: 103 us -> 17.9 us
  local copies, waits for them, and re-layouts: 78.7 us -> 28.9 us
  Pallas kernels: 0 us -> 48.9 us
  matrix products: 44.7 us -> 0 us
  other arithmetic: 37 us -> 0.07 us
  between operations: 14.2 us -> 0.77 us
    all_gather x4 -> x0, waiting for transfers between devices: 894 us -> none  [the longest x1 307 us: per_device(): lax.all_gather(own_key, ('row', 'col'), axis=0, tiled=True)]
    all_gather x3 -> x0, blocking collectives: 103 us -> none  [the longest x2 68.4 us: combined_all(): pieces = jax.tree.map(lambda part: lax.all_gather(part, axis), value)]
    pallas_call x0 -> x7, Pallas kernels: none -> 48.9 us  [the longest x2 22.2 us: pair_forward(): pl.pallas_call(pair_kernel, grid=(count,), in_specs=[pl.BlockSpec((GROUP,...]
    dot_general x17 -> x0, matrix products: 44.7 us -> none  [the longest x1 17.2 us: per_device(): jnp.einsum('hij,ch->ijc', grad_scores, bias_weight.astype(jnp.float32), p...]
    concatenate x16 -> x0, local copies, waits for them, and re-layouts: 28 us -> none  [windows(): jnp.concatenate([tile_rows[offset:offset + blocks] for offset in range(4)...]
    all_to_all x0 -> x1, blocking collectives: none -> 17.9 us  [per_device(): received = lax.all_to_all(payload, 'col', 0, 0)]
    reduce_sum x8 -> x0, other arithmetic: 14.2 us -> none  [the longest x2 7.15 us: layer_norm(): center = values - jnp.mean(values, axis=-1, keepdims=True)]
    convert_element_type x2 -> x0, other arithmetic: 12.8 us -> none  [the longest x1 11.5 us: per_device(): (inv_spread * (scaled - first_mean - standard * second_mean)).astype(jnp....]
  transfers between devices with their start and end apart: 8 -> 5, of which waited for: 4 -> 3; matrix products, arithmetic and copies ran while one was open for 3% -> 1% of each run, Pallas kernels for 0% -> 18%
where the time goes in v1:
time: 130 us; the launch traced here: 128 us
  Pallas kernels  48.9 us (38%)
  local copies, waits for them, and re-layouts  28.9 us (22%)
  starting transfers between devices  18.5 us (14%)
  blocking collectives  17.9 us (14%)
  waiting for transfers between devices  13.3 us (10%)
    unnamed x49, local copies, waits for them, and re-layouts  28.2 us
    pallas_call x2, Pallas kernels, pair_forward(): pl.pallas_call(pair_kernel, grid=(count,), in_specs=[pl.BlockSpec((GROUP,...  22.2 us
    all_to_all x1, blocking collectives, per_device(): received = lax.all_to_all(payload, 'col', 0, 0)  17.9 us
    pallas_call x1, Pallas kernels, gradient_stage(): pl.pallas_call(gradient_kernel, grid=(rows // GROUP,), in_specs=[tile, ti...  11.5 us
    pallas_call x1, Pallas kernels, attend_stage(): pl.pallas_call(attend_kernel, grid=(owners,), in_specs=[pl.BlockSpec(memo...  8.55 us
    all_to_all x1, waiting for transfers between devices, per_device(): gathered = lax.all_to_all(send, 'col', 0, 0)  7.5 us
    ppermute x2, starting transfers between devices, per_device(): first, second = [lax.ppermute(gathered, both, route) for route in routes]  6.39 us
    ppermute x1, waiting for transfers between devices, per_device(): lax.ppermute(atom_feats, both, [(i + 1, i) for i in range(devices - 1)])  5.68 us
  transfers between devices with their start and end apart: 5, of which 3 were waited for; matrix products, arithmetic and copies ran while one was open for 1% of the time, Pallas kernels for 18%

profile of v1, /device:TPU:0, one launch (start us, length us, event | category | flops | bytes accessed | tf_op | source)
XLA Modules:
  0.0 128.3 jit_solution(16564970162006259252)
XLA Ops:
  0.6 5.2 %collective-permute-start = (bf16[256,128]{1,0:T(8,128)(2,1)}, bf16[256,128]{1,0:T(8,128)(2,1)S(1)}, u32[]{:S(2)}, u32[]{:S(2)}) collective-permute-start(bf16[256,128]{1,0:T(8,128)(2,1)} %own_ref.1), channel_id=1, source_target_pairs={{0,1},{1,2},{2,3},{3,4},{4,5},{5,6},{6,7},{7,8},{8,9},{9,10},{10,1... | collective-permute-start | bytes 196616 | tf_op jit(solution)/shard_map/ppermute | solution.py:523
  5.8 1.3 %collective-permute-start.1 = (bf16[256,128]{1,0:T(8,128)(2,1)}, bf16[256,128]{1,0:T(8,128)(2,1)S(1)}, u32[]{:S(2)}, u32[]{:S(2)}) collective-permute-start(bf16[256,128]{1,0:T(8,128)(2,1)} %own_ref.1), channel_id=1, source_target_pairs={{1,0},{2,1},{3,2},{4,3},{5,4},{6,5},{7,6},{8,7},{9,8},{10,9},{11,1... | collective-permute-start | bytes 196616 | tf_op jit(solution)/shard_map/ppermute | solution.py:524
  7.1 0.7 reshape.27.token_gain_ref
  7.8 0.1 pad_add_fusion.first_ref
  7.9 0.1 collective-permute-done.left_ref
  8.0 5.7 %collective-permute-done.1.right_ref = bf16[256,128]{1,0:T(8,128)(2,1)S(1)} collective-permute-done((bf16[256,128]{1,0:T(8,128)(2,1)}, bf16[256,128]{1,0:T(8,128)(2,1)S(1)}, u32[]{:S(2)}, u32[]{:S(2)}) %collective-permute-start.1) | collective-permute-done | bytes 65568 | tf_op jit(solution)/shard_map/ppermute | solution.py:524
  13.7 0.7 copy-done.13
  14.4 0.7 copy-done.15
  15.0 0.0 copy-start.17
  15.0 0.9 copy-done.17
  16.0 0.0 copy-start.18
  16.0 0.9 copy-done.18
  16.9 0.0 copy-start.19
  16.9 0.8 copy-done.19
  17.7 0.0 copy-start.20
  17.7 0.8 copy-done.20
  18.5 0.0 copy-start.21
  18.5 0.7 copy-done.21
  19.2 0.0 copy-start.22
  19.2 0.7 copy-done.22
  19.9 0.7 copy-done.23
  20.5 4.2 %atom_stage.1 = (bf16[256,128]{1,0:T(8,128)(2,1)S(1)}, f32[16,768]{1,0:T(8,128)S(1)}, bf16[8,16,896]{2,1,0:T(8,128)(2,1)}) custom-call(s32[2]{0:T(128)S(1)} %pad_add_fusion.first_ref, bf16[256,128]{1,0:T(8,128)(2,1)S(1)} %collective-permute-done.left_ref, bf16[256,128]{1,0:T(8,128)(2,1)S(1)} %copy-done.19, ...), custom_call_target="tpu_custom_call" | custom-call | flops 419430400 | bytes 2097152 | tf_op jit(solution)/shard_map/atom_stage/pallas_call | solution.py:215
  24.7 5.6 %all-to-all-start = ((bf16[8,16,896]{2,1,0:T(8,128)(2,1)}), bf16[8,16,896]{2,1,0:T(8,128)(2,1)S(1)}, u32[]{:S(2)}, u32[]{:S(2)}) async-start(bf16[8,16,896]{2,1,0:T(8,128)(2,1)} %get-tuple-element.20), calls=%async_computation | async-start | bytes 458752 | tf_op jit(solution)/shard_map/all_to_all | solution.py:534
  30.3 0.8 copy.23.weight_ref.bias_weight_ref
  31.1 7.5 %all-to-all-done = bf16[8,16,896]{2,1,0:T(8,128)(2,1)S(1)} async-done(((bf16[8,16,896]{2,1,0:T(8,128)(2,1)}), bf16[8,16,896]{2,1,0:T(8,128)(2,1)S(1)}, u32[]{:S(2)}, u32[]{:S(2)}) %all-to-all-start) | async-done | bytes 229408 | tf_op jit(solution)/shard_map/all_to_all | solution.py:534
  38.6 0.7 collective-permute-start.2
  39.3 5.7 %collective-permute-start.3 = (bf16[128,896]{1,0:T(8,128)(2,1)S(1)}, bf16[128,896]{1,0:T(8,128)(2,1)S(1)}, u32[]{:S(2)}, u32[]{:S(2)}) collective-permute-start(bf16[128,896]{1,0:T(8,128)(2,1)S(1)} %bitcast.7), channel_id=1, source_target_pairs={{0,64},{1,72},{2,80},{3,88},{4,96},{5,104},{6,112},{7,120},{8,0},{... | collective-permute-start | bytes 688136 | tf_op jit(solution)/shard_map/ppermute | solution.py:546
  45.0 0.0 copy-start
  45.0 3.4 %copy-done = bf16[128,256,128]{2,1,0:T(8,128)(2,1)S(1)} copy-done((bf16[128,256,128]{2,1,0:T(8,128)(2,1)S(1)}, bf16[128,256,128]{2,1,0:T(8,128)(2,1)}, u32[]{:S(2)}) %copy-start) | copy-done | bytes 8388632
  48.4 0.0 copy-start.11
  48.4 0.7 copy-done.11
  49.1 0.0 copy-start.12
  49.1 11.1 %pair_forward.2 = (f32[256,2048]{1,0:T(8,128)S(1)}, f32[256,2048]{1,0:T(8,128)S(1)}, bf16[128,256,128]{2,1,0:T(8,128)(2,1)S(1)}) custom-call(bf16[128,256,128]{2,1,0:T(8,128)(2,1)S(1)} %copy-done, f32[1,128]{1,0:T(1,128)S(1)} %bitcast.9, bf16[128,16]{1,0:T(8,128)(2,1)S(1)} %copy.23.weight_ref.bias_weight_ref), custom_call_target="tpu_custom_call" | custom-call | flops 1677721600 | bytes 10485760 | tf_op jit(solution)/shard_map/pair_forward/pallas_call | solution.py:108
  60.2 0.0 copy-start.3
  60.2 3.4 %copy-done.3 = bf16[128,256,128]{2,1,0:T(8,128)(2,1)} copy-done((bf16[128,256,128]{2,1,0:T(8,128)(2,1)}, bf16[128,256,128]{2,1,0:T(8,128)(2,1)S(1)}, u32[]{:S(2)}) %copy-start.3) | copy-done | bytes 8388632
  63.6 0.0 copy-start.7
  63.6 1.3 %copy-done.7 = f32[256,2048]{1,0:T(8,128)} copy-done((f32[256,2048]{1,0:T(8,128)}, f32[256,2048]{1,0:T(8,128)S(1)}, u32[]{:S(2)}) %copy-start.7) | copy-done | bytes 2097176
  64.9 0.0 copy-done.12
  64.9 0.0 copy-start.1
  64.9 3.4 %copy-done.1 = bf16[128,256,128]{2,1,0:T(8,128)(2,1)S(1)} copy-done((bf16[128,256,128]{2,1,0:T(8,128)(2,1)S(1)}, bf16[128,256,128]{2,1,0:T(8,128)(2,1)}, u32[]{:S(2)}) %copy-start.1) | copy-done | bytes 8388632
  68.3 0.0 copy-start.4
  68.3 3.4 %copy-done.4 = bf16[128,256,128]{2,1,0:T(8,128)(2,1)S(1)} copy-done((bf16[128,256,128]{2,1,0:T(8,128)(2,1)S(1)}, bf16[128,256,128]{2,1,0:T(8,128)(2,1)}, u32[]{:S(2)}) %copy-start.4) | copy-done | bytes 8388632
  71.7 0.0 copy-start.8
  71.7 1.6 %copy-done.8 = f32[256,2048]{1,0:T(8,128)S(1)} copy-done((f32[256,2048]{1,0:T(8,128)S(1)}, f32[256,2048]{1,0:T(8,128)}, u32[]{:S(2)}) %copy-start.8) | copy-done | bytes 2097176
  73.3 0.0 copy-start.2
  73.3 11.1 %pair_forward.3 = (f32[256,2048]{1,0:T(8,128)S(1)}, f32[256,2048]{1,0:T(8,128)S(1)}, bf16[128,256,128]{2,1,0:T(8,128)(2,1)S(1)}) custom-call(bf16[128,256,128]{2,1,0:T(8,128)(2,1)S(1)} %copy-done.1, f32[1,128]{1,0:T(1,128)S(1)} %bitcast.10, ...), custom_call_target="tpu_custom_call", output_to_operand_aliasing={{0}: (3, {}), {1}: (4, {}), {2}: (5, {})} | custom-call | flops 1677721600 | bytes 10485760 | tf_op jit(solution)/shard_map/pair_forward/pallas_call | solution.py:108
  84.4 0.0 copy-start.5
  84.4 3.4 %copy-done.5 = bf16[128,256,128]{2,1,0:T(8,128)(2,1)} copy-done((bf16[128,256,128]{2,1,0:T(8,128)(2,1)}, bf16[128,256,128]{2,1,0:T(8,128)(2,1)S(1)}, u32[]{:S(2)}) %copy-start.5) | copy-done | bytes 8388632
  87.8 0.0 copy-done.2
  87.8 0.0 copy-done.9
  87.8 0.0 copy-done.10
  87.8 0.8 query_stage.1
  88.6 0.0 collective-permute-done.2.first_ref
  88.6 0.0 collective-permute-done.3.second_ref
  88.6 0.0 copy-start.14
  88.6 0.0 copy-start.16
  88.6 0.0 copy-start.6
  88.7 8.6 %attend_stage.1 = (f32[256,2048]{1,0:T(8,128)S(1)}, f32[256,2048]{1,0:T(8,128)S(1)}, bf16[256,2048]{1,0:T(8,128)(2,1)S(1)}, f32[8,144,128]{2,1,0:T(8,128)S(1)}) custom-call(s32[1]{0:T(128)} %bitcast.1.half_ref, bf16[128,896]{1,0:T(8,128)(2,1)S(1)} %collective-permute-done.2.first_ref, bf16[128,896]{1,0:T(8,128)(2,1)S(1)} %collective-permute-done.3.second_ref, ...), custom_call_target="tpu_custom_call" | custom-call | flops 3145728000 | bytes 12582912 | tf_op jit(solution)/shard_map/attend_stage/pallas_call | solution.py:323
  97.2 17.9 %all_to_all.10.received_ref = f32[8,144,128]{2,1,0:T(8,128)S(1)} all-to-all(f32[8,144,128]{2,1,0:T(8,128)S(1)} %get-tuple-element.28.own_ref), channel_id=1, replica_groups=mesh['row'=16,'col'=8] {'col'}, dimensions={0} | all-to-all | bytes 1179648 | tf_op jit(solution)/shard_map/all_to_all | solution.py:553
  115.1 0.0 copy-done.14
  115.1 0.0 copy-done.16
  115.1 1.7 %update_stage.1 = (f32[3,256]{1,0:T(4,128)}, bf16[16,768]{1,0:T(8,128)(2,1)}) custom-call(s32[1]{0:T(128)} %bitcast.column_ref, f32[8,144,128]{2,1,0:T(8,128)S(1)} %all_to_all.10.received_ref, f32[16,768]{1,0:T(8,128)S(1)} %get-tuple-element.29.state_ref, bf16[256,128]{1,0:T(8,128)(2,1)S(1)} %get-tuple-element.30.hidden_ref, s32[1,16]{1,0:T(1,128)S(1)} %copy-done.16, ...), custom_call_target="tpu_custom_call" | custom-call | flops 104857600 | bytes 3145728 | tf_op jit(solution)/shard_map/update_stage/pallas_call | solution.py:500
  116.8 0.0 copy-done.6
  116.8 11.5 %gradient_stage.1 = bf16[128,256,128]{2,1,0:T(8,128)(2,1)} custom-call(f32[256,2048]{1,0:T(8,128)S(1)} %get-tuple-element.33.weight_ref, f32[256,2048]{1,0:T(8,128)S(1)} %get-tuple-element.34.grad_ref, bf16[256,2048]{1,0:T(8,128)(2,1)S(1)} %get-tuple-element.35.small_ref, bf16[128,256,128]{2,1,0:T(8,128)(2,1)S(1)} %copy-done.6, ...), custom_call_target="tpu_custom_call" | custom-call | flops 16777216000 | bytes 23068672 | tf_op jit(solution)/shard_map/gradient_stage/pallas_call | solution.py:408
  (5 shorter events, 0.0 us)
Async XLA Ops:
  0.6 7.4 %collective-permute-start = (bf16[256,128]{1,0:T(8,128)(2,1)}, bf16[256,128]{1,0:T(8,128)(2,1)S(1)}, u32[]{:S(2)}, u32[]{:S(2)}) collective-permute-start(bf16[256,128]{1,0:T(8,128)(2,1)} %own_ref.1), channel_id=1, source_target_pairs={{0,1},{1,2},{2,3},{3,4},{4,5},{5,6},{6,7},{7,8},{8,9},{9,10},{10,1... | collective-permute-start | bytes 196616 | tf_op jit(solution)/shard_map/ppermute | solution.py:523
  5.8 7.9 %collective-permute-start.1 = (bf16[256,128]{1,0:T(8,128)(2,1)}, bf16[256,128]{1,0:T(8,128)(2,1)S(1)}, u32[]{:S(2)}, u32[]{:S(2)}) collective-permute-start(bf16[256,128]{1,0:T(8,128)(2,1)} %own_ref.1), channel_id=1, source_target_pairs={{1,0},{2,1},{3,2},{4,3},{5,4},{6,5},{7,6},{8,7},{9,8},{10,9},{11,1... | collective-permute-start | bytes 196616 | tf_op jit(solution)/shard_map/ppermute | solution.py:524
  13.7 0.7 copy-start.13
  14.4 0.7 copy-start.15
  15.0 0.9 copy-start.17
  16.0 0.9 copy-start.18
  16.9 0.8 copy-start.19
  17.7 0.8 copy-start.20
  18.5 0.7 copy-start.21
  19.2 0.7 copy-start.22
  19.9 0.7 copy-start.23
  24.7 13.9 %all-to-all-start = ((bf16[8,16,896]{2,1,0:T(8,128)(2,1)}), bf16[8,16,896]{2,1,0:T(8,128)(2,1)S(1)}, u32[]{:S(2)}, u32[]{:S(2)}) async-start(bf16[8,16,896]{2,1,0:T(8,128)(2,1)} %get-tuple-element.20), calls=%async_computation | async-start | bytes 458752 | tf_op jit(solution)/shard_map/all_to_all | solution.py:534
  38.6 50.0 %collective-permute-start.2 = (bf16[128,896]{1,0:T(8,128)(2,1)S(1)}, bf16[128,896]{1,0:T(8,128)(2,1)S(1)}, u32[]{:S(2)}, u32[]{:S(2)}) collective-permute-start(bf16[128,896]{1,0:T(8,128)(2,1)S(1)} %bitcast.6), channel_id=1, source_target_pairs={{0,0},{1,8},{2,16},{3,24},{4,32},{5,40},{6,48},{7,56},{8,64},{9,72... | collective-permute-start | bytes 688136 | tf_op jit(solution)/shard_map/ppermute | solution.py:546
  39.3 49.3 %collective-permute-start.3 = (bf16[128,896]{1,0:T(8,128)(2,1)S(1)}, bf16[128,896]{1,0:T(8,128)(2,1)S(1)}, u32[]{:S(2)}, u32[]{:S(2)}) collective-permute-start(bf16[128,896]{1,0:T(8,128)(2,1)S(1)} %bitcast.7), channel_id=1, source_target_pairs={{0,64},{1,72},{2,80},{3,88},{4,96},{5,104},{6,112},{7,120},{8,0},{... | collective-permute-start | bytes 688136 | tf_op jit(solution)/shard_map/ppermute | solution.py:546
  45.0 3.4 %copy-start = (bf16[128,256,128]{2,1,0:T(8,128)(2,1)S(1)}, bf16[128,256,128]{2,1,0:T(8,128)(2,1)}, u32[]{:S(2)}) copy-start(bf16[128,256,128]{2,1,0:T(8,128)(2,1)} %x_ref.3) | copy-start | bytes 25165828
  48.4 0.7 copy-start.11
  49.1 15.8 %copy-start.12 = (f32[128]{0:T(128)S(1)}, f32[128]{0:T(128)}, u32[]{:S(2)}) copy-start(f32[128]{0:T(128)} %param.27) | copy-start | bytes 1540
  60.2 3.4 %copy-start.3 = (bf16[128,256,128]{2,1,0:T(8,128)(2,1)}, bf16[128,256,128]{2,1,0:T(8,128)(2,1)S(1)}, u32[]{:S(2)}) copy-start(bf16[128,256,128]{2,1,0:T(8,128)(2,1)S(1)} %get-tuple-element.25.rest_2_) | copy-start | bytes 25165828
  63.6 1.3 %copy-start.7 = (f32[256,2048]{1,0:T(8,128)}, f32[256,2048]{1,0:T(8,128)S(1)}, u32[]{:S(2)}) copy-start(f32[256,2048]{1,0:T(8,128)S(1)} %get-tuple-element.24.rest_1_) | copy-start | bytes 6291460
  64.9 3.4 %copy-start.1 = (bf16[128,256,128]{2,1,0:T(8,128)(2,1)S(1)}, bf16[128,256,128]{2,1,0:T(8,128)(2,1)}, u32[]{:S(2)}) copy-start(bf16[128,256,128]{2,1,0:T(8,128)(2,1)} %x_ref.3) | copy-start | bytes 25165828
  68.3 3.4 %copy-start.4 = (bf16[128,256,128]{2,1,0:T(8,128)(2,1)S(1)}, bf16[128,256,128]{2,1,0:T(8,128)(2,1)}, u32[]{:S(2)}) copy-start(bf16[128,256,128]{2,1,0:T(8,128)(2,1)} %copy-done.3) | copy-start | bytes 25165828
  71.7 1.6 %copy-start.8 = (f32[256,2048]{1,0:T(8,128)S(1)}, f32[256,2048]{1,0:T(8,128)}, u32[]{:S(2)}) copy-start(f32[256,2048]{1,0:T(8,128)} %copy-done.7) | copy-start | bytes 6291460
  73.3 14.5 %copy-start.2 = (bf16[768,2304]{1,0:T(8,128)(2,1)S(1)}, bf16[768,2304]{1,0:T(8,128)(2,1)}, u32[]{:S(2)}) copy-start(bf16[768,2304]{1,0:T(8,128)(2,1)} %value_project_ref.1) | copy-start | bytes 10616836
  73.3 14.5 %copy-start.9 = (bf16[768,768]{1,0:T(8,128)(2,1)S(1)}, bf16[768,768]{1,0:T(8,128)(2,1)}, u32[]{:S(2)}) copy-start(bf16[768,768]{1,0:T(8,128)(2,1)} %merge_ref.5) | copy-start | bytes 3538948
  73.3 14.5 %copy-start.10 = (bf16[768,128]{1,0:T(8,128)(2,1)S(1)}, bf16[768,128]{1,0:T(8,128)(2,1)}, u32[]{:S(2)}) copy-start(bf16[768,128]{1,0:T(8,128)(2,1)} %down_ref.3) | copy-start | bytes 589828
  84.4 3.4 %copy-start.5 = (bf16[128,256,128]{2,1,0:T(8,128)(2,1)}, bf16[128,256,128]{2,1,0:T(8,128)(2,1)S(1)}, u32[]{:S(2)}) copy-start(bf16[128,256,128]{2,1,0:T(8,128)(2,1)S(1)} %get-tuple-element.36.standard_ref) | copy-start | bytes 25165828
  88.6 26.5 %copy-start.14 = (bf16[3,128]{1,0:T(4,128)(2,1)S(1)}, bf16[3,128]{1,0:T(4,128)(2,1)}, u32[]{:S(2)}) copy-start(bf16[3,128]{1,0:T(4,128)(2,1)} %weight_ref.5) | copy-start | bytes 2308
  88.6 26.5 %copy-start.16 = (s32[1,16]{1,0:T(1,128)S(1)}, s32[1,16]{1,0:T(1,128)}, u32[]{:S(2)}) copy-start(s32[1,16]{1,0:T(1,128)} %counts_ref.3) | copy-start | bytes 196
  88.6 28.2 %copy-start.6 = (bf16[128,256,128]{2,1,0:T(8,128)(2,1)S(1)}, bf16[128,256,128]{2,1,0:T(8,128)(2,1)}, u32[]{:S(2)}) copy-start(bf16[128,256,128]{2,1,0:T(8,128)(2,1)} %copy-done.5) | copy-start | bytes 25165828

commit v2 on v1

--- a/solution.py
+++ b/solution.py
@@ -15,6 +15,7 @@
 KEYS = 128
 LANES = 128
 GROUP = 8
+STACK = 4
 F32 = jnp.float32
 BF16 = jnp.bfloat16
 NT = (((1,), (1,)), ((), ()))
@@ -57,105 +58,104 @@
 
 
 def pair_kernel(x_ref, gain_ref, weight_ref, *rest):
-    bias_ref, spread_ref, standard_ref, block_ref, ones_ref = rest[-5:]
-    heads = weight_ref.shape[1]
+    bias_ref, spread_ref, standard_ref, block_ref, ones_ref, normed_ref = rest[-6:]
+    heads = weight_ref.shape[0]
     width = x_ref.shape[2]
 
     @pl.when(pl.program_id(0) == 0)
     def _():
         lane = iota((heads, LANES), 1)
         repeat = (lane % heads == iota((heads, LANES), 0)).astype(BF16)
-        tiled = dot(weight_ref[...], repeat)
+        tiled = dot_tn(weight_ref[...], repeat)
         owner = iota((width, LANES), 1) // heads
         for i in range(GROUP):
             block_ref[i * width : (i + 1) * width, :] = jnp.where(owner == i, tiled, 0.0).astype(BF16)
-        same = (iota((2 * width, 2 * width), 0) // width) == (iota((2 * width, 2 * width), 1) // width)
-        ones_ref[...] = jnp.where(same, 1.0 / width, 0.0).astype(BF16)
-
-    gain = jnp.concatenate([gain_ref[...], gain_ref[...]], axis=1)
-    ones = ones_ref[...]
+        ones_ref[...] = jnp.full((width, width), 1.0 / width, BF16)
+
+    gain = gain_ref[...][None, :]
     keys = x_ref.shape[1]
     owner = iota((keys, LANES), 1) // heads
-    bias = jnp.zeros((keys, LANES), F32)
-    spread_all = jnp.zeros((keys, LANES), F32)
-    for i in range(0, GROUP, 2):
-        x = jnp.concatenate([x_ref[i], x_ref[i + 1]], axis=1)
-        center = x.astype(F32) - dot(x, ones)
-        high, low = split(center * center)
-        spread = lax.rsqrt(dot(high, ones) + dot(low, ones) + EPS)
-        standard = center * spread
-        rounded = standard.astype(BF16)
-        standard_ref[i] = rounded[:, :width]
-        standard_ref[i + 1] = rounded[:, width:]
-        normed = (standard * gain).astype(BF16)
-        bias = bias + dot(normed, block_ref[i * width : (i + 2) * width, :])
-        spread_all = jnp.where(owner == i, spread[:, :width], spread_all)
-        spread_all = jnp.where(owner == i + 1, spread[:, width:], spread_all)
-    bias_ref[...] = bias
-    spread_ref[...] = spread_all
-
-
-def pair_forward(pair, gain, weight, first, count, previous=None):
+    for q in range(STACK):
+        lanes = slice(q * LANES, (q + 1) * LANES)
+        spread_all = jnp.zeros((keys, LANES), F32)
+        for i in range(GROUP):
+            x = x_ref[q * GROUP + i]
+            center = x.astype(F32) - dot(x, ones_ref[...])
+            spread = lax.rsqrt(jnp.sum(center * center, axis=1, keepdims=True) * (1.0 / width) + EPS)
+            standard = center * spread
+            standard_ref[q * GROUP + i] = standard.astype(BF16)
+            normed_ref[q * keys : (q + 1) * keys, i * width : (i + 1) * width] = (standard * gain).astype(BF16)
+            spread_all = jnp.where(owner == i, spread, spread_all)
+        spread_ref[:, lanes] = spread_all
+    bias = dot(normed_ref[...], block_ref[...])
+    for q in range(STACK):
+        bias_ref[:, q * LANES : (q + 1) * LANES] = bias[q * keys : (q + 1) * keys]
+
+
+def pair_forward(pair, gain, weight, first, count, previous=(), after=()):
     rows, keys, width = pair.shape
-    heads = weight.shape[1]
+    heads = weight.shape[0]
     lanes = rows * heads
     outs = (
         jax.ShapeDtypeStruct((keys, lanes), F32),
         jax.ShapeDtypeStruct((keys, lanes), F32),
         jax.ShapeDtypeStruct(pair.shape, BF16),
     )
-    before = () if previous is None else tuple(previous)
+    before = tuple(previous)
+    others = before + tuple(after)
     return pl.pallas_call(
         pair_kernel,
-        grid=(count,),
+        grid=(count // STACK,),
         in_specs=[
-            pl.BlockSpec((GROUP, keys, width), lambda g: (g + first, 0, 0)),
-            pl.BlockSpec((1, width), lambda g: (0, 0)),
-            pl.BlockSpec((width, heads), lambda g: (0, 0)),
+            pl.BlockSpec((STACK * GROUP, keys, width), lambda g: (g + first // STACK, 0, 0)),
+            whole(gain),
+            whole(weight),
         ]
-        + [pl.BlockSpec(memory_space=pl.ANY)] * len(before),
+        + [pl.BlockSpec(memory_space=pl.ANY)] * len(others),
         out_specs=(
-            pl.BlockSpec((keys, LANES), lambda g: (0, g + first)),
-            pl.BlockSpec((keys, LANES), lambda g: (0, g + first)),
-            pl.BlockSpec((GROUP, keys, width), lambda g: (g + first, 0, 0)),
+            pl.BlockSpec((keys, STACK * LANES), lambda g: (0, g + first // STACK)),
+            pl.BlockSpec((keys, STACK * LANES), lambda g: (0, g + first // STACK)),
+            pl.BlockSpec((STACK * GROUP, keys, width), lambda g: (g + first // STACK, 0, 0)),
         ),
         out_shape=outs,
         scratch_shapes=[
             pltpu.VMEM((GROUP * width, LANES), BF16),
-            pltpu.VMEM((2 * width, 2 * width), BF16),
+            pltpu.VMEM((width, width), BF16),
+            pltpu.VMEM((STACK * keys, GROUP * width), BF16),
         ],
         input_output_aliases={3 + i: i for i in range(len(before))},
-        compiler_params=pltpu.CompilerParams(vmem_limit_bytes=24 * MIB),
+        compiler_params=pltpu.CompilerParams(vmem_limit_bytes=56 * MIB),
         cost_estimate=pl.CostEstimate(
-            flops=count * GROUP * keys * width * 800, bytes_accessed=count * GROUP * keys * width * 5, transcendentals=0
+            flops=count * GROUP * keys * width * 5000, bytes_accessed=count * GROUP * keys * width * 5, transcendentals=0
         ),
         name="pair_forward",
-    )(pair, gain, weight, *before)
+    )(pair, gain, weight, *others)
 
 
 def atom_kernel(
-    first_ref, left_ref, own_ref, right_ref, gain_ref, project_ref, merge_ref, up_ref,
-    counts_ref, single_ref, token_gain_ref, weight_ref, cotangent_ref,
-    hidden_ref, state_ref, send_ref, key_ref, value_ref, query_ref, attended_ref,
+    left_ref, own_ref, right_ref, gain_ref, project_ref, merge_ref, up_ref,
+    counts_ref, single_ref, token_gain_ref, weight_ref, cotangent_ref, _,
+    hidden_ref, state_ref, normed_ref, send_ref, key_ref, value_ref, query_ref, attended_ref,
 ):
     atoms, width = own_ref.shape
     tokens = single_ref.shape[0]
-    first = first_ref[0]
+    rows, columns = lax.axis_size("row"), lax.axis_size("col")
+    first = (lax.axis_index("row") * columns + lax.axis_index("col")) * atoms
     feats = jnp.concatenate(
         [left_ref[atoms - LEFT :, :], own_ref[...], right_ref[:RIGHT, :]], axis=0
     )
-    normed = normalize(feats.astype(F32), gain_ref[...]).astype(BF16)
+    normed = normalize(feats.astype(F32), gain_ref[...][None, :]).astype(BF16)
     projected = dot(normed, project_ref[...]).astype(BF16)
     query_ref[...] = projected[LEFT : LEFT + atoms, :width]
     key_ref[...] = projected[:, width : 2 * width]
     value_ref[...] = projected[:, 2 * width :]
     size = width // ATOM_HEADS
-    rows = ATOM_HEADS * WINDOW
-    lane_head = iota((rows, width), 1) // size
-    row_head = iota((rows, width), 0) // WINDOW
+    stacked = ATOM_HEADS * WINDOW
+    lane_head = iota((stacked, width), 1) // size
+    row_head = iota((stacked, width), 0) // WINDOW
     mask = lane_head == row_head
-    key_index = iota((rows, KEYS), 1)
-    total = jnp.int32(atoms) * first_ref[1]
+    key_index = iota((stacked, KEYS), 1)
+    total = rows * columns * atoms
     for b in range(atoms // WINDOW):
         at = b * WINDOW
         queries = jnp.concatenate([query_ref[at : at + WINDOW, :]] * ATOM_HEADS, axis=0)
@@ -184,7 +184,8 @@
     member = ((atom < ends) & (atom >= ends - counts_col)).astype(F32).astype(BF16)
     state = dot(member, lifted) / counts_col + single_ref[...].astype(F32)
     state_ref[...] = state
-    token_normed = normalize(state, token_gain_ref[...]).astype(BF16)
+    token_normed = normalize(state, token_gain_ref[...][None, :]).astype(BF16)
+    normed_ref[...] = token_normed
     turned = jnp.transpose(
         jnp.concatenate([cotangent_ref[...], jnp.zeros((LANES - 3, atoms), F32)], axis=0)
     )
@@ -203,19 +204,21 @@
     return pl.BlockSpec(array.shape, lambda *_: zeros)
 
 
-def atom_stage(first, left, own, right, gain, project, merge, up, counts, single, token_gain, weight, cotangent, copies):
+def atom_stage(left, own, right, gain, project, merge, up, counts, single, token_gain, weight, cotangent, copies, after):
     atoms, width = own.shape
     tokens, token_width = single.shape
     arrays = (left, own, right, gain, project, merge, up, counts, single, token_gain, weight, cotangent)
     outs = (
         jax.ShapeDtypeStruct((atoms, width), BF16),
         jax.ShapeDtypeStruct((tokens, token_width), F32),
+        jax.ShapeDtypeStruct((tokens, token_width), BF16),
         jax.ShapeDtypeStruct((copies, tokens, token_width + width), BF16),
     )
     return pl.pallas_call(
         atom_kernel,
         grid=(1,),
-        in_specs=[pl.BlockSpec(memory_space=pltpu.SMEM)] + [whole(a) for a in arrays],
+        in_specs=[whole(a) for a in arrays]
+        + [pl.BlockSpec(memory_space=pl.ANY)],
         out_specs=tuple(whole(a) for a in outs),
         out_shape=outs,
         scratch_shapes=[
@@ -224,10 +227,10 @@
             pltpu.VMEM((atoms, width), BF16),
             pltpu.VMEM((atoms, width), BF16),
         ],
-        compiler_params=pltpu.CompilerParams(vmem_limit_bytes=16 * MIB),
+        compiler_params=pltpu.CompilerParams(vmem_limit_bytes=56 * MIB),
         cost_estimate=pl.CostEstimate(flops=400 * MIB, bytes_accessed=2 * MIB, transcendentals=0),
         name="atom_stage",
-    )(first, *arrays)
+    )(*arrays, after)
 
 
 def query_kernel(rows_ref, project_ref, down_ref, merge_ref, query_ref, mix_ref):
@@ -248,14 +251,14 @@
         in_specs=[whole(rows), pl.BlockSpec((width, width), lambda g: (0, 0)), whole(down), whole(merge)],
         out_specs=(whole(out), whole(out)),
         out_shape=(out, out),
-        compiler_params=pltpu.CompilerParams(vmem_limit_bytes=16 * MIB),
+        compiler_params=pltpu.CompilerParams(vmem_limit_bytes=24 * MIB),
         cost_estimate=pl.CostEstimate(flops=400 * MIB, bytes_accessed=4 * MIB, transcendentals=0),
         name="query_stage",
     )(rows, project, down, merge)
 
 
 def attend_kernel(
-    half_ref, first_ref, second_ref, key_project_ref, value_project_ref, query_ref, mix_ref,
+    rows_ref, key_project_ref, value_project_ref, query_ref, mix_ref,
     bias_ref, spread_ref,
     weight_ref, grad_ref, small_ref, send_ref, key_ref, value_ref,
 ):
@@ -266,15 +269,9 @@
 
     @pl.when(step == 0)
     def _():
-        count = first_ref.shape[0]
-        swap = half_ref[0] == 1
-        first = first_ref[:, :width]
-        second = second_ref[:, :width]
-        low = jnp.where(swap, second, first)
-        high = jnp.where(swap, first, second)
-        for at, rows in ((0, low), (count, high)):
-            key_ref[at : at + count, :] = dot(rows, key_project_ref[...]).astype(BF16)
-            value_ref[at : at + count, :] = dot(rows, value_project_ref[...]).astype(BF16)
+        rows = rows_ref[...]
+        key_ref[...] = dot(rows, key_project_ref[...]).astype(BF16)
+        value_ref[...] = dot(rows, value_project_ref[...]).astype(BF16)
 
     mask = head_mask(heads, width, heads)
     rows = query_ref.shape[0]
@@ -312,7 +309,7 @@
             send_ref[c, : 3 * stat_rows, :] = stats
 
 
-def attend_stage(half, first, second, project, query, mix, bias, spread, owners):
+def attend_stage(key_rows, project, query, mix, bias, spread, owners):
     keys, lanes = bias.shape
     count, width = query.shape
     rows = count // owners
@@ -324,9 +321,7 @@
         attend_kernel,
         grid=(owners,),
         in_specs=[
-            pl.BlockSpec(memory_space=pltpu.SMEM),
-            whole(first),
-            whole(second),
+            whole(key_rows),
             pl.BlockSpec((width, width), lambda g: (0, 1)),
             pl.BlockSpec((width, width), lambda g: (0, 2)),
             pl.BlockSpec((rows, width), lambda g: (g, 0)),
@@ -345,7 +340,7 @@
         compiler_params=pltpu.CompilerParams(vmem_limit_bytes=32 * MIB),
         cost_estimate=pl.CostEstimate(flops=3000 * MIB, bytes_accessed=12 * MIB, transcendentals=0),
         name="attend_stage",
-    )(half, first, second, project, project, query, mix, bias, spread)
+    )(key_rows, project, project, query, mix, bias, spread)
 
 
 def gradient_kernel(
@@ -353,14 +348,14 @@
     out_ref, block_ref, ones_ref, factor_ref, inner_ref,
 ):
     step = pl.program_id(0)
-    width, heads = bias_weight_ref.shape
+    heads, width = bias_weight_ref.shape
     rows = factor_ref.shape[0]
 
     @pl.when(step == 0)
     def _():
         lane = iota((heads, LANES), 1)
         repeat = (lane % heads == iota((heads, LANES), 0)).astype(BF16)
-        tiled = jnp.transpose(dot(bias_weight_ref[...], repeat)) * gain_ref[...]
+        tiled = dot_tn(repeat, bias_weight_ref[...]) * gain_ref[...][None, :]
         tiled = tiled - jnp.mean(tiled, axis=1, keepdims=True)
         high, low = split(tiled)
         owner = iota((LANES, width), 0) // heads
@@ -385,29 +380,36 @@
         factor_ref[...] = jnp.exp(own_ref[0, :rows, :] - top) / total
         inner_ref[...] = inner / total
 
-    factor = factor_ref[pl.ds(step, 1), :]
-    inner = inner_ref[pl.ds(step, 1), :]
-    grad = weight_ref[...] * factor * (grad_ref[...] - inner)
-    rounded = grad.astype(BF16)
-    left = jnp.concatenate([rounded, rounded], axis=1)
-    high, low = split(grad * small_ref[...].astype(F32))
-    right = jnp.concatenate([high, low], axis=1)
+    keys = weight_ref.shape[0]
+    lefts, rights = [], []
+    for q in range(STACK):
+        lanes = slice(q * LANES, (q + 1) * LANES)
+        factor = factor_ref[pl.ds(step * STACK + q, 1), :]
+        inner = inner_ref[pl.ds(step * STACK + q, 1), :]
+        grad = weight_ref[:, lanes] * factor * (grad_ref[:, lanes] - inner)
+        rounded = grad.astype(BF16)
+        lefts.append(jnp.concatenate([rounded, rounded], axis=1))
+        rights.append(jnp.concatenate(split(grad * small_ref[:, lanes].astype(F32)), axis=1))
+    left = jnp.concatenate(lefts, axis=0)
+    right = jnp.concatenate(rights, axis=0)
     for i in range(0, GROUP, 2):
         at = slice(i * width, (i + 2) * width)
         direct = dot(left, block_ref[:, at])
         along = dot(right, ones_ref[:, at])
-        for k in range(2):
-            part = slice(k * width, (k + 1) * width)
-            out_ref[i + k] = (direct[:, part] - standard_ref[i + k].astype(F32) * along[:, part]).astype(BF16)
+        for q in range(STACK):
+            for k in range(2):
+                part = (slice(q * keys, (q + 1) * keys), slice(k * width, (k + 1) * width))
+                r = q * GROUP + i + k
+                out_ref[r] = (direct[part] - standard_ref[r].astype(F32) * along[part]).astype(BF16)
 
 
 def gradient_stage(weights, grad, small, standard, received, own, gain, bias_weight):
     rows, keys, width = standard.shape
-    tile = pl.BlockSpec((keys, LANES), lambda g: (0, g))
-    block = pl.BlockSpec((GROUP, keys, width), lambda g: (g, 0, 0))
+    tile = pl.BlockSpec((keys, STACK * LANES), lambda g: (0, g))
+    block = pl.BlockSpec((STACK * GROUP, keys, width), lambda g: (g, 0, 0))
     return pl.pallas_call(
         gradient_kernel,
-        grid=(rows // GROUP,),
+        grid=(rows // GROUP // STACK,),
         in_specs=[tile, tile, tile, block, whole(received), whole(own), whole(gain), whole(bias_weight)],
         out_specs=block,
         out_shape=jax.ShapeDtypeStruct(standard.shape, BF16),
@@ -417,17 +419,17 @@
             pltpu.VMEM((rows // GROUP, LANES), F32),
             pltpu.VMEM((rows // GROUP, LANES), F32),
         ],
-        compiler_params=pltpu.CompilerParams(vmem_limit_bytes=24 * MIB),
+        compiler_params=pltpu.CompilerParams(vmem_limit_bytes=32 * MIB),
         cost_estimate=pl.CostEstimate(flops=16000 * MIB, bytes_accessed=22 * MIB, transcendentals=0),
         name="gradient_stage",
     )(weights, grad, small, standard, received, own, gain, bias_weight)
 
 
 def update_kernel(
-    column_ref, received_ref, state_ref, hidden_ref, counts_ref, merge_ref, down_ref, weight_ref,
+    received_ref, state_ref, hidden_ref, counts_ref, merge_ref, down_ref, weight_ref,
     positions_ref, update_ref,
 ):
-    column = column_ref[0]
+    column = lax.axis_index("col")
     tokens, width = state_ref.shape
     heads = 16
     parts = received_ref.shape[0]
@@ -490,7 +492,7 @@
     positions_ref[...] = dot_nt(weight_ref[...], hidden_next)
 
 
-def update_stage(column, received, state, hidden, counts, merge, down, weight):
+def update_stage(received, state, hidden, counts, merge, down, weight):
     tokens, width = state.shape
     arrays = (received, state, hidden, counts, merge, down, weight)
     outs = (
@@ -500,13 +502,13 @@
     return pl.pallas_call(
         update_kernel,
         grid=(1,),
-        in_specs=[pl.BlockSpec(memory_space=pltpu.SMEM)] + [whole(a) for a in arrays],
+        in_specs=[whole(a) for a in arrays],
         out_specs=tuple(whole(a) for a in outs),
         out_shape=outs,
-        compiler_params=pltpu.CompilerParams(vmem_limit_bytes=16 * MIB),
+        compiler_params=pltpu.CompilerParams(vmem_limit_bytes=24 * MIB),
         cost_estimate=pl.CostEstimate(flops=100 * MIB, bytes_accessed=3 * MIB, transcendentals=0),
         name="update_stage",
-    )(column, *arrays)
+    )(*arrays)
 
 
 def per_device(
@@ -517,45 +519,36 @@
     both = ("row", "col")
     rows, columns = lax.axis_size("row"), lax.axis_size("col")
     devices = rows * columns
-    row, column = lax.axis_index("row"), lax.axis_index("col")
-    device = row * columns + column
-    atoms = atom_feats.shape[0]
     left = lax.ppermute(atom_feats, both, [(i, i + 1) for i in range(devices - 1)])
     right = lax.ppermute(atom_feats, both, [(i + 1, i) for i in range(devices - 1)])
-    gain = pair_gain.reshape(1, -1)
+    gain = pair_gain
+    bias_turned = bias_weight.T
     groups = pair_state.shape[0] // GROUP
-    cut = groups // 2
-    pair_first = pair_forward(pair_state, gain, bias_weight, 0, cut)
-    first_atom = jnp.stack([device * atoms, devices]).astype(jnp.int32)
-    hidden, state, send = atom_stage(
-        first_atom, left, atom_feats, right, atom_gain.reshape(1, -1), atom_project, atom_merge, atom_up,
-        token_counts, token_single, token_gain.reshape(1, -1), position_weight, position_cotangent, columns,
-    )
+    cuts = (0, STACK, groups - STACK, groups)
+    pair_part = pair_forward(pair_state, gain, bias_turned, 0, cuts[1])
+    hidden, state, token_normed, send = atom_stage(
+        left, atom_feats, right, atom_gain, atom_project, atom_merge, atom_up,
+        token_counts, token_single, token_gain, position_weight, position_cotangent, columns, pair_part[0],
+    )
+    pair_part = pair_forward(pair_state, gain, bias_turned, cuts[1], cuts[2] - cuts[1], pair_part, (send,))
+    route = [(c * rows + r, r * columns + c) for r in range(rows) for c in range(columns)]
+    block = lax.ppermute(token_normed, both, route)
     gathered = lax.all_to_all(send, "col", 0, 0)
     gathered = gathered.reshape(-1, gathered.shape[-1])
-    per_column = rows // columns
-    routes = []
-    for shift in range(per_column):
-        route = []
-        for c in range(columns):
-            for k in range(per_column):
-                for m in range(columns):
-                    target = m + columns * ((k + shift) % per_column)
-                    route.append(((per_column * c + k) * columns + m, target * columns + c))
-        routes.append(route)
-    first, second = [lax.ppermute(gathered, both, route) for route in routes]
+    key_rows = lax.all_to_all(jnp.broadcast_to(block[None], (rows,) + block.shape), "row", 0, 0)
+    key_rows = key_rows.reshape(-1, key_rows.shape[-1])
     query, mix = query_stage(gathered, token_project, atom_down, token_merge)
-    bias, spread, standard = pair_forward(pair_state, gain, bias_weight, cut, groups - cut, pair_first)
-    half = (row // columns).astype(jnp.int32).reshape(1)
+    bias, spread, standard = pair_forward(
+        pair_state, gain, bias_turned, cuts[2], cuts[3] - cuts[2], pair_part, (gathered,)
+    )
     weights, grad, small, payload = attend_stage(
-        half, first, second, token_project, query, mix, bias, spread, columns
+        key_rows, token_project, query, mix, bias, spread, columns
     )
     received = lax.all_to_all(payload, "col", 0, 0)
     positions, token_update = update_stage(
-        column.astype(jnp.int32).reshape(1), received, state, hidden, token_counts, token_merge, atom_down,
-        position_weight,
-    )
-    pair_grad = gradient_stage(weights, grad, small, standard, received, payload, gain, bias_weight)
+        received, state, hidden, token_counts, token_merge, atom_down, position_weight,
+    )
+    pair_grad = gradient_stage(weights, grad, small, standard, received, payload, gain, bias_turned)
     return (positions, token_update, pair_grad)
 
 

time: 130 us -> 98.5 us (0.76)
  local copies, waits for them, and re-layouts: 28.9 us -> 10.8 us
  waiting for transfers between devices: 13.3 us -> 1.34 us
  starting transfers between devices: 18.5 us -> 25.3 us
  Pallas kernels: 48.9 us -> 43 us
  blocking collectives: 17.9 us -> 16.4 us
    unnamed x49 -> x40, local copies, waits for them, and re-layouts: 28.2 us -> 9.24 us
    all_to_all x0 -> x1, starting transfers between devices: none -> 10.3 us  [per_device(): lax.all_to_all(jnp.broadcast_to(block[None], (rows,) + block.shape), 'row...]
    all_to_all x1, waiting for transfers between devices: 7.5 us -> 0.01 us  [per_device(): gathered = lax.all_to_all(send, 'col', 0, 0)]
    pallas_call x6 -> x7, Pallas kernels: 48.1 us -> 41.3 us  [the longest x3 18 us: pair_forward(): pl.pallas_call(pair_kernel, grid=(count // STACK,), in_specs=[pl.BlockSpe...]
    ppermute x2 -> x1, starting transfers between devices: 6.39 us -> 1.98 us  [per_device(): block = lax.ppermute(token_normed, both, route)]
    ppermute x1, waiting for transfers between devices: 5.68 us -> 1.33 us  [per_device(): lax.ppermute(atom_feats, both, [(i + 1, i) for i in range(devices - 1)])]
    broadcast_in_dim x0 -> x1, local copies, waits for them, and re-layouts: none -> 1.53 us  [per_device(): jnp.broadcast_to(block[None], (rows,) + block.shape)]
    all_to_all x1, blocking collectives: 17.9 us -> 16.4 us  [per_device(): received = lax.all_to_all(payload, 'col', 0, 0)]
  transfers between devices with their start and end apart: 5 -> 5, of which waited for: 3 -> 1; matrix products, arithmetic and copies ran while one was open for 1% -> 0% of each run, Pallas kernels for 18% -> 20%
where the time goes in v2:
time: 98.5 us; the launch traced here: 97.7 us
  Pallas kernels  43 us (44%)
  starting transfers between devices  25.3 us (26%)
  blocking collectives  16.4 us (17%)
  local copies, waits for them, and re-layouts  10.8 us (11%)
  waiting for transfers between devices  1.34 us (1%)
    pallas_call x3, Pallas kernels, pair_forward(): pl.pallas_call(pair_kernel, grid=(count // STACK,), in_specs=[pl.BlockSpe...  18 us
    all_to_all x1, blocking collectives, per_device(): received = lax.all_to_all(payload, 'col', 0, 0)  16.4 us
    all_to_all x1, starting transfers between devices, per_device(): lax.all_to_all(jnp.broadcast_to(block[None], (rows,) + block.shape), 'row...  10.3 us
    pallas_call x1, Pallas kernels, attend_stage(): pl.pallas_call(attend_kernel, grid=(owners,), in_specs=[whole(key_rows),...  9.48 us
    unnamed x40, local copies, waits for them, and re-layouts  9.24 us
    pallas_call x1, Pallas kernels, gradient_stage(): pl.pallas_call(gradient_kernel, grid=(rows // GROUP // STACK,), in_specs=...  7.31 us
    all_to_all x1, starting transfers between devices, per_device(): gathered = lax.all_to_all(send, 'col', 0, 0)  6.58 us
    ppermute x1, starting transfers between devices, per_device(): lax.ppermute(atom_feats, both, [(i, i + 1) for i in range(devices - 1)])  5.19 us
  transfers between devices with their start and end apart: 5, of which 1 were waited for; matrix products, arithmetic and copies ran while one was open for 0% of the time, Pallas kernels for 20%

profile of v2, /device:TPU:0, one launch (start us, length us, event | category | flops | bytes accessed | tf_op | source)
XLA Modules:
  0.0 97.7 jit_solution(10667263021916749639)
XLA Ops:
  0.6 5.2 %collective-permute-start = (bf16[256,128]{1,0:T(8,128)(2,1)}, bf16[256,128]{1,0:T(8,128)(2,1)S(1)}, u32[]{:S(2)}, u32[]{:S(2)}) collective-permute-start(bf16[256,128]{1,0:T(8,128)(2,1)} %own_ref.1), channel_id=1, source_target_pairs={{0,1},{1,2},{2,3},{3,4},{4,5},{5,6},{6,7},{7,8},{8,9},{9,10},{10,1... | collective-permute-start | bytes 196616 | tf_op jit(solution)/shard_map/ppermute | solution.py:522
  5.8 1.3 %collective-permute-start.1 = (bf16[256,128]{1,0:T(8,128)(2,1)}, bf16[256,128]{1,0:T(8,128)(2,1)S(1)}, u32[]{:S(2)}, u32[]{:S(2)}) collective-permute-start(bf16[256,128]{1,0:T(8,128)(2,1)} %own_ref.1), channel_id=1, source_target_pairs={{1,0},{2,1},{3,2},{4,3},{5,4},{6,5},{7,6},{8,7},{9,8},{10,9},{11,1... | collective-permute-start | bytes 196616 | tf_op jit(solution)/shard_map/ppermute | solution.py:523
  7.1 5.2 %pair_forward.3 = (f32[256,2048]{1,0:T(8,128)}, f32[256,2048]{1,0:T(8,128)}, bf16[128,256,128]{2,1,0:T(8,128)(2,1)}) custom-call(bf16[128,256,128]{2,1,0:T(8,128)(2,1)} %x_ref.5, f32[128]{0:T(128)} %gain_ref.9, bf16[16,128]{1,0:T(8,128)(2,1)} %bitcast.3), custom_call_target="tpu_custom_call" | custom-call | flops 5242880000 | bytes 5242880 | tf_op jit(solution)/shard_map/pair_forward/pallas_call | solution.py:106
  12.4 0.0 collective-permute-done.left_ref
  12.4 0.0 copy-start.18
  12.4 1.3 %collective-permute-done.1.right_ref = bf16[256,128]{1,0:T(8,128)(2,1)S(1)} collective-permute-done((bf16[256,128]{1,0:T(8,128)(2,1)}, bf16[256,128]{1,0:T(8,128)(2,1)S(1)}, u32[]{:S(2)}, u32[]{:S(2)}) %collective-permute-start.1) | collective-permute-done | bytes 65568 | tf_op jit(solution)/shard_map/ppermute | solution.py:523
  13.7 0.0 copy-start.19
  13.7 0.0 copy-done.18
  13.7 0.6 copy-done.19
  14.3 4.8 %atom_stage.1 = (bf16[256,128]{1,0:T(8,128)(2,1)}, f32[16,768]{1,0:T(8,128)}, bf16[16,768]{1,0:T(8,128)(2,1)}, bf16[8,16,896]{2,1,0:T(8,128)(2,1)}) custom-call(bf16[256,128]{1,0:T(8,128)(2,1)} %copy-done.18, bf16[256,128]{1,0:T(8,128)(2,1)} %own_ref.1, bf16[256,128]{1,0:T(8,128)(2,1)} %copy-done.19, f32[128]{0:T(128)} %gain_ref.6, ...), custom_call_target="tpu_custom_call" | custom-call | flops 419430400 | bytes 2097152 | tf_op jit(solution)/shard_map/atom_stage/pallas_call | solution.py:217
  19.1 6.6 %all-to-all-start.1 = ((bf16[8,16,896]{2,1,0:T(8,128)(2,1)}), bf16[8,16,896]{2,1,0:T(8,128)(2,1)}, u32[]{:S(2)}, u32[]{:S(2)}) async-start(bf16[8,16,896]{2,1,0:T(8,128)(2,1)} %get-tuple-element.26.rest_3_), calls=%async_computation.1 | async-start | bytes 458752 | tf_op jit(solution)/shard_map/all_to_all | solution.py:536
  25.7 2.0 %collective-permute-start.2 = (bf16[16,768]{1,0:T(8,128)(2,1)}, bf16[16,768]{1,0:T(8,128)(2,1)}, u32[]{:S(2)}, u32[]{:S(2)}) collective-permute-start(bf16[16,768]{1,0:T(8,128)(2,1)} %get-tuple-element.25), channel_id=1, source_target_pairs={{0,0},{16,1},{32,2},{48,3},{64,4},{80,5},{96,6},{112,7},{1,8},{17,... | collective-permute-start | bytes 73736 | tf_op jit(solution)/shard_map/ppermute | solution.py:535
  27.7 0.0 copy-start
  27.7 7.6 %pair_forward.4 = (f32[256,2048]{1,0:T(8,128)}, f32[256,2048]{1,0:T(8,128)}, bf16[128,256,128]{2,1,0:T(8,128)(2,1)}) custom-call(bf16[128,256,128]{2,1,0:T(8,128)(2,1)} %x_ref.5, f32[128]{0:T(128)} %gain_ref.9, bf16[16,128]{1,0:T(8,128)(2,1)} %bitcast.4, ...), custom_call_target="tpu_custom_call", output_to_operand_aliasing={{0}: (3, {}), {1}: (4, {}), {2}: (5, {})} | custom-call | flops 10485760000 | bytes 10485760 | tf_op jit(solution)/shard_map/pair_forward/pallas_call | solution.py:106
  35.2 0.0 collective-permute-done.2
  35.2 0.0 all-to-all-done.1
  35.3 1.5 %broadcast_in_dim.2 = bf16[16,16,768]{2,1,0:T(8,128)(2,1)} broadcast(bf16[16,768]{1,0:T(8,128)(2,1)} %collective-permute-done.2), dimensions={1,2} | broadcast | bytes 417792 | tf_op jit(solution)/shard_map/broadcast_in_dim | solution.py:538
  36.8 10.3 %all-to-all-start = ((bf16[16,16,768]{2,1,0:T(8,128)(2,1)}), bf16[16,16,768]{2,1,0:T(8,128)(2,1)}, u32[]{:S(2)}, u32[]{:S(2)}) async-start(bf16[16,16,768]{2,1,0:T(8,128)(2,1)} %broadcast_in_dim.2), calls=%async_computation | async-start | bytes 786432 | tf_op jit(solution)/shard_map/all_to_all | solution.py:538
  47.1 0.0 copy-done
  47.1 0.0 copy-start.4
  47.1 1.3 %copy-done.4 = bf16[768,768]{1,0:T(8,128)(2,1)S(1)} copy-done((bf16[768,768]{1,0:T(8,128)(2,1)S(1)}, bf16[768,768]{1,0:T(8,128)(2,1)}, u32[]{:S(2)}) %copy-start.4) | copy-done | bytes 1179672
  48.4 0.0 copy-start.6
  48.4 0.9 copy-done.6
  49.3 1.7 %query_stage.1 = (bf16[128,768]{1,0:T(8,128)(2,1)S(1)}, bf16[128,768]{1,0:T(8,128)(2,1)S(1)}) custom-call(bf16[128,896]{1,0:T(8,128)(2,1)} %bitcast.2.rows_ref.rest_3_, bf16[768,2304]{1,0:T(8,128)(2,1)S(1)} %copy-done, bf16[768,128]{1,0:T(8,128)(2,1)S(1)} %copy-done.6, bf16[768,768]{1,0:T(8,128)(2,1)S(1)} %copy-done.4), custom_call_target="tpu_custom_call" | custom-call | flops 419430400 | bytes 4194304 | tf_op jit(solution)/shard_map/query_stage/pallas_call | solution.py:248
  51.0 0.0 copy-start.8
  51.0 0.7 copy-done.8
  51.7 0.0 copy-start.10
  51.7 0.7 copy-done.10
  52.4 5.2 %pair_forward.5 = (f32[256,2048]{1,0:T(8,128)}, f32[256,2048]{1,0:T(8,128)}, bf16[128,256,128]{2,1,0:T(8,128)(2,1)}) custom-call(bf16[128,256,128]{2,1,0:T(8,128)(2,1)} %x_ref.5, f32[128]{0:T(128)} %gain_ref.9, bf16[16,128]{1,0:T(8,128)(2,1)} %bitcast.5, ...), custom_call_target="tpu_custom_call", output_to_operand_aliasing={{0}: (3, {}), {1}: (4, {}), {2}: (5, {})} | custom-call | flops 5242880000 | bytes 5242880 | tf_op jit(solution)/shard_map/pair_forward/pallas_call | solution.py:106
  57.6 0.0 all-to-all-done
  57.6 0.0 copy-start.1
  57.6 1.6 %copy-done.1 = f32[256,2048]{1,0:T(8,128)S(1)} copy-done((f32[256,2048]{1,0:T(8,128)S(1)}, f32[256,2048]{1,0:T(8,128)}, u32[]{:S(2)}) %copy-start.1) | copy-done | bytes 2097176
  59.2 0.0 copy-start.3
  59.2 1.6 %copy-done.3 = f32[256,2048]{1,0:T(8,128)S(1)} copy-done((f32[256,2048]{1,0:T(8,128)S(1)}, f32[256,2048]{1,0:T(8,128)}, u32[]{:S(2)}) %copy-start.3) | copy-done | bytes 2097176
  60.8 0.0 copy-start.9
  60.8 0.9 copy-done.9
  61.7 0.0 copy-start.11
  61.7 0.9 copy-done.11
  62.6 0.0 copy-start.5
  62.7 0.0 copy-start.7
  62.7 0.0 copy-start.12
  62.7 0.0 copy-start.13
  62.7 0.0 copy-start.15
  62.7 0.0 copy-start.16
  62.7 0.0 copy-start.2
  62.7 9.5 %attend_stage.1 = (f32[256,2048]{1,0:T(8,128)S(1)}, f32[256,2048]{1,0:T(8,128)S(1)}, bf16[256,2048]{1,0:T(8,128)(2,1)S(1)}, f32[8,144,128]{2,1,0:T(8,128)S(1)}) custom-call(bf16[256,768]{1,0:T(8,128)(2,1)} %bitcast.1.rows_ref, bf16[768,2304]{1,0:T(8,128)(2,1)S(1)} %copy-done, bf16[768,2304]{1,0:T(8,128)(2,1)S(1)} %copy-done, bf16[128,768]{1,0:T(8,128)(2,1)S(1)} %copy-done.9, ...), custom_call_target="tpu_custom_call" | custom-call | flops 3145728000 | bytes 12582912 | tf_op jit(solution)/shard_map/attend_stage/pallas_call | solution.py:320
  72.2 0.0 copy-start.14
  72.2 0.0 copy-start.17
  72.2 16.4 %all_to_all.15.received_ref = f32[8,144,128]{2,1,0:T(8,128)S(1)} all-to-all(f32[8,144,128]{2,1,0:T(8,128)S(1)} %get-tuple-element.36.own_ref), channel_id=1, replica_groups=mesh['row'=16,'col'=8] {'col'}, dimensions={0} | all-to-all | bytes 1179648 | tf_op jit(solution)/shard_map/all_to_all | solution.py:547
  88.7 0.0 copy-done.5
  88.7 0.0 copy-done.7
  88.7 0.0 copy-done.12
  88.7 0.0 copy-done.13
  88.7 0.0 copy-done.15
  88.7 0.0 copy-done.16
  88.7 1.7 %update_stage.1 = (f32[3,256]{1,0:T(4,128)}, bf16[16,768]{1,0:T(8,128)(2,1)}) custom-call(f32[8,144,128]{2,1,0:T(8,128)S(1)} %all_to_all.15.received_ref, f32[16,768]{1,0:T(8,128)S(1)} %copy-done.13, bf16[256,128]{1,0:T(8,128)(2,1)S(1)} %copy-done.12, s32[1,16]{1,0:T(1,128)S(1)} %copy-done.16, bf16[768,768]{1,0:T(8,128)(2,1)S(1)} %copy-done.5, ...), custom_call_target="tpu_custom_call" | custom-call | flops 104857600 | bytes 3145728 | tf_op jit(solution)/shard_map/update_stage/pallas_call | solution.py:502
  90.4 0.0 copy-done.2
  90.4 0.0 copy-done.14
  90.4 0.0 copy-done.17
  90.4 7.3 %gradient_stage.1 = bf16[128,256,128]{2,1,0:T(8,128)(2,1)} custom-call(f32[256,2048]{1,0:T(8,128)S(1)} %get-tuple-element.41.weight_ref, f32[256,2048]{1,0:T(8,128)S(1)} %get-tuple-element.42.grad_ref, bf16[256,2048]{1,0:T(8,128)(2,1)S(1)} %get-tuple-element.43.small_ref, bf16[128,256,128]{2,1,0:T(8,128)(2,1)S(1)} %copy-done.2, ...), custom_call_target="tpu_custom_call" | custom-call | flops 16777216000 | bytes 23068672 | tf_op jit(solution)/shard_map/gradient_stage/pallas_call | solution.py:410
Async XLA Ops:
  0.6 11.7 %collective-permute-start = (bf16[256,128]{1,0:T(8,128)(2,1)}, bf16[256,128]{1,0:T(8,128)(2,1)S(1)}, u32[]{:S(2)}, u32[]{:S(2)}) collective-permute-start(bf16[256,128]{1,0:T(8,128)(2,1)} %own_ref.1), channel_id=1, source_target_pairs={{0,1},{1,2},{2,3},{3,4},{4,5},{5,6},{6,7},{7,8},{8,9},{9,10},{10,1... | collective-permute-start | bytes 196616 | tf_op jit(solution)/shard_map/ppermute | solution.py:522
  5.8 7.9 %collective-permute-start.1 = (bf16[256,128]{1,0:T(8,128)(2,1)}, bf16[256,128]{1,0:T(8,128)(2,1)S(1)}, u32[]{:S(2)}, u32[]{:S(2)}) collective-permute-start(bf16[256,128]{1,0:T(8,128)(2,1)} %own_ref.1), channel_id=1, source_target_pairs={{1,0},{2,1},{3,2},{4,3},{5,4},{6,5},{7,6},{8,7},{9,8},{10,9},{11,1... | collective-permute-start | bytes 196616 | tf_op jit(solution)/shard_map/ppermute | solution.py:523
  12.4 1.3 %copy-start.18 = (bf16[256,128]{1,0:T(8,128)(2,1)}, bf16[256,128]{1,0:T(8,128)(2,1)S(1)}, u32[]{:S(2)}) copy-start(bf16[256,128]{1,0:T(8,128)(2,1)S(1)} %collective-permute-done.left_ref) | copy-start | bytes 196612
  13.7 0.6 copy-start.19
  19.1 16.1 %all-to-all-start.1 = ((bf16[8,16,896]{2,1,0:T(8,128)(2,1)}), bf16[8,16,896]{2,1,0:T(8,128)(2,1)}, u32[]{:S(2)}, u32[]{:S(2)}) async-start(bf16[8,16,896]{2,1,0:T(8,128)(2,1)} %get-tuple-element.26.rest_3_), calls=%async_computation.1 | async-start | bytes 458752 | tf_op jit(solution)/shard_map/all_to_all | solution.py:536
  25.7 9.5 %collective-permute-start.2 = (bf16[16,768]{1,0:T(8,128)(2,1)}, bf16[16,768]{1,0:T(8,128)(2,1)}, u32[]{:S(2)}, u32[]{:S(2)}) collective-permute-start(bf16[16,768]{1,0:T(8,128)(2,1)} %get-tuple-element.25), channel_id=1, source_target_pairs={{0,0},{16,1},{32,2},{48,3},{64,4},{80,5},{96,6},{112,7},{1,8},{17,... | collective-permute-start | bytes 73736 | tf_op jit(solution)/shard_map/ppermute | solution.py:535
  27.7 19.4 %copy-start = (bf16[768,2304]{1,0:T(8,128)(2,1)S(1)}, bf16[768,2304]{1,0:T(8,128)(2,1)}, u32[]{:S(2)}) copy-start(bf16[768,2304]{1,0:T(8,128)(2,1)} %value_project_ref.1) | copy-start | bytes 10616836
  36.8 20.8 %all-to-all-start = ((bf16[16,16,768]{2,1,0:T(8,128)(2,1)}), bf16[16,16,768]{2,1,0:T(8,128)(2,1)}, u32[]{:S(2)}, u32[]{:S(2)}) async-start(bf16[16,16,768]{2,1,0:T(8,128)(2,1)} %broadcast_in_dim.2), calls=%async_computation | async-start | bytes 786432 | tf_op jit(solution)/shard_map/all_to_all | solution.py:538
  47.1 1.3 %copy-start.4 = (bf16[768,768]{1,0:T(8,128)(2,1)S(1)}, bf16[768,768]{1,0:T(8,128)(2,1)}, u32[]{:S(2)}) copy-start(bf16[768,768]{1,0:T(8,128)(2,1)} %merge_ref.5) | copy-start | bytes 3538948
  48.4 0.9 copy-start.6
  51.0 0.7 copy-start.8
  51.7 0.7 copy-start.10
  57.6 1.6 %copy-start.1 = (f32[256,2048]{1,0:T(8,128)S(1)}, f32[256,2048]{1,0:T(8,128)}, u32[]{:S(2)}) copy-start(f32[256,2048]{1,0:T(8,128)} %get-tuple-element.34.bias_ref) | copy-start | bytes 6291460
  59.2 1.6 %copy-start.3 = (f32[256,2048]{1,0:T(8,128)S(1)}, f32[256,2048]{1,0:T(8,128)}, u32[]{:S(2)}) copy-start(f32[256,2048]{1,0:T(8,128)} %get-tuple-element.35.spread_ref) | copy-start | bytes 6291460
  60.8 0.9 copy-start.9
  61.7 0.9 copy-start.11
  62.6 26.0 %copy-start.5 = (bf16[768,768]{1,0:T(8,128)(2,1)S(1)}, bf16[768,768]{1,0:T(8,128)(2,1)}, u32[]{:S(2)}) copy-start(bf16[768,768]{1,0:T(8,128)(2,1)} %merge_ref.5) | copy-start | bytes 3538948
  62.7 26.0 %copy-start.7 = (bf16[768,128]{1,0:T(8,128)(2,1)S(1)}, bf16[768,128]{1,0:T(8,128)(2,1)}, u32[]{:S(2)}) copy-start(bf16[768,128]{1,0:T(8,128)(2,1)} %down_ref.3) | copy-start | bytes 589828
  62.7 26.0 %copy-start.12 = (bf16[256,128]{1,0:T(8,128)(2,1)S(1)}, bf16[256,128]{1,0:T(8,128)(2,1)}, u32[]{:S(2)}) copy-start(bf16[256,128]{1,0:T(8,128)(2,1)} %get-tuple-element.38.hidden_ref) | copy-start | bytes 196612
  62.7 26.0 %copy-start.13 = (f32[16,768]{1,0:T(8,128)S(1)}, f32[16,768]{1,0:T(8,128)}, u32[]{:S(2)}) copy-start(f32[16,768]{1,0:T(8,128)} %get-tuple-element.37.state_ref) | copy-start | bytes 147460
  62.7 26.0 %copy-start.15 = (bf16[3,128]{1,0:T(4,128)(2,1)S(1)}, bf16[3,128]{1,0:T(4,128)(2,1)}, u32[]{:S(2)}) copy-start(bf16[3,128]{1,0:T(4,128)(2,1)} %weight_ref.3) | copy-start | bytes 2308
  62.7 26.0 %copy-start.16 = (s32[1,16]{1,0:T(1,128)S(1)}, s32[1,16]{1,0:T(1,128)}, u32[]{:S(2)}) copy-start(s32[1,16]{1,0:T(1,128)} %counts_ref.3) | copy-start | bytes 196
  62.7 27.7 %copy-start.2 = (bf16[128,256,128]{2,1,0:T(8,128)(2,1)S(1)}, bf16[128,256,128]{2,1,0:T(8,128)(2,1)}, u32[]{:S(2)}) copy-start(bf16[128,256,128]{2,1,0:T(8,128)(2,1)} %get-tuple-element.44.standard_ref) | copy-start | bytes 25165828
  72.2 18.2 %copy-start.14 = (bf16[128,16]{0,1:T(8,128)(2,1)S(1)}, bf16[128,16]{0,1:T(8,128)(2,1)}, u32[]{:S(2)}) copy-start(bf16[128,16]{0,1:T(8,128)(2,1)} %param.28) | copy-start | bytes 12292
  72.2 18.2 %copy-start.17 = (f32[128]{0:T(128)S(1)}, f32[128]{0:T(128)}, u32[]{:S(2)}) copy-start(f32[128]{0:T(128)} %gain_ref.9) | copy-start | bytes 1540

commit v3 on v2

v3 whole, which is shorter than its diff:
```python
import math

import jax
import jax.numpy as jnp
from jax import lax
from jax.experimental import pallas as pl
from jax.experimental.pallas import tpu as pltpu
from jax.sharding import PartitionSpec as P

ATOM_HEADS = 4
TOKEN_HEADS = 16
EPS = 1e-05
NEGATIVE = -1e30
LEFT, RIGHT = 48, 80
WINDOW = 32
KEYS = 128
LANES = 128
GROUP = 8
TERM_SLOTS = 8
KINDS = 3
ATTEND_STACK = 4
PAIR_STACK = 2
STACK = 4
F32 = jnp.float32
BF16 = jnp.bfloat16
NT = (((1,), (1,)), ((), ()))
TN = (((0,), (0,)), ((), ()))
MIB = 1 << 20
PAIR_LIMIT = 56
ATOM_LIMIT = 40
ATTEND_LIMIT = 46
GRADIENT_LIMIT = 32


def iota(shape, axis):
    return lax.broadcasted_iota(jnp.int32, shape, axis)


def dot(a, b):
    return jnp.dot(a, b, preferred_element_type=F32)


def dot_nt(a, b):
    return lax.dot_general(a, b, NT, preferred_element_type=F32)


def dot_tn(a, b):
    return lax.dot_general(a, b, TN, preferred_element_type=F32)


def split(value):
    high = value.astype(BF16)
    return high, (value - high.astype(F32)).astype(BF16)


def normalize(values, gain):
    center = values - jnp.mean(values, axis=-1, keepdims=True)
    spread = lax.rsqrt(jnp.mean(center * center, axis=-1, keepdims=True) + EPS)
    return center * spread * gain


def head_mask(rows, width, heads):
    size = width // heads
    head = iota((rows, width), 0) % heads
    column = iota((rows, width), 1)
    return ((column >= head * size) & (column < (head + 1) * size)).astype(F32)


def pair_kernel(x_ref, gain_ref, weight_ref, *rest):
    terms_ref, standard_ref, block_ref, ones_ref, normed_ref = rest[-5:]
    heads = weight_ref.shape[0]
    width = x_ref.shape[2]

    @pl.when(pl.program_id(0) == 0)
    def _():
        lane = iota((heads, LANES), 1)
        repeat = (lane % heads == iota((heads, LANES), 0)).astype(BF16)
        tiled = dot_tn(weight_ref[...], repeat)
        owner = iota((width, LANES), 1) // heads
        for i in range(GROUP):
            block_ref[i * width : (i + 1) * width, :] = jnp.where(owner == i, tiled, 0.0).astype(BF16)
        ones_ref[...] = jnp.full((width, width), 1.0 / width, BF16)

    gain = gain_ref[...][None, :]
    keys = x_ref.shape[1]
    owner = iota((keys, LANES), 1) // heads
    for q in range(PAIR_STACK):
        lanes = slice(q * LANES, (q + 1) * LANES)
        spread_all = jnp.zeros((keys, LANES), F32)
        for i in range(GROUP):
            x = x_ref[q * GROUP + i]
            center = x.astype(F32) - dot(x, ones_ref[...])
            spread = lax.rsqrt(jnp.sum(center * center, axis=1, keepdims=True) * (1.0 / width) + EPS)
            standard = center * spread
            standard_ref[q * GROUP + i] = standard.astype(BF16)
            normed_ref[q * keys : (q + 1) * keys, i * width : (i + 1) * width] = (standard * gain).astype(BF16)
            spread_all = jnp.where(owner == i, spread, spread_all)
        terms_ref[1, :, lanes] = spread_all
    bias = dot(normed_ref[...], block_ref[...])
    for q in range(PAIR_STACK):
        terms_ref[0, :, q * LANES : (q + 1) * LANES] = bias[q * keys : (q + 1) * keys]


def pair_forward(pair, gain, weight, first, count, previous=(), after=()):
    rows, keys, width = pair.shape
    heads = weight.shape[0]
    lanes = rows * heads
    outs = (
        jax.ShapeDtypeStruct((TERM_SLOTS, keys, lanes), F32),
        jax.ShapeDtypeStruct(pair.shape, BF16),
    )
    before = tuple(previous)
    others = before + tuple(after)
    return pl.pallas_call(
        pair_kernel,
        grid=(count // PAIR_STACK,),
        in_specs=[
            pl.BlockSpec((PAIR_STACK * GROUP, keys, width), lambda g: (g + first // PAIR_STACK, 0, 0)),
            whole(gain),
            whole(weight),
        ]
        + [pl.BlockSpec(memory_space=pl.ANY)] * len(others),
        out_specs=(
            pl.BlockSpec((2, keys, PAIR_STACK * LANES), lambda g: (0, 0, g + first // PAIR_STACK)),
            pl.BlockSpec((PAIR_STACK * GROUP, keys, width), lambda g: (g + first // PAIR_STACK, 0, 0)),
        ),
        out_shape=outs,
        scratch_shapes=[
            pltpu.VMEM((GROUP * width, LANES), BF16),
            pltpu.VMEM((width, width), BF16),
            pltpu.VMEM((PAIR_STACK * keys, GROUP * width), BF16),
        ],
        input_output_aliases={3 + i: i for i in range(len(before))},
        compiler_params=pltpu.CompilerParams(vmem_limit_bytes=PAIR_LIMIT * MIB),
        cost_estimate=pl.CostEstimate(
            flops=count * GROUP * keys * width * 5000, bytes_accessed=count * GROUP * keys * width * 5, transcendentals=0
        ),
        name="pair_forward",
    )(pair, gain, weight, *others)


def atom_kernel(
    left_ref, own_ref, right_ref, gain_ref, project_ref, merge_ref, up_ref,
    counts_ref, single_ref, token_gain_ref, weight_ref, cotangent_ref, _,
    hidden_ref, state_ref, packed_ref, send_ref, key_ref, value_ref, query_ref, attended_ref,
):
    atoms, width = own_ref.shape
    tokens = single_ref.shape[0]
    rows, columns = lax.axis_size("row"), lax.axis_size("col")
    first = (lax.axis_index("row") * columns + lax.axis_index("col")) * atoms
    feats = jnp.concatenate(
        [left_ref[atoms - LEFT :, :], own_ref[...], right_ref[:RIGHT, :]], axis=0
    )
    normed = normalize(feats.astype(F32), gain_ref[...][None, :]).astype(BF16)
    projected = dot(normed, project_ref[...]).astype(BF16)
    query_ref[...] = projected[LEFT : LEFT + atoms, :width]
    key_ref[...] = projected[:, width : 2 * width]
    value_ref[...] = projected[:, 2 * width :]
    size = width // ATOM_HEADS
    stacked = ATOM_HEADS * WINDOW
    lane_head = iota((stacked, width), 1) // size
    row_head = iota((stacked, width), 0) // WINDOW
    mask = lane_head == row_head
    key_index = iota((stacked, KEYS), 1)
    total = rows * columns * atoms
    for b in range(atoms // WINDOW):
        at = b * WINDOW
        queries = jnp.concatenate([query_ref[at : at + WINDOW, :]] * ATOM_HEADS, axis=0)
        queries = jnp.where(mask, queries.astype(F32), 0.0).astype(BF16)
        scores = dot_nt(queries, key_ref[at : at + KEYS, :]) / math.sqrt(size)
        position = first - LEFT + at + key_index
        scores = jnp.where((position >= 0) & (position < total), scores, NEGATIVE)
        weights = jnp.exp(scores - jnp.max(scores, axis=1, keepdims=True))
        row_total = jnp.sum(weights, axis=1, keepdims=True)
        mixture = dot(weights.astype(BF16), value_ref[at : at + KEYS, :]) / row_total
        mixture = jnp.where(mask, mixture, 0.0)
        joined = mixture[:WINDOW]
        for h in range(1, ATOM_HEADS):
            joined = joined + mixture[h * WINDOW : (h + 1) * WINDOW]
        attended_ref[at : at + WINDOW, :] = joined.astype(BF16)
    hidden = (own_ref[...].astype(F32) + dot(attended_ref[...], merge_ref[...])).astype(BF16)
    hidden_ref[...] = hidden
    lifted = jnp.maximum(dot(hidden, up_ref[...]), 0.0).astype(BF16)
    counts_row = counts_ref[...].astype(F32)
    square = jnp.broadcast_to(counts_row, (tokens, tokens))
    above = iota((tokens, tokens), 0)
    below = iota((tokens, tokens), 1)
    counts_col = jnp.sum(jnp.where(above == below, square, 0.0), axis=1, keepdims=True)
    ends = jnp.sum(jnp.where(below <= above, square, 0.0), axis=1, keepdims=True)
    atom = iota((tokens, atoms), 1).astype(F32)
    member = ((atom < ends) & (atom >= ends - counts_col)).astype(F32).astype(BF16)
    state = dot(member, lifted) / counts_col + single_ref[...].astype(F32)
    state_ref[...] = state
    token_normed = normalize(state, token_gain_ref[...][None, :]).astype(BF16)
    turned = jnp.transpose(
        jnp.concatenate([cotangent_ref[...], jnp.zeros((LANES - 3, atoms), F32)], axis=0)
    )
    position_weight = weight_ref[...].astype(F32)
    grad_hidden = turned[:, 0:1] * position_weight[0:1, :]
    for k in range(1, 3):
        grad_hidden = grad_hidden + turned[:, k : k + 1] * position_weight[k : k + 1, :]
    grad_tokens = dot(member, grad_hidden.astype(BF16)).astype(BF16)
    tiles = [token_normed[:, t * LANES : (t + 1) * LANES] for t in range(token_normed.shape[1] // LANES)]
    block = jnp.concatenate(tiles, axis=0)
    packed_ref[...] = jnp.concatenate([block, grad_tokens], axis=0)
    for c in range(send_ref.shape[0]):
        send_ref[c] = block


def whole(array):
    zeros = (0,) * array.ndim
    return pl.BlockSpec(array.shape, lambda *_: zeros)


def atom_stage(left, own, right, gain, project, merge, up, counts, single, token_gain, weight, cotangent, copies, after):
    atoms, width = own.shape
    tokens, token_width = single.shape
    arrays = (left, own, right, gain, project, merge, up, counts, single, token_gain, weight, cotangent)
    outs = (
        jax.ShapeDtypeStruct((atoms, width), BF16),
        jax.ShapeDtypeStruct((tokens, token_width), F32),
        jax.ShapeDtypeStruct((tokens * token_width // LANES + tokens, LANES), BF16),
        jax.ShapeDtypeStruct((copies, tokens * token_width // LANES, LANES), BF16),
    )
    return pl.pallas_call(
        atom_kernel,
        grid=(1,),
        in_specs=[whole(a) for a in arrays]
        + [pl.BlockSpec(memory_space=pl.ANY)],
        out_specs=tuple(whole(a) for a in outs),
        out_shape=outs,
        scratch_shapes=[
            pltpu.VMEM((LEFT + atoms + RIGHT, width), BF16),
            pltpu.VMEM((LEFT + atoms + RIGHT, width), BF16),
            pltpu.VMEM((atoms, width), BF16),
            pltpu.VMEM((atoms, width), BF16),
        ],
        compiler_params=pltpu.CompilerParams(vmem_limit_bytes=ATOM_LIMIT * MIB),
        cost_estimate=pl.CostEstimate(flops=400 * MIB, bytes_accessed=2 * MIB, transcendentals=0),
        name="atom_stage",
    )(*arrays, after)


def attend_kernel(
    gathered_ref, down_ref, project_hbm, merge_hbm, terms_hbm,
    weight_ref, grad_ref, small_ref, send_ref,
    query_ref, mix_ref, key_ref, value_ref, stat_ref, project_ref, merge_ref, terms_ref,
    weight_semaphores, semaphores,
):
    step = pl.program_id(0)
    owners = send_ref.shape[0]
    steps = owners // ATTEND_STACK
    width = project_ref.shape[1]
    heads = TOKEN_HEADS
    chunk = weight_ref.shape[1]
    per = chunk // LANES
    stat_rows = steps * per
    part_rows = query_ref.shape[0] // owners
    part_lanes = chunk // ATTEND_STACK

    def terms_copy(at):
        lanes = pl.ds(pl.multiple_of(at * chunk, chunk), chunk)
        return pltpu.make_async_copy(terms_hbm.at[0:2, :, lanes], terms_ref.at[:, :, lanes], semaphores.at[at])

    @pl.when(step == 0)
    def _():
        thirds = [
            pltpu.make_async_copy(
                project_hbm.at[:, k * width : (k + 1) * width], project_ref.at[k], weight_semaphores.at[k]
            )
            for k in range(3)
        ]
        merge = pltpu.make_async_copy(merge_hbm, merge_ref, weight_semaphores.at[3])
        for copy in (*thirds, merge, terms_copy(0), terms_copy(1)):
            copy.start()
        tiles = width // LANES
        own = gathered_ref.shape[1] // (KINDS * tiles + 1)

        def tile(index):
            return gathered_ref[:, index * own : (index + 1) * own, :].reshape(-1, LANES)

        blocks = [
            jnp.concatenate([tile(k * tiles + t) for t in range(tiles)], axis=1) for k in range(KINDS)
        ]
        rows = jnp.concatenate(blocks[:-1], axis=0)
        update = dot_nt(tile(KINDS * tiles), down_ref[...]).astype(BF16)
        thirds[0].wait()
        query_ref[...] = dot(blocks[-1], project_ref[0]).astype(BF16)
        thirds[1].wait()
        key_ref[...] = dot(rows, project_ref[1]).astype(BF16)
        thirds[2].wait()
        value_ref[...] = dot(rows, project_ref[2]).astype(BF16)
        merge.wait()
        mix_ref[...] = dot_nt(update, merge_ref[...]).astype(BF16)

    @pl.when(step < steps - 2)
    def _():
        terms_copy(step + 2).start()

    terms_copy(step).wait()
    mask = head_mask(heads, width, heads)

    def expanded(ref, at):
        own = pl.ds(pl.multiple_of(at * part_rows, part_rows), part_rows)
        spread_out = ref[own, :].astype(F32)[:, None, :] * mask[None]
        return spread_out.reshape(part_rows * heads, width).astype(BF16)

    values = value_ref[...]
    all_rounded = []
    for sub in range(ATTEND_STACK):
        at = step * ATTEND_STACK + sub
        inside = slice(sub * part_lanes, (sub + 1) * part_lanes)
        lanes = pl.ds(pl.multiple_of(at * part_lanes, part_lanes), part_lanes)
        bias = terms_ref[0, :, lanes]
        scores = dot_nt(key_ref[...], expanded(query_ref, at)) / math.sqrt(width // heads) + bias
        grad_probs = dot_nt(values, expanded(mix_ref, at))
        row_max = jnp.max(scores, axis=0, keepdims=True).astype(BF16).astype(F32)
        weights = jnp.exp(scores - row_max)
        row_total = jnp.sum(weights, axis=0, keepdims=True)
        rounded = weights.astype(BF16)
        all_rounded.append(rounded)
        inner = jnp.sum(rounded.astype(F32) * grad_probs, axis=0, keepdims=True)
        weight_ref[:, inside] = (weights * terms_ref[1, :, lanes]).astype(BF16)
        grad_ref[:, inside] = grad_probs
        small_ref[:, inside] = (bias * (1.0 / LANES)).astype(BF16)
        for k, stat in enumerate((row_max, row_total, inner)):
            for p in range(part_lanes // LANES):
                row = k * stat_rows + at * (part_lanes // LANES) + p
                stat_ref[pl.ds(row, 1), :] = stat[:, p * LANES : (p + 1) * LANES]
    mixture = dot_tn(jnp.concatenate(all_rounded, axis=1), values).reshape(-1, heads, width) * mask[None]
    part = jnp.sum(mixture, axis=1).astype(BF16)
    for sub in range(ATTEND_STACK):
        for t in range(width // LANES):
            low = 5 * stat_rows + t * part_rows
            send_ref[step * ATTEND_STACK + sub, low : low + part_rows, :] = part[
                sub * part_rows : (sub + 1) * part_rows, t * LANES : (t + 1) * LANES
            ]

    @pl.when(step == steps - 1)
    def _():
        pieces = [stat_ref[:stat_rows, :].astype(BF16)]
        for k in (1, 2):
            pieces.extend(split(stat_ref[k * stat_rows : (k + 1) * stat_rows, :]))
        stats = jnp.concatenate(pieces, axis=0)
        for c in range(owners):
            send_ref[c, : 5 * stat_rows, :] = stats


def attend_stage(gathered, project, down, merge, terms, owners):
    _, keys, lanes = terms.shape
    width = project.shape[0]
    count = gathered.shape[0] * gathered.shape[1] // (KINDS * (width // LANES) + 1)
    rows = count // owners
    steps = owners // ATTEND_STACK
    chunk = lanes // steps
    stat_rows = lanes // LANES
    payload = jax.ShapeDtypeStruct((owners, 5 * stat_rows + rows * width // LANES, LANES), BF16)
    tile = pl.BlockSpec((keys, chunk), lambda g: (0, g))
    arrays = (gathered, down)
    return pl.pallas_call(
        attend_kernel,
        grid=(steps,),
        in_specs=[whole(a) for a in arrays] + [pl.BlockSpec(memory_space=pl.ANY)] * 3,
        out_specs=(tile, tile, tile, whole(payload)),
        out_shape=(
            jax.ShapeDtypeStruct((keys, lanes), BF16),
            jax.ShapeDtypeStruct((keys, lanes), F32),
            jax.ShapeDtypeStruct((keys, lanes), BF16),
            payload,
        ),
        scratch_shapes=[
            pltpu.VMEM((count, width), BF16),
            pltpu.VMEM((count, width), BF16),
            pltpu.VMEM((keys, width), BF16),
            pltpu.VMEM((keys, width), BF16),
            pltpu.VMEM((3 * stat_rows, LANES), F32),
            pltpu.VMEM((3, width, width), BF16),
            pltpu.VMEM((width, width), BF16),
            pltpu.VMEM((2, keys, lanes), F32),
            pltpu.SemaphoreType.DMA((4,)),
            pltpu.SemaphoreType.DMA((steps,)),
        ],
        compiler_params=pltpu.CompilerParams(vmem_limit_bytes=ATTEND_LIMIT * MIB),
        cost_estimate=pl.CostEstimate(flops=8000 * MIB, bytes_accessed=12 * MIB, transcendentals=0),
        name="attend_stage",
    )(*arrays, project, merge, terms)


def combined(received_ref, rows):
    parts = received_ref.shape[0]

    def stat(part, index):
        return received_ref[part, index * rows : (index + 1) * rows, :].astype(F32)

    maxima = [stat(s, 0) for s in range(parts)]
    top = maxima[0]
    for s in range(1, parts):
        top = jnp.maximum(top, maxima[s])
    scales = [jnp.exp(value - top) for value in maxima]
    total = jnp.zeros_like(top)
    inner = jnp.zeros_like(top)
    for s in range(parts):
        total = total + scales[s] * (stat(s, 1) + stat(s, 2))
        inner = inner + scales[s] * (stat(s, 3) + stat(s, 4))
    return top, scales, total, inner


def update_tokens(
    received_ref, state_ref, hidden_ref, counts_ref, merge_ref, down_ref, weight_ref, positions_ref, update_ref,
    scales, total,
):
    column = lax.axis_index("col")
    tokens, width = state_ref.shape
    heads = TOKEN_HEADS
    parts = received_ref.shape[0]
    stat_rows = (received_ref.shape[1] - tokens * width // LANES) // 5
    halves = tokens // GROUP
    sub = iota((tokens, LANES), 0)
    mine = iota((tokens, LANES), 1) // heads == sub % GROUP
    stat_row = iota((stat_rows, LANES), 0)
    rows = []
    for s in range(parts):
        scale = scales[s] / total
        picked = jnp.zeros((tokens, LANES), F32)
        for p in range(halves):
            one = jnp.sum(jnp.where(stat_row == column * halves + p, scale, 0.0), axis=0, keepdims=True)
            picked = jnp.where(sub // GROUP == p, one, picked)
        rows.append(jnp.where(mine, picked, 0.0))
    stacked = jnp.concatenate(rows, axis=0)
    spread_out = head_mask(LANES, width, heads).astype(BF16)
    high, low = split(stacked)
    rest = stacked - high.astype(F32) - low.astype(F32)
    scale = dot(high, spread_out) + dot(low, spread_out) + dot(rest.astype(BF16), spread_out)
    pieces = []
    for t in range(width // LANES):
        at = 5 * stat_rows + t * tokens
        piece = jnp.zeros((tokens, LANES), F32)
        for s in range(parts):
            factor = scale[s * tokens : (s + 1) * tokens, t * LANES : (t + 1) * LANES]
            piece = piece + factor * received_ref[s, at : at + tokens, :].astype(F32)
        pieces.append(piece.astype(BF16))
    attention = jnp.concatenate(pieces, axis=1)
    update = (state_ref[...] + dot(attention, merge_ref[...])).astype(BF16)
    update_ref[...] = update
    lowered = dot(update, down_ref[...]).astype(BF16)
    atoms = hidden_ref.shape[0]
    counts_row = counts_ref[...].astype(F32)
    square = jnp.broadcast_to(counts_row, (tokens, tokens))
    above = iota((tokens, tokens), 0)
    below = iota((tokens, tokens), 1)
    counts_col = jnp.sum(jnp.where(above == below, square, 0.0), axis=1, keepdims=True)
    ends = jnp.sum(jnp.where(below <= above, square, 0.0), axis=1, keepdims=True)
    atom = iota((tokens, atoms), 1).astype(F32)
    member = ((atom < ends) & (atom >= ends - counts_col)).astype(F32).astype(BF16)
    hidden_next = (hidden_ref[...].astype(F32) + dot_tn(member, lowered)).astype(BF16)
    positions_ref[...] = dot_nt(weight_ref[...], hidden_next)


def gradient_kernel(
    weight_ref, grad_ref, small_ref, standard_ref, received_ref, own_ref, gain_ref, bias_weight_ref,
    state_ref, hidden_ref, counts_ref, merge_ref, down_ref, position_ref,
    out_ref, positions_ref, update_ref, block_ref, ones_ref, factor_ref, inner_ref,
):
    step = pl.program_id(0)
    heads, width = bias_weight_ref.shape
    rows = factor_ref.shape[0]

    @pl.when(step == 0)
    def _():
        lane = iota((heads, LANES), 1)
        repeat = (lane % heads == iota((heads, LANES), 0)).astype(BF16)
        tiled = dot_tn(repeat, bias_weight_ref[...]) * gain_ref[...][None, :]
        tiled = tiled - jnp.mean(tiled, axis=1, keepdims=True)
        high, low = split(tiled)
        owner = iota((LANES, width), 0) // heads
        for i in range(GROUP):
            mine = owner == i
            at = slice(i * width, (i + 1) * width)
            block_ref[:LANES, at] = jnp.where(mine, high.astype(F32), 0.0).astype(BF16)
            block_ref[LANES:, at] = jnp.where(mine, low.astype(F32), 0.0).astype(BF16)
            ones = jnp.where(mine, 1.0, 0.0).astype(BF16)
            ones_ref[:LANES, at] = ones
            ones_ref[LANES:, at] = ones
        top, scales, total, inner = combined(received_ref, rows)
        factor_ref[...] = jnp.exp(own_ref[0, :rows, :].astype(F32) - top) / total
        inner_ref[...] = inner / total
        update_tokens(
            received_ref, state_ref, hidden_ref, counts_ref, merge_ref, down_ref, position_ref,
            positions_ref, update_ref, scales, total,
        )

    keys = weight_ref.shape[0]
    lefts, rights = [], []
    for q in range(STACK):
        lanes = slice(q * LANES, (q + 1) * LANES)
        factor = factor_ref[pl.ds(step * STACK + q, 1), :]
        inner = inner_ref[pl.ds(step * STACK + q, 1), :]
        grad = weight_ref[:, lanes].astype(F32) * factor * (grad_ref[:, lanes] - inner)
        rounded = grad.astype(BF16)
        lefts.append(jnp.concatenate([rounded, rounded], axis=1))
        rights.append(jnp.concatenate(split(grad * small_ref[:, lanes].astype(F32)), axis=1))
    left = jnp.concatenate(lefts, axis=0)
    right = jnp.concatenate(rights, axis=0)
    for i in range(0, GROUP, 2):
        at = slice(i * width, (i + 2) * width)
        direct = dot(left, block_ref[:, at])
        along = dot(right, ones_ref[:, at])
        for q in range(STACK):
            for k in range(2):
                part = (slice(q * keys, (q + 1) * keys), slice(k * width, (k + 1) * width))
                r = q * GROUP + i + k
                out_ref[r] = (direct[part] - standard_ref[r].astype(F32) * along[part]).astype(BF16)


def gradient_stage(weights, grad, small, standard, received, own, gain, bias_weight, state, hidden, counts, merge, down, weight):
    rows, keys, width = standard.shape
    arrays = (received, own, gain, bias_weight, state, hidden, counts, merge, down, weight)
    outs = (
        jax.ShapeDtypeStruct((weight.shape[0], hidden.shape[0]), F32),
        jax.ShapeDtypeStruct(state.shape, BF16),
    )
    tile = pl.BlockSpec((keys, STACK * LANES), lambda g: (0, g))
    block = pl.BlockSpec((STACK * GROUP, keys, width), lambda g: (g, 0, 0))
    return pl.pallas_call(
        gradient_kernel,
        grid=(rows // GROUP // STACK,),
        in_specs=[tile, tile, tile, block] + [whole(a) for a in arrays],
        out_specs=(block, *(whole(a) for a in outs)),
        out_shape=(jax.ShapeDtypeStruct(standard.shape, BF16), *outs),
        scratch_shapes=[
            pltpu.VMEM((2 * LANES, GROUP * width), BF16),
            pltpu.VMEM((2 * LANES, GROUP * width), BF16),
            pltpu.VMEM((rows // GROUP, LANES), F32),
            pltpu.VMEM((rows // GROUP, LANES), F32),
        ],
        compiler_params=pltpu.CompilerParams(vmem_limit_bytes=GRADIENT_LIMIT * MIB),
        cost_estimate=pl.CostEstimate(flops=16000 * MIB, bytes_accessed=22 * MIB, transcendentals=0),
        name="gradient_stage",
    )(weights, grad, small, standard, *arrays)


def per_device(
    atom_feats, atom_gain, atom_project, atom_merge, atom_up, token_counts, token_single, token_gain,
    token_project, token_merge, pair_state, pair_gain, bias_weight, atom_down, position_weight,
    position_cotangent,
):
    both = ("row", "col")
    rows, columns = lax.axis_size("row"), lax.axis_size("col")
    devices = rows * columns
    left = lax.ppermute(atom_feats, both, [(i, i + 1) for i in range(devices - 1)])
    right = lax.ppermute(atom_feats, both, [(i + 1, i) for i in range(devices - 1)])
    gain = pair_gain
    bias_turned = bias_weight.T
    groups = pair_state.shape[0] // GROUP
    cuts = (0, groups // 4, groups * 5 // 8, groups)
    pair_part = pair_forward(pair_state, gain, bias_turned, 0, cuts[1])
    hidden, state, packed, send = atom_stage(
        left, atom_feats, right, atom_gain, atom_project, atom_merge, atom_up,
        token_counts, token_single, token_gain, position_weight, position_cotangent, rows, pair_part[0],
    )
    pair_part = pair_forward(pair_state, gain, bias_turned, cuts[1], cuts[2] - cuts[1], pair_part, (send,))
    shared = lax.all_to_all(send, "row", 0, 0)
    shared = shared.reshape(columns, -1, shared.shape[-1])
    mixed = jnp.concatenate([shared, jnp.broadcast_to(packed[None], (columns,) + packed.shape)], axis=1)
    gathered = lax.all_to_all(mixed, "col", 0, 0)
    terms, standard = pair_forward(
        pair_state, gain, bias_turned, cuts[2], cuts[3] - cuts[2], pair_part, (mixed,)
    )
    weights, grad, small, payload = attend_stage(
        gathered, token_project, atom_down, token_merge, terms, columns
    )
    received = lax.all_to_all(payload, "col", 0, 0)
    pair_grad, positions, token_update = gradient_stage(
        weights, grad, small, standard, received, payload, gain, bias_turned,
        state, hidden, token_counts, token_merge, atom_down, position_weight,
    )
    return (positions, token_update, pair_grad)


def solution(mesh):
    placed = (
        P(("row", "col"), None), P(), P(), P(), P(), P(("row", "col"), None), P(("row", "col"), None), P(),
        P(), P(), P("row", "col", None), P(), P(), P(), P(), P(None, ("row", "col")),
    )
    return jax.shard_map(
        per_device,
        mesh=mesh,
        in_specs=placed,
        out_specs=(P(None, ("row", "col")), P(("row", "col"), None), P("row", "col", None)),
        check_vma=False,
    )
```

time: 98.5 us -> 81.5 us (0.83)
  local copies, waits for them, and re-layouts: 10.8 us -> 0.1 us
  waiting for transfers between devices: 1.34 us -> 9.24 us
  starting transfers between devices: 25.3 us -> 19.3 us
  Pallas kernels: 43 us -> 38 us
  blocking collectives: 16.4 us -> 12.7 us
    unnamed x40 -> x30, local copies, waits for them, and re-layouts: 9.24 us -> 0.07 us
    all_to_all x2, waiting for transfers between devices: 0.01 us -> 7.7 us  [the longest x1 4.76 us: per_device(): gathered = lax.all_to_all(mixed, 'col', 0, 0)]
    pallas_call x6 -> x4, Pallas kernels: 30.9 us -> 26.1 us  [the longest x3 18 us: pair_forward(): pl.pallas_call(pair_kernel, grid=(count // PAIR_STACK,), in_specs=[pl.Blo...]
    all_to_all x2, starting transfers between devices: 16.9 us -> 12.8 us  [the longest x1 7.29 us: per_device(): shared = lax.all_to_all(send, 'row', 0, 0)]
    all_to_all x1, blocking collectives: 16.4 us -> 12.7 us  [per_device(): received = lax.all_to_all(payload, 'col', 0, 0)]
    ppermute x1 -> x0, starting transfers between devices: 1.98 us -> none  [per_device(): block = lax.ppermute(token_normed, both, route)]
    broadcast_in_dim x1, local copies, waits for them, and re-layouts: 1.53 us -> 0.03 us  [per_device(): jnp.broadcast_to(packed[None], (columns,) + packed.shape)]
    pallas_call x1, Pallas kernels: 4.8 us -> 3.63 us  [atom_stage(): pl.pallas_call(atom_kernel, grid=(1,), in_specs=[whole(a) for a in arrays...]
  transfers between devices with their start and end apart: 5 -> 4, of which waited for: 1 -> 3; matrix products, arithmetic and copies ran while one was open for 0% -> 0% of each run, Pallas kernels for 20% -> 22%
where the time goes in v3:
time: 81.5 us; the launch traced here: 81 us
  Pallas kernels  38 us (47%)
  starting transfers between devices  19.3 us (24%)
  blocking collectives  12.7 us (16%)
  waiting for transfers between devices  9.24 us (11%)
  other arithmetic  0.89 us (1%)
  between operations  0.84 us (1%)
    pallas_call x3, Pallas kernels, pair_forward(): pl.pallas_call(pair_kernel, grid=(count // PAIR_STACK,), in_specs=[pl.Blo...  18 us
    all_to_all x1, blocking collectives, per_device(): received = lax.all_to_all(payload, 'col', 0, 0)  12.7 us
    pallas_call x1, Pallas kernels, gradient_stage(): pl.pallas_call(gradient_kernel, grid=(rows // GROUP // STACK,), in_specs=...  8.24 us
    pallas_call x1, Pallas kernels, attend_stage(): pl.pallas_call(attend_kernel, grid=(steps,), in_specs=[whole(a) for a in...  8.13 us
    all_to_all x1, starting transfers between devices, per_device(): shared = lax.all_to_all(send, 'row', 0, 0)  7.29 us
    all_to_all x1, starting transfers between devices, per_device(): gathered = lax.all_to_all(mixed, 'col', 0, 0)  5.52 us
    ppermute x1, starting transfers between devices, per_device(): lax.ppermute(atom_feats, both, [(i, i + 1) for i in range(devices - 1)])  5.18 us
    all_to_all x1, waiting for transfers between devices, per_device(): gathered = lax.all_to_all(mixed, 'col', 0, 0)  4.76 us
  transfers between devices with their start and end apart: 4, of which 3 were waited for; matrix products, arithmetic and copies ran while one was open for 0% of the time, Pallas kernels for 22%

profile of v3, /device:TPU:0, one launch (start us, length us, event | category | flops | bytes accessed | tf_op | source)
XLA Modules:
  0.0 81.0 jit_solution(11139741569183356004)
XLA Ops:
  0.6 5.2 %collective-permute-start = (bf16[256,128]{1,0:T(8,128)(2,1)}, bf16[256,128]{1,0:T(8,128)(2,1)S(1)}, u32[]{:S(2)}, u32[]{:S(2)}) collective-permute-start(bf16[256,128]{1,0:T(8,128)(2,1)} %own_ref.1), channel_id=1, source_target_pairs={{0,1},{1,2},{2,3},{3,4},{4,5},{5,6},{6,7},{7,8},{8,9},{9,10},{10,1... | collective-permute-start | bytes 196616 | tf_op jit(solution)/shard_map/ppermute | solution.py:550
  5.8 1.3 %collective-permute-start.1 = (bf16[256,128]{1,0:T(8,128)(2,1)}, bf16[256,128]{1,0:T(8,128)(2,1)S(1)}, u32[]{:S(2)}, u32[]{:S(2)}) collective-permute-start(bf16[256,128]{1,0:T(8,128)(2,1)} %own_ref.1), channel_id=1, source_target_pairs={{1,0},{2,1},{3,2},{4,3},{5,4},{6,5},{7,6},{8,7},{9,8},{10,9},{11,1... | collective-permute-start | bytes 196616 | tf_op jit(solution)/shard_map/ppermute | solution.py:551
  7.1 0.0 copy-start.1
  7.1 0.0 copy-start.2
  7.1 0.0 copy-start.3
  7.2 0.0 copy-start.4
  7.2 0.0 copy-start.5
  7.2 0.0 copy-start.7
  7.2 0.0 copy-start.8
  7.2 0.0 copy-start.10
  7.2 0.0 copy-start.11
  7.2 0.0 copy-start.12
  7.2 4.9 %pair_forward.3 = (f32[8,256,2048]{2,1,0:T(8,128)}, bf16[128,256,128]{2,1,0:T(8,128)(2,1)}) custom-call(bf16[128,256,128]{2,1,0:T(8,128)(2,1)} %x_ref.5, f32[128]{0:T(128)} %gain_ref.9, bf16[16,128]{1,0:T(8,128)(2,1)} %bitcast.2), custom_call_target="tpu_custom_call" | custom-call | flops 5242880000 | bytes 5242880 | tf_op jit(solution)/shard_map/pair_forward/pallas_call | solution.py:114
  12.2 0.0 collective-permute-done.left_ref
  12.2 1.5 %collective-permute-done.1.right_ref = bf16[256,128]{1,0:T(8,128)(2,1)S(1)} collective-permute-done((bf16[256,128]{1,0:T(8,128)(2,1)}, bf16[256,128]{1,0:T(8,128)(2,1)S(1)}, u32[]{:S(2)}, u32[]{:S(2)}) %collective-permute-start.1) | collective-permute-done | bytes 65568 | tf_op jit(solution)/shard_map/ppermute | solution.py:551
  13.7 0.0 copy-done.1
  13.7 0.0 copy-done.2
  13.7 0.0 copy-done.3
  13.7 0.0 copy-done.4
  13.7 0.0 copy-done.5
  13.7 0.0 copy-done.7
  13.7 0.0 copy-done.8
  13.7 0.0 copy-done.10
  13.8 0.0 copy-done.11
  13.8 0.0 copy-done.12
  13.8 3.6 %atom_stage.1 = (bf16[256,128]{1,0:T(8,128)(2,1)S(1)}, f32[16,768]{1,0:T(8,128)S(1)}, bf16[112,128]{1,0:T(8,128)(2,1)S(1)}, bf16[16,96,128]{2,1,0:T(8,128)(2,1)}) custom-call(bf16[256,128]{1,0:T(8,128)(2,1)S(1)} %collective-permute-done.left_ref, bf16[256,128]{1,0:T(8,128)(2,1)S(1)} %copy-done.3, bf16[256,128]{1,0:T(8,128)(2,1)S(1)} %collective-permute-done.1.right_ref, ...), custom_call_target="tpu_custom_call" | custom-call | flops 419430400 | bytes 2097152 | tf_op jit(solution)/shard_map/atom_stage/pallas_call | solution.py:225
  17.4 7.3 %all-to-all-start = ((bf16[16,96,128]{2,1,0:T(8,128)(2,1)}), bf16[16,96,128]{2,1,0:T(8,128)(2,1)S(1)}, u32[]{:S(2)}, u32[]{:S(2)}) async-start(bf16[16,96,128]{2,1,0:T(8,128)(2,1)} %get-tuple-element.21.rest_2_), calls=%async_computation | async-start | bytes 786432 | tf_op jit(solution)/shard_map/all_to_all | solution.py:562
  24.7 6.5 %pair_forward.4 = (f32[8,256,2048]{2,1,0:T(8,128)}, bf16[128,256,128]{2,1,0:T(8,128)(2,1)}) custom-call(bf16[128,256,128]{2,1,0:T(8,128)(2,1)} %x_ref.5, f32[128]{0:T(128)} %gain_ref.9, bf16[16,128]{1,0:T(8,128)(2,1)} %bitcast.3, f32[8,256,2048]{2,1,0:T(8,128)} %get-tuple-element.20._.rest_0_, ...), custom_call_target="tpu_custom_call", output_to_operand_aliasing={{0}: (3, {}), {1}: (4, {})} | custom-call | flops 7864320000 | bytes 7864320 | tf_op jit(solution)/shard_map/pair_forward/pallas_call | solution.py:114
  31.2 2.9 %all-to-all-done = bf16[16,96,128]{2,1,0:T(8,128)(2,1)S(1)} async-done(((bf16[16,96,128]{2,1,0:T(8,128)(2,1)}), bf16[16,96,128]{2,1,0:T(8,128)(2,1)S(1)}, u32[]{:S(2)}, u32[]{:S(2)}) %all-to-all-start) | async-done | bytes 393248 | tf_op jit(solution)/shard_map/all_to_all | solution.py:562
  34.2 0.9 %pad_maximum_fusion.rest_2_ = bf16[8,304,128]{2,1,0:T(8,128)(2,1)} fusion(bf16[8,112,128]{2,1,0:T(8,128)(2,1)S(1)} %broadcast_in_dim.2, bf16[8,192,128]{2,1,0:T(8,128)(2,1)S(1)} %bitcast.6), kind=kLoop, calls=%fused_computation | loop fusion | flops 1245184 | bytes 1245184 | tf_op jit(solution)/shard_map/concatenate | solution.py:564
  35.1 5.5 %all-to-all-start.1 = ((bf16[8,304,128]{2,1,0:T(8,128)(2,1)}), bf16[8,304,128]{2,1,0:T(8,128)(2,1)S(1)}, u32[]{:S(2)}, u32[]{:S(2)}) async-start(bf16[8,304,128]{2,1,0:T(8,128)(2,1)} %pad_maximum_fusion.rest_2_), calls=%async_computation.1 | async-start | bytes 1245184 | tf_op jit(solution)/shard_map/all_to_all | solution.py:565
  40.6 0.0 copy-start.13
  40.6 0.0 copy-start.14
  40.6 6.5 %pair_forward.5 = (f32[8,256,2048]{2,1,0:T(8,128)}, bf16[128,256,128]{2,1,0:T(8,128)(2,1)}) custom-call(bf16[128,256,128]{2,1,0:T(8,128)(2,1)} %x_ref.5, f32[128]{0:T(128)} %gain_ref.9, bf16[16,128]{1,0:T(8,128)(2,1)} %bitcast.4, f32[8,256,2048]{2,1,0:T(8,128)} %get-tuple-element.24.rest_0_, ...), custom_call_target="tpu_custom_call", output_to_operand_aliasing={{0}: (3, {}), {1}: (4, {})} | custom-call | flops 7864320000 | bytes 7864320 | tf_op jit(solution)/shard_map/pair_forward/pallas_call | solution.py:114
  47.2 4.8 %all-to-all-done.1.gathered_ref = bf16[8,304,128]{2,1,0:T(8,128)(2,1)S(1)} async-done(((bf16[8,304,128]{2,1,0:T(8,128)(2,1)}), bf16[8,304,128]{2,1,0:T(8,128)(2,1)S(1)}, u32[]{:S(2)}, u32[]{:S(2)}) %all-to-all-start.1) | async-done | bytes 622624 | tf_op jit(solution)/shard_map/all_to_all | solution.py:565
  51.9 0.0 copy-done.13
  51.9 0.0 copy-done.14
  51.9 0.0 copy-start
  51.9 0.0 copy-start.6
  51.9 0.0 copy-start.9
  52.0 8.1 %attend_stage.1 = (bf16[256,2048]{1,0:T(8,128)(2,1)S(1)}, f32[256,2048]{1,0:T(8,128)S(1)}, bf16[256,2048]{1,0:T(8,128)(2,1)S(1)}, bf16[8,176,128]{2,1,0:T(8,128)(2,1)S(1)}) custom-call(bf16[8,304,128]{2,1,0:T(8,128)(2,1)S(1)} %all-to-all-done.1.gathered_ref, bf16[768,128]{1,0:T(8,128)(2,1)S(1)} %copy-done.14, bf16[768,2304]{1,0:T(8,128)(2,1)} %project_hbm.1, ...), custom_call_target="tpu_custom_call" | custom-call | flops 8388608000 | bytes 12582912 | tf_op jit(solution)/shard_map/attend_stage/pallas_call | solution.py:360
  60.1 12.7 %all_to_all.15.received_ref = bf16[8,176,128]{2,1,0:T(8,128)(2,1)S(1)} all-to-all(bf16[8,176,128]{2,1,0:T(8,128)(2,1)S(1)} %get-tuple-element.31.own_ref), channel_id=1, replica_groups=mesh['row'=16,'col'=8] {'col'}, dimensions={0} | all-to-all | bytes 720896 | tf_op jit(solution)/shard_map/all_to_all | solution.py:572
  72.8 0.0 copy-done
  72.8 0.0 copy-done.6
  72.8 0.0 copy-done.9
  72.8 8.2 %gradient_stage.1 = (bf16[128,256,128]{2,1,0:T(8,128)(2,1)}, f32[3,256]{1,0:T(4,128)}, bf16[16,768]{1,0:T(8,128)(2,1)}) custom-call(bf16[256,2048]{1,0:T(8,128)(2,1)S(1)} %get-tuple-element.27.weight_ref, f32[256,2048]{1,0:T(8,128)S(1)} %get-tuple-element.28.grad_ref, bf16[256,2048]{1,0:T(8,128)(2,1)S(1)} %get-tuple-element.29.small_ref, ...), custom_call_target="tpu_custom_call" | custom-call | flops 16777216000 | bytes 23068672 | tf_op jit(solution)/shard_map/gradient_stage/pallas_call | solution.py:524
  (1 shorter events, 0.0 us)
Async XLA Ops:
  0.6 11.5 %collective-permute-start = (bf16[256,128]{1,0:T(8,128)(2,1)}, bf16[256,128]{1,0:T(8,128)(2,1)S(1)}, u32[]{:S(2)}, u32[]{:S(2)}) collective-permute-start(bf16[256,128]{1,0:T(8,128)(2,1)} %own_ref.1), channel_id=1, source_target_pairs={{0,1},{1,2},{2,3},{3,4},{4,5},{5,6},{6,7},{7,8},{8,9},{9,10},{10,1... | collective-permute-start | bytes 196616 | tf_op jit(solution)/shard_map/ppermute | solution.py:550
  5.8 7.9 %collective-permute-start.1 = (bf16[256,128]{1,0:T(8,128)(2,1)}, bf16[256,128]{1,0:T(8,128)(2,1)S(1)}, u32[]{:S(2)}, u32[]{:S(2)}) collective-permute-start(bf16[256,128]{1,0:T(8,128)(2,1)} %own_ref.1), channel_id=1, source_target_pairs={{1,0},{2,1},{3,2},{4,3},{5,4},{6,5},{7,6},{8,7},{9,8},{10,9},{11,1... | collective-permute-start | bytes 196616 | tf_op jit(solution)/shard_map/ppermute | solution.py:551
  7.1 6.6 %copy-start.1 = (bf16[128,768]{1,0:T(8,128)(2,1)S(1)}, bf16[128,768]{1,0:T(8,128)(2,1)}, u32[]{:S(2)}) copy-start(bf16[128,768]{1,0:T(8,128)(2,1)} %up_ref.1) | copy-start | bytes 589828
  7.1 6.6 %copy-start.2 = (bf16[128,384]{1,0:T(8,128)(2,1)S(1)}, bf16[128,384]{1,0:T(8,128)(2,1)}, u32[]{:S(2)}) copy-start(bf16[128,384]{1,0:T(8,128)(2,1)} %project_ref.1) | copy-start | bytes 294916
  7.1 6.6 %copy-start.3 = (bf16[256,128]{1,0:T(8,128)(2,1)S(1)}, bf16[256,128]{1,0:T(8,128)(2,1)}, u32[]{:S(2)}) copy-start(bf16[256,128]{1,0:T(8,128)(2,1)} %own_ref.1) | copy-start | bytes 196612
  7.2 6.6 %copy-start.4 = (bf16[128,128]{1,0:T(8,128)(2,1)S(1)}, bf16[128,128]{1,0:T(8,128)(2,1)}, u32[]{:S(2)}) copy-start(bf16[128,128]{1,0:T(8,128)(2,1)} %merge_ref.2) | copy-start | bytes 98308
  7.2 6.6 %copy-start.5 = (bf16[16,768]{1,0:T(8,128)(2,1)S(1)}, bf16[16,768]{1,0:T(8,128)(2,1)}, u32[]{:S(2)}) copy-start(bf16[16,768]{1,0:T(8,128)(2,1)} %single_ref.1) | copy-start | bytes 73732
  7.2 6.6 %copy-start.7 = (f32[768]{0:T(1024)S(1)}, f32[768]{0:T(1024)}, u32[]{:S(2)}) copy-start(f32[768]{0:T(1024)} %token_gain_ref.1) | copy-start | bytes 9220
  7.2 6.6 %copy-start.8 = (f32[3,256]{1,0:T(4,128)S(1)}, f32[3,256]{1,0:T(4,128)}, u32[]{:S(2)}) copy-start(f32[3,256]{1,0:T(4,128)} %cotangent_ref.1) | copy-start | bytes 9220
  7.2 6.6 %copy-start.10 = (bf16[3,128]{1,0:T(4,128)(2,1)S(1)}, bf16[3,128]{1,0:T(4,128)(2,1)}, u32[]{:S(2)}) copy-start(bf16[3,128]{1,0:T(4,128)(2,1)} %position_ref.1) | copy-start | bytes 2308
  7.2 6.6 %copy-start.11 = (f32[128]{0:T(128)S(1)}, f32[128]{0:T(128)}, u32[]{:S(2)}) copy-start(f32[128]{0:T(128)} %gain_ref.6) | copy-start | bytes 1540
  7.2 6.6 %copy-start.12 = (s32[1,16]{1,0:T(1,128)S(1)}, s32[1,16]{1,0:T(1,128)}, u32[]{:S(2)}) copy-start(s32[1,16]{1,0:T(1,128)} %counts_ref.3) | copy-start | bytes 196
  17.4 16.8 %all-to-all-start = ((bf16[16,96,128]{2,1,0:T(8,128)(2,1)}), bf16[16,96,128]{2,1,0:T(8,128)(2,1)S(1)}, u32[]{:S(2)}, u32[]{:S(2)}) async-start(bf16[16,96,128]{2,1,0:T(8,128)(2,1)} %get-tuple-element.21.rest_2_), calls=%async_computation | async-start | bytes 786432 | tf_op jit(solution)/shard_map/all_to_all | solution.py:562
  35.1 16.8 %all-to-all-start.1 = ((bf16[8,304,128]{2,1,0:T(8,128)(2,1)}), bf16[8,304,128]{2,1,0:T(8,128)(2,1)S(1)}, u32[]{:S(2)}, u32[]{:S(2)}) async-start(bf16[8,304,128]{2,1,0:T(8,128)(2,1)} %pad_maximum_fusion.rest_2_), calls=%async_computation.1 | async-start | bytes 1245184 | tf_op jit(solution)/shard_map/all_to_all | solution.py:565
  40.6 11.3 %copy-start.13 = (bf16[768,768]{1,0:T(8,128)(2,1)S(1)}, bf16[768,768]{1,0:T(8,128)(2,1)}, u32[]{:S(2)}) copy-start(bf16[768,768]{1,0:T(8,128)(2,1)} %merge_ref.3) | copy-start | bytes 3538948
  40.6 11.3 %copy-start.14 = (bf16[768,128]{1,0:T(8,128)(2,1)S(1)}, bf16[768,128]{1,0:T(8,128)(2,1)}, u32[]{:S(2)}) copy-start(bf16[768,128]{1,0:T(8,128)(2,1)} %down_ref.3) | copy-start | bytes 589828
  51.9 20.8 %copy-start = (bf16[128,256,128]{2,1,0:T(8,128)(2,1)S(1)}, bf16[128,256,128]{2,1,0:T(8,128)(2,1)}, u32[]{:S(2)}) copy-start(bf16[128,256,128]{2,1,0:T(8,128)(2,1)} %get-tuple-element.30.standard_ref) | copy-start | bytes 25165828
  51.9 20.8 %copy-start.6 = (bf16[128,16]{0,1:T(8,128)(2,1)S(1)}, bf16[128,16]{0,1:T(8,128)(2,1)}, u32[]{:S(2)}) copy-start(bf16[128,16]{0,1:T(8,128)(2,1)} %param.28) | copy-start | bytes 12292
  51.9 20.8 %copy-start.9 = (f32[128]{0:T(128)S(1)}, f32[128]{0:T(128)}, u32[]{:S(2)}) copy-start(f32[128]{0:T(128)} %gain_ref.9) | copy-start | bytes 1540

commit v4 on v3

--- a/solution.py
+++ b/solution.py
@@ -459,7 +459,7 @@
 def gradient_kernel(
     weight_ref, grad_ref, small_ref, standard_ref, received_ref, own_ref, gain_ref, bias_weight_ref,
     state_ref, hidden_ref, counts_ref, merge_ref, down_ref, position_ref,
-    out_ref, positions_ref, update_ref, block_ref, ones_ref, factor_ref, inner_ref,
+    out_hbm, positions_ref, update_ref, block_ref, ones_ref, factor_ref, inner_ref, slots_ref, semaphores,
 ):
     step = pl.program_id(0)
     heads, width = bias_weight_ref.shape
@@ -481,13 +481,22 @@
             ones = jnp.where(mine, 1.0, 0.0).astype(BF16)
             ones_ref[:LANES, at] = ones
             ones_ref[LANES:, at] = ones
-        top, scales, total, inner = combined(received_ref, rows)
+        top, _, total, inner = combined(received_ref, rows)
         factor_ref[...] = jnp.exp(own_ref[0, :rows, :].astype(F32) - top) / total
         inner_ref[...] = inner / total
-        update_tokens(
-            received_ref, state_ref, hidden_ref, counts_ref, merge_ref, down_ref, position_ref,
-            positions_ref, update_ref, scales, total,
+
+    steps = pl.num_programs(0)
+    slot = step % 2
+    count = slots_ref.shape[1]
+
+    def out_copy(at):
+        return pltpu.make_async_copy(
+            slots_ref.at[at % 2], out_hbm.at[pl.ds(at * count, count)], semaphores.at[at % 2]
         )
+
+    @pl.when(step >= 2)
+    def _():
+        out_copy(step - 2).wait()
 
     keys = weight_ref.shape[0]
     lefts, rights = [], []
@@ -509,7 +518,19 @@
             for k in range(2):
                 part = (slice(q * keys, (q + 1) * keys), slice(k * width, (k + 1) * width))
                 r = q * GROUP + i + k
-                out_ref[r] = (direct[part] - standard_ref[r].astype(F32) * along[part]).astype(BF16)
+                slots_ref[slot, r] = (direct[part] - standard_ref[r].astype(F32) * along[part]).astype(BF16)
+
+    out_copy(step).start()
+
+    @pl.when(step == steps - 1)
+    def _():
+        _, scales, total, _ = combined(received_ref, rows)
+        update_tokens(
+            received_ref, state_ref, hidden_ref, counts_ref, merge_ref, down_ref, position_ref,
+            positions_ref, update_ref, scales, total,
+        )
+        out_copy(step - 1).wait()
+        out_copy(step).wait()
 
 
 def gradient_stage(weights, grad, small, standard, received, own, gain, bias_weight, state, hidden, counts, merge, down, weight):
@@ -525,13 +546,15 @@
         gradient_kernel,
         grid=(rows // GROUP // STACK,),
         in_specs=[tile, tile, tile, block] + [whole(a) for a in arrays],
-        out_specs=(block, *(whole(a) for a in outs)),
+        out_specs=(pl.BlockSpec(memory_space=pl.ANY), *(whole(a) for a in outs)),
         out_shape=(jax.ShapeDtypeStruct(standard.shape, BF16), *outs),
         scratch_shapes=[
             pltpu.VMEM((2 * LANES, GROUP * width), BF16),
             pltpu.VMEM((2 * LANES, GROUP * width), BF16),
             pltpu.VMEM((rows // GROUP, LANES), F32),
             pltpu.VMEM((rows // GROUP, LANES), F32),
+            pltpu.VMEM((2, STACK * GROUP, keys, width), BF16),
+            pltpu.SemaphoreType.DMA((2,)),
         ],
         compiler_params=pltpu.CompilerParams(vmem_limit_bytes=GRADIENT_LIMIT * MIB),
         cost_estimate=pl.CostEstimate(flops=16000 * MIB, bytes_accessed=22 * MIB, transcendentals=0),

time: 81.5 us -> 81.1 us (level)
  no operation moved by 1% of the time
where the time goes in v4:
time: 81.1 us; the launch traced here: 80.6 us
  Pallas kernels  37.6 us (46%)
  starting transfers between devices  19.3 us (24%)
  blocking collectives  12.7 us (16%)
  waiting for transfers between devices  9.24 us (11%)
  other arithmetic  0.89 us (1%)
  between operations  0.84 us (1%)
    pallas_call x3, Pallas kernels, pair_forward(): pl.pallas_call(pair_kernel, grid=(count // PAIR_STACK,), in_specs=[pl.Blo...  18 us
    all_to_all x1, blocking collectives, per_device(): received = lax.all_to_all(payload, 'col', 0, 0)  12.7 us
    pallas_call x1, Pallas kernels, attend_stage(): pl.pallas_call(attend_kernel, grid=(steps,), in_specs=[whole(a) for a in...  8.13 us
    pallas_call x1, Pallas kernels, gradient_stage(): pl.pallas_call(gradient_kernel, grid=(rows // GROUP // STACK,), in_specs=...  7.86 us
    all_to_all x1, starting transfers between devices, per_device(): shared = lax.all_to_all(send, 'row', 0, 0)  7.29 us
    all_to_all x1, starting transfers between devices, per_device(): gathered = lax.all_to_all(mixed, 'col', 0, 0)  5.52 us
    ppermute x1, starting transfers between devices, per_device(): lax.ppermute(atom_feats, both, [(i, i + 1) for i in range(devices - 1)])  5.18 us
    all_to_all x1, waiting for transfers between devices, per_device(): gathered = lax.all_to_all(mixed, 'col', 0, 0)  4.76 us
  transfers between devices with their start and end apart: 4, of which 3 were waited for; matrix products, arithmetic and copies ran while one was open for 0% of the time, Pallas kernels for 22%

profile of v4, /device:TPU:0, one launch (start us, length us, event | category | flops | bytes accessed | tf_op | source)
XLA Modules:
  0.0 80.6 jit_solution(16111461228980450399)
XLA Ops:
  0.6 5.2 %collective-permute-start = (bf16[256,128]{1,0:T(8,128)(2,1)}, bf16[256,128]{1,0:T(8,128)(2,1)S(1)}, u32[]{:S(2)}, u32[]{:S(2)}) collective-permute-start(bf16[256,128]{1,0:T(8,128)(2,1)} %own_ref.1), channel_id=1, source_target_pairs={{0,1},{1,2},{2,3},{3,4},{4,5},{5,6},{6,7},{7,8},{8,9},{9,10},{10,1... | collective-permute-start | bytes 196616 | tf_op jit(solution)/shard_map/ppermute | solution.py:573
  5.8 1.3 %collective-permute-start.1 = (bf16[256,128]{1,0:T(8,128)(2,1)}, bf16[256,128]{1,0:T(8,128)(2,1)S(1)}, u32[]{:S(2)}, u32[]{:S(2)}) collective-permute-start(bf16[256,128]{1,0:T(8,128)(2,1)} %own_ref.1), channel_id=1, source_target_pairs={{1,0},{2,1},{3,2},{4,3},{5,4},{6,5},{7,6},{8,7},{9,8},{10,9},{11,1... | collective-permute-start | bytes 196616 | tf_op jit(solution)/shard_map/ppermute | solution.py:574
  7.1 0.0 copy-start.1
  7.1 0.0 copy-start.2
  7.1 0.0 copy-start.3
  7.2 0.0 copy-start.4
  7.2 0.0 copy-start.5
  7.2 0.0 copy-start.7
  7.2 0.0 copy-start.8
  7.2 0.0 copy-start.10
  7.2 0.0 copy-start.11
  7.2 0.0 copy-start.12
  7.2 4.9 %pair_forward.3 = (f32[8,256,2048]{2,1,0:T(8,128)}, bf16[128,256,128]{2,1,0:T(8,128)(2,1)}) custom-call(bf16[128,256,128]{2,1,0:T(8,128)(2,1)} %x_ref.5, f32[128]{0:T(128)} %gain_ref.9, bf16[16,128]{1,0:T(8,128)(2,1)} %bitcast.2), custom_call_target="tpu_custom_call" | custom-call | flops 5242880000 | bytes 5242880 | tf_op jit(solution)/shard_map/pair_forward/pallas_call | solution.py:114
  12.2 0.0 collective-permute-done.left_ref
  12.2 1.5 %collective-permute-done.1.right_ref = bf16[256,128]{1,0:T(8,128)(2,1)S(1)} collective-permute-done((bf16[256,128]{1,0:T(8,128)(2,1)}, bf16[256,128]{1,0:T(8,128)(2,1)S(1)}, u32[]{:S(2)}, u32[]{:S(2)}) %collective-permute-start.1) | collective-permute-done | bytes 65568 | tf_op jit(solution)/shard_map/ppermute | solution.py:574
  13.7 0.0 copy-done.1
  13.7 0.0 copy-done.2
  13.7 0.0 copy-done.3
  13.7 0.0 copy-done.4
  13.7 0.0 copy-done.5
  13.7 0.0 copy-done.7
  13.7 0.0 copy-done.8
  13.7 0.0 copy-done.10
  13.8 0.0 copy-done.11
  13.8 0.0 copy-done.12
  13.8 3.6 %atom_stage.1 = (bf16[256,128]{1,0:T(8,128)(2,1)S(1)}, f32[16,768]{1,0:T(8,128)S(1)}, bf16[112,128]{1,0:T(8,128)(2,1)S(1)}, bf16[16,96,128]{2,1,0:T(8,128)(2,1)}) custom-call(bf16[256,128]{1,0:T(8,128)(2,1)S(1)} %collective-permute-done.left_ref, bf16[256,128]{1,0:T(8,128)(2,1)S(1)} %copy-done.3, bf16[256,128]{1,0:T(8,128)(2,1)S(1)} %collective-permute-done.1.right_ref, ...), custom_call_target="tpu_custom_call" | custom-call | flops 419430400 | bytes 2097152 | tf_op jit(solution)/shard_map/atom_stage/pallas_call | solution.py:225
  17.4 7.3 %all-to-all-start = ((bf16[16,96,128]{2,1,0:T(8,128)(2,1)}), bf16[16,96,128]{2,1,0:T(8,128)(2,1)S(1)}, u32[]{:S(2)}, u32[]{:S(2)}) async-start(bf16[16,96,128]{2,1,0:T(8,128)(2,1)} %get-tuple-element.21.rest_2_), calls=%async_computation | async-start | bytes 786432 | tf_op jit(solution)/shard_map/all_to_all | solution.py:585
  24.7 6.5 %pair_forward.4 = (f32[8,256,2048]{2,1,0:T(8,128)}, bf16[128,256,128]{2,1,0:T(8,128)(2,1)}) custom-call(bf16[128,256,128]{2,1,0:T(8,128)(2,1)} %x_ref.5, f32[128]{0:T(128)} %gain_ref.9, bf16[16,128]{1,0:T(8,128)(2,1)} %bitcast.3, f32[8,256,2048]{2,1,0:T(8,128)} %get-tuple-element.20._.rest_0_, ...), custom_call_target="tpu_custom_call", output_to_operand_aliasing={{0}: (3, {}), {1}: (4, {})} | custom-call | flops 7864320000 | bytes 7864320 | tf_op jit(solution)/shard_map/pair_forward/pallas_call | solution.py:114
  31.2 2.9 %all-to-all-done = bf16[16,96,128]{2,1,0:T(8,128)(2,1)S(1)} async-done(((bf16[16,96,128]{2,1,0:T(8,128)(2,1)}), bf16[16,96,128]{2,1,0:T(8,128)(2,1)S(1)}, u32[]{:S(2)}, u32[]{:S(2)}) %all-to-all-start) | async-done | bytes 393248 | tf_op jit(solution)/shard_map/all_to_all | solution.py:585
  34.2 0.9 %pad_maximum_fusion.rest_2_ = bf16[8,304,128]{2,1,0:T(8,128)(2,1)} fusion(bf16[8,112,128]{2,1,0:T(8,128)(2,1)S(1)} %broadcast_in_dim.2, bf16[8,192,128]{2,1,0:T(8,128)(2,1)S(1)} %bitcast.6), kind=kLoop, calls=%fused_computation | loop fusion | flops 1245184 | bytes 1245184 | tf_op jit(solution)/shard_map/concatenate | solution.py:587
  35.1 5.5 %all-to-all-start.1 = ((bf16[8,304,128]{2,1,0:T(8,128)(2,1)}), bf16[8,304,128]{2,1,0:T(8,128)(2,1)S(1)}, u32[]{:S(2)}, u32[]{:S(2)}) async-start(bf16[8,304,128]{2,1,0:T(8,128)(2,1)} %pad_maximum_fusion.rest_2_), calls=%async_computation.1 | async-start | bytes 1245184 | tf_op jit(solution)/shard_map/all_to_all | solution.py:588
  40.6 0.0 copy-start.13
  40.6 0.0 copy-start.14
  40.6 6.5 %pair_forward.5 = (f32[8,256,2048]{2,1,0:T(8,128)}, bf16[128,256,128]{2,1,0:T(8,128)(2,1)}) custom-call(bf16[128,256,128]{2,1,0:T(8,128)(2,1)} %x_ref.5, f32[128]{0:T(128)} %gain_ref.9, bf16[16,128]{1,0:T(8,128)(2,1)} %bitcast.4, f32[8,256,2048]{2,1,0:T(8,128)} %get-tuple-element.24.rest_0_, ...), custom_call_target="tpu_custom_call", output_to_operand_aliasing={{0}: (3, {}), {1}: (4, {})} | custom-call | flops 7864320000 | bytes 7864320 | tf_op jit(solution)/shard_map/pair_forward/pallas_call | solution.py:114
  47.2 4.8 %all-to-all-done.1.gathered_ref = bf16[8,304,128]{2,1,0:T(8,128)(2,1)S(1)} async-done(((bf16[8,304,128]{2,1,0:T(8,128)(2,1)}), bf16[8,304,128]{2,1,0:T(8,128)(2,1)S(1)}, u32[]{:S(2)}, u32[]{:S(2)}) %all-to-all-start.1) | async-done | bytes 622624 | tf_op jit(solution)/shard_map/all_to_all | solution.py:588
  51.9 0.0 copy-done.13
  51.9 0.0 copy-done.14
  51.9 0.0 copy-start
  51.9 0.0 copy-start.6
  51.9 0.0 copy-start.9
  52.0 8.1 %attend_stage.1 = (bf16[256,2048]{1,0:T(8,128)(2,1)S(1)}, f32[256,2048]{1,0:T(8,128)S(1)}, bf16[256,2048]{1,0:T(8,128)(2,1)S(1)}, bf16[8,176,128]{2,1,0:T(8,128)(2,1)S(1)}) custom-call(bf16[8,304,128]{2,1,0:T(8,128)(2,1)S(1)} %all-to-all-done.1.gathered_ref, bf16[768,128]{1,0:T(8,128)(2,1)S(1)} %copy-done.14, bf16[768,2304]{1,0:T(8,128)(2,1)} %project_hbm.1, ...), custom_call_target="tpu_custom_call" | custom-call | flops 8388608000 | bytes 12582912 | tf_op jit(solution)/shard_map/attend_stage/pallas_call | solution.py:360
  60.1 12.7 %all_to_all.15.received_ref = bf16[8,176,128]{2,1,0:T(8,128)(2,1)S(1)} all-to-all(bf16[8,176,128]{2,1,0:T(8,128)(2,1)S(1)} %get-tuple-element.31.own_ref), channel_id=1, replica_groups=mesh['row'=16,'col'=8] {'col'}, dimensions={0} | all-to-all | bytes 720896 | tf_op jit(solution)/shard_map/all_to_all | solution.py:595
  72.8 0.0 copy-done
  72.8 0.0 copy-done.6
  72.8 0.0 copy-done.9
  72.8 7.9 %gradient_stage.1 = (bf16[128,256,128]{2,1,0:T(8,128)(2,1)}, f32[3,256]{1,0:T(4,128)}, bf16[16,768]{1,0:T(8,128)(2,1)}) custom-call(bf16[256,2048]{1,0:T(8,128)(2,1)S(1)} %get-tuple-element.27.weight_ref, f32[256,2048]{1,0:T(8,128)S(1)} %get-tuple-element.28.grad_ref, bf16[256,2048]{1,0:T(8,128)(2,1)S(1)} %get-tuple-element.29.small_ref, ...), custom_call_target="tpu_custom_call" | custom-call | flops 16777216000 | bytes 23068672 | tf_op jit(solution)/shard_map/gradient_stage/pallas_call | solution.py:545
  (1 shorter events, 0.0 us)
Async XLA Ops:
  0.6 11.5 %collective-permute-start = (bf16[256,128]{1,0:T(8,128)(2,1)}, bf16[256,128]{1,0:T(8,128)(2,1)S(1)}, u32[]{:S(2)}, u32[]{:S(2)}) collective-permute-start(bf16[256,128]{1,0:T(8,128)(2,1)} %own_ref.1), channel_id=1, source_target_pairs={{0,1},{1,2},{2,3},{3,4},{4,5},{5,6},{6,7},{7,8},{8,9},{9,10},{10,1... | collective-permute-start | bytes 196616 | tf_op jit(solution)/shard_map/ppermute | solution.py:573
  5.8 7.9 %collective-permute-start.1 = (bf16[256,128]{1,0:T(8,128)(2,1)}, bf16[256,128]{1,0:T(8,128)(2,1)S(1)}, u32[]{:S(2)}, u32[]{:S(2)}) collective-permute-start(bf16[256,128]{1,0:T(8,128)(2,1)} %own_ref.1), channel_id=1, source_target_pairs={{1,0},{2,1},{3,2},{4,3},{5,4},{6,5},{7,6},{8,7},{9,8},{10,9},{11,1... | collective-permute-start | bytes 196616 | tf_op jit(solution)/shard_map/ppermute | solution.py:574
  7.1 6.6 %copy-start.1 = (bf16[128,768]{1,0:T(8,128)(2,1)S(1)}, bf16[128,768]{1,0:T(8,128)(2,1)}, u32[]{:S(2)}) copy-start(bf16[128,768]{1,0:T(8,128)(2,1)} %up_ref.1) | copy-start | bytes 589828
  7.1 6.6 %copy-start.2 = (bf16[128,384]{1,0:T(8,128)(2,1)S(1)}, bf16[128,384]{1,0:T(8,128)(2,1)}, u32[]{:S(2)}) copy-start(bf16[128,384]{1,0:T(8,128)(2,1)} %project_ref.1) | copy-start | bytes 294916
  7.1 6.6 %copy-start.3 = (bf16[256,128]{1,0:T(8,128)(2,1)S(1)}, bf16[256,128]{1,0:T(8,128)(2,1)}, u32[]{:S(2)}) copy-start(bf16[256,128]{1,0:T(8,128)(2,1)} %own_ref.1) | copy-start | bytes 196612
  7.2 6.6 %copy-start.4 = (bf16[128,128]{1,0:T(8,128)(2,1)S(1)}, bf16[128,128]{1,0:T(8,128)(2,1)}, u32[]{:S(2)}) copy-start(bf16[128,128]{1,0:T(8,128)(2,1)} %merge_ref.2) | copy-start | bytes 98308
  7.2 6.6 %copy-start.5 = (bf16[16,768]{1,0:T(8,128)(2,1)S(1)}, bf16[16,768]{1,0:T(8,128)(2,1)}, u32[]{:S(2)}) copy-start(bf16[16,768]{1,0:T(8,128)(2,1)} %single_ref.1) | copy-start | bytes 73732
  7.2 6.6 %copy-start.7 = (f32[768]{0:T(1024)S(1)}, f32[768]{0:T(1024)}, u32[]{:S(2)}) copy-start(f32[768]{0:T(1024)} %token_gain_ref.1) | copy-start | bytes 9220
  7.2 6.6 %copy-start.8 = (f32[3,256]{1,0:T(4,128)S(1)}, f32[3,256]{1,0:T(4,128)}, u32[]{:S(2)}) copy-start(f32[3,256]{1,0:T(4,128)} %cotangent_ref.1) | copy-start | bytes 9220
  7.2 6.6 %copy-start.10 = (bf16[3,128]{1,0:T(4,128)(2,1)S(1)}, bf16[3,128]{1,0:T(4,128)(2,1)}, u32[]{:S(2)}) copy-start(bf16[3,128]{1,0:T(4,128)(2,1)} %position_ref.1) | copy-start | bytes 2308
  7.2 6.6 %copy-start.11 = (f32[128]{0:T(128)S(1)}, f32[128]{0:T(128)}, u32[]{:S(2)}) copy-start(f32[128]{0:T(128)} %gain_ref.6) | copy-start | bytes 1540
  7.2 6.6 %copy-start.12 = (s32[1,16]{1,0:T(1,128)S(1)}, s32[1,16]{1,0:T(1,128)}, u32[]{:S(2)}) copy-start(s32[1,16]{1,0:T(1,128)} %counts_ref.3) | copy-start | bytes 196
  17.4 16.8 %all-to-all-start = ((bf16[16,96,128]{2,1,0:T(8,128)(2,1)}), bf16[16,96,128]{2,1,0:T(8,128)(2,1)S(1)}, u32[]{:S(2)}, u32[]{:S(2)}) async-start(bf16[16,96,128]{2,1,0:T(8,128)(2,1)} %get-tuple-element.21.rest_2_), calls=%async_computation | async-start | bytes 786432 | tf_op jit(solution)/shard_map/all_to_all | solution.py:585
  35.1 16.8 %all-to-all-start.1 = ((bf16[8,304,128]{2,1,0:T(8,128)(2,1)}), bf16[8,304,128]{2,1,0:T(8,128)(2,1)S(1)}, u32[]{:S(2)}, u32[]{:S(2)}) async-start(bf16[8,304,128]{2,1,0:T(8,128)(2,1)} %pad_maximum_fusion.rest_2_), calls=%async_computation.1 | async-start | bytes 1245184 | tf_op jit(solution)/shard_map/all_to_all | solution.py:588
  40.6 11.3 %copy-start.13 = (bf16[768,768]{1,0:T(8,128)(2,1)S(1)}, bf16[768,768]{1,0:T(8,128)(2,1)}, u32[]{:S(2)}) copy-start(bf16[768,768]{1,0:T(8,128)(2,1)} %merge_ref.3) | copy-start | bytes 3538948
  40.6 11.3 %copy-start.14 = (bf16[768,128]{1,0:T(8,128)(2,1)S(1)}, bf16[768,128]{1,0:T(8,128)(2,1)}, u32[]{:S(2)}) copy-start(bf16[768,128]{1,0:T(8,128)(2,1)} %down_ref.3) | copy-start | bytes 589828
  51.9 20.8 %copy-start = (bf16[128,256,128]{2,1,0:T(8,128)(2,1)S(1)}, bf16[128,256,128]{2,1,0:T(8,128)(2,1)}, u32[]{:S(2)}) copy-start(bf16[128,256,128]{2,1,0:T(8,128)(2,1)} %get-tuple-element.30.standard_ref) | copy-start | bytes 25165828
  51.9 20.8 %copy-start.6 = (bf16[128,16]{0,1:T(8,128)(2,1)S(1)}, bf16[128,16]{0,1:T(8,128)(2,1)}, u32[]{:S(2)}) copy-start(bf16[128,16]{0,1:T(8,128)(2,1)} %param.28) | copy-start | bytes 12292
  51.9 20.8 %copy-start.9 = (f32[128]{0:T(128)S(1)}, f32[128]{0:T(128)}, u32[]{:S(2)}) copy-start(f32[128]{0:T(128)} %gain_ref.9) | copy-start | bytes 1540

commit v5 on v4

--- a/solution.py
+++ b/solution.py
@@ -1,5 +1,3 @@
-import math
-
 import jax
 import jax.numpy as jnp
 from jax import lax
@@ -167,7 +165,7 @@
         at = b * WINDOW
         queries = jnp.concatenate([query_ref[at : at + WINDOW, :]] * ATOM_HEADS, axis=0)
         queries = jnp.where(mask, queries.astype(F32), 0.0).astype(BF16)
-        scores = dot_nt(queries, key_ref[at : at + KEYS, :]) / math.sqrt(size)
+        scores = dot_nt(queries, key_ref[at : at + KEYS, :]) * size**-0.5
         position = first - LEFT + at + key_index
         scores = jnp.where((position >= 0) & (position < total), scores, NEGATIVE)
         weights = jnp.exp(scores - jnp.max(scores, axis=1, keepdims=True))
@@ -312,7 +310,7 @@
         inside = slice(sub * part_lanes, (sub + 1) * part_lanes)
         lanes = pl.ds(pl.multiple_of(at * part_lanes, part_lanes), part_lanes)
         bias = terms_ref[0, :, lanes]
-        scores = dot_nt(key_ref[...], expanded(query_ref, at)) / math.sqrt(width // heads) + bias
+        scores = dot_nt(key_ref[...], expanded(query_ref, at)) * (width // heads) ** -0.5 + bias
         grad_probs = dot_nt(values, expanded(mix_ref, at))
         row_max = jnp.max(scores, axis=0, keepdims=True).astype(BF16).astype(F32)
         weights = jnp.exp(scores - row_max)
@@ -322,7 +320,7 @@
         inner = jnp.sum(rounded.astype(F32) * grad_probs, axis=0, keepdims=True)
         weight_ref[:, inside] = (weights * terms_ref[1, :, lanes]).astype(BF16)
         grad_ref[:, inside] = grad_probs
-        small_ref[:, inside] = (bias * (1.0 / LANES)).astype(BF16)
+        small_ref[:, inside] = bias.astype(BF16)
         for k, stat in enumerate((row_max, row_total, inner)):
             for p in range(part_lanes // LANES):
                 row = k * stat_rows + at * (part_lanes // LANES) + p
@@ -478,7 +476,7 @@
             at = slice(i * width, (i + 1) * width)
             block_ref[:LANES, at] = jnp.where(mine, high.astype(F32), 0.0).astype(BF16)
             block_ref[LANES:, at] = jnp.where(mine, low.astype(F32), 0.0).astype(BF16)
-            ones = jnp.where(mine, 1.0, 0.0).astype(BF16)
+            ones = jnp.where(mine, 1.0 / width, 0.0).astype(BF16)
             ones_ref[:LANES, at] = ones
             ones_ref[LANES:, at] = ones
         top, _, total, inner = combined(received_ref, rows)
@@ -570,8 +568,8 @@
     both = ("row", "col")
     rows, columns = lax.axis_size("row"), lax.axis_size("col")
     devices = rows * columns
+    right = lax.ppermute(atom_feats, both, [(i + 1, i) for i in range(devices - 1)])
     left = lax.ppermute(atom_feats, both, [(i, i + 1) for i in range(devices - 1)])
-    right = lax.ppermute(atom_feats, both, [(i + 1, i) for i in range(devices - 1)])
     gain = pair_gain
     bias_turned = bias_weight.T
     groups = pair_state.shape[0] // GROUP

time: 81.1 us -> 81.1 us (level)
  no operation moved by 1% of the time
where the time goes in v5:
time: 81.1 us; the launch traced here: 80.6 us
  Pallas kernels  37.6 us (46%)
  starting transfers between devices  19.3 us (24%)
  blocking collectives  12.7 us (16%)
  waiting for transfers between devices  9.24 us (11%)
  other arithmetic  0.89 us (1%)
  between operations  0.84 us (1%)
    pallas_call x3, Pallas kernels, pair_forward(): pl.pallas_call(pair_kernel, grid=(count // PAIR_STACK,), in_specs=[pl.Blo...  18 us
    all_to_all x1, blocking collectives, per_device(): received = lax.all_to_all(payload, 'col', 0, 0)  12.7 us
    pallas_call x1, Pallas kernels, attend_stage(): pl.pallas_call(attend_kernel, grid=(steps,), in_specs=[whole(a) for a in...  8.1 us
    pallas_call x1, Pallas kernels, gradient_stage(): pl.pallas_call(gradient_kernel, grid=(rows // GROUP // STACK,), in_specs=...  7.86 us
    all_to_all x1, starting transfers between devices, per_device(): shared = lax.all_to_all(send, 'row', 0, 0)  7.29 us
    all_to_all x1, starting transfers between devices, per_device(): gathered = lax.all_to_all(mixed, 'col', 0, 0)  5.52 us
    ppermute x1, starting transfers between devices, per_device(): lax.ppermute(atom_feats, both, [(i, i + 1) for i in range(devices - 1)])  5.18 us
    all_to_all x1, waiting for transfers between devices, per_device(): gathered = lax.all_to_all(mixed, 'col', 0, 0)  4.76 us
  transfers between devices with their start and end apart: 4, of which 3 were waited for; matrix products, arithmetic and copies ran while one was open for 0% of the time, Pallas kernels for 22%

profile of v5, /device:TPU:0, one launch (start us, length us, event | category | flops | bytes accessed | tf_op | source)
XLA Modules:
  0.0 80.6 jit_solution(9295473277987336454)
XLA Ops:
  0.6 5.2 %collective-permute-start = (bf16[256,128]{1,0:T(8,128)(2,1)}, bf16[256,128]{1,0:T(8,128)(2,1)S(1)}, u32[]{:S(2)}, u32[]{:S(2)}) collective-permute-start(bf16[256,128]{1,0:T(8,128)(2,1)} %own_ref.1), channel_id=1, source_target_pairs={{0,1},{1,2},{2,3},{3,4},{4,5},{5,6},{6,7},{7,8},{8,9},{9,10},{10,1... | collective-permute-start | bytes 196616 | tf_op jit(solution)/shard_map/ppermute | solution.py:572
  5.8 1.3 %collective-permute-start.1 = (bf16[256,128]{1,0:T(8,128)(2,1)}, bf16[256,128]{1,0:T(8,128)(2,1)S(1)}, u32[]{:S(2)}, u32[]{:S(2)}) collective-permute-start(bf16[256,128]{1,0:T(8,128)(2,1)} %own_ref.1), channel_id=1, source_target_pairs={{1,0},{2,1},{3,2},{4,3},{5,4},{6,5},{7,6},{8,7},{9,8},{10,9},{11,1... | collective-permute-start | bytes 196616 | tf_op jit(solution)/shard_map/ppermute | solution.py:571
  7.1 0.0 copy-start.1
  7.1 0.0 copy-start.2
  7.1 0.0 copy-start.3
  7.2 0.0 copy-start.4
  7.2 0.0 copy-start.5
  7.2 0.0 copy-start.7
  7.2 0.0 copy-start.8
  7.2 0.0 copy-start.10
  7.2 0.0 copy-start.11
  7.2 0.0 copy-start.12
  7.2 4.9 %pair_forward.3 = (f32[8,256,2048]{2,1,0:T(8,128)}, bf16[128,256,128]{2,1,0:T(8,128)(2,1)}) custom-call(bf16[128,256,128]{2,1,0:T(8,128)(2,1)} %x_ref.5, f32[128]{0:T(128)} %gain_ref.9, bf16[16,128]{1,0:T(8,128)(2,1)} %bitcast.2), custom_call_target="tpu_custom_call" | custom-call | flops 5242880000 | bytes 5242880 | tf_op jit(solution)/shard_map/pair_forward/pallas_call | solution.py:112
  12.2 0.0 collective-permute-done.left_ref
  12.2 1.5 %collective-permute-done.1.right_ref = bf16[256,128]{1,0:T(8,128)(2,1)S(1)} collective-permute-done((bf16[256,128]{1,0:T(8,128)(2,1)}, bf16[256,128]{1,0:T(8,128)(2,1)S(1)}, u32[]{:S(2)}, u32[]{:S(2)}) %collective-permute-start.1) | collective-permute-done | bytes 65568 | tf_op jit(solution)/shard_map/ppermute | solution.py:571
  13.7 0.0 copy-done.1
  13.7 0.0 copy-done.2
  13.7 0.0 copy-done.3
  13.7 0.0 copy-done.4
  13.7 0.0 copy-done.5
  13.7 0.0 copy-done.7
  13.7 0.0 copy-done.8
  13.7 0.0 copy-done.10
  13.8 0.0 copy-done.11
  13.8 0.0 copy-done.12
  13.8 3.6 %atom_stage.1 = (bf16[256,128]{1,0:T(8,128)(2,1)S(1)}, f32[16,768]{1,0:T(8,128)S(1)}, bf16[112,128]{1,0:T(8,128)(2,1)S(1)}, bf16[16,96,128]{2,1,0:T(8,128)(2,1)}) custom-call(bf16[256,128]{1,0:T(8,128)(2,1)S(1)} %collective-permute-done.left_ref, bf16[256,128]{1,0:T(8,128)(2,1)S(1)} %copy-done.3, bf16[256,128]{1,0:T(8,128)(2,1)S(1)} %collective-permute-done.1.right_ref, ...), custom_call_target="tpu_custom_call" | custom-call | flops 419430400 | bytes 2097152 | tf_op jit(solution)/shard_map/atom_stage/pallas_call | solution.py:223
  17.4 7.3 %all-to-all-start = ((bf16[16,96,128]{2,1,0:T(8,128)(2,1)}), bf16[16,96,128]{2,1,0:T(8,128)(2,1)S(1)}, u32[]{:S(2)}, u32[]{:S(2)}) async-start(bf16[16,96,128]{2,1,0:T(8,128)(2,1)} %get-tuple-element.21.rest_2_), calls=%async_computation | async-start | bytes 786432 | tf_op jit(solution)/shard_map/all_to_all | solution.py:583
  24.7 6.5 %pair_forward.4 = (f32[8,256,2048]{2,1,0:T(8,128)}, bf16[128,256,128]{2,1,0:T(8,128)(2,1)}) custom-call(bf16[128,256,128]{2,1,0:T(8,128)(2,1)} %x_ref.5, f32[128]{0:T(128)} %gain_ref.9, bf16[16,128]{1,0:T(8,128)(2,1)} %bitcast.3, f32[8,256,2048]{2,1,0:T(8,128)} %get-tuple-element.20._.rest_0_, ...), custom_call_target="tpu_custom_call", output_to_operand_aliasing={{0}: (3, {}), {1}: (4, {})} | custom-call | flops 7864320000 | bytes 7864320 | tf_op jit(solution)/shard_map/pair_forward/pallas_call | solution.py:112
  31.2 2.9 %all-to-all-done = bf16[16,96,128]{2,1,0:T(8,128)(2,1)S(1)} async-done(((bf16[16,96,128]{2,1,0:T(8,128)(2,1)}), bf16[16,96,128]{2,1,0:T(8,128)(2,1)S(1)}, u32[]{:S(2)}, u32[]{:S(2)}) %all-to-all-start) | async-done | bytes 393248 | tf_op jit(solution)/shard_map/all_to_all | solution.py:583
  34.2 0.9 %pad_maximum_fusion.rest_2_ = bf16[8,304,128]{2,1,0:T(8,128)(2,1)} fusion(bf16[8,112,128]{2,1,0:T(8,128)(2,1)S(1)} %broadcast_in_dim.2, bf16[8,192,128]{2,1,0:T(8,128)(2,1)S(1)} %bitcast.6), kind=kLoop, calls=%fused_computation | loop fusion | flops 1245184 | bytes 1245184 | tf_op jit(solution)/shard_map/concatenate | solution.py:585
  35.1 5.5 %all-to-all-start.1 = ((bf16[8,304,128]{2,1,0:T(8,128)(2,1)}), bf16[8,304,128]{2,1,0:T(8,128)(2,1)S(1)}, u32[]{:S(2)}, u32[]{:S(2)}) async-start(bf16[8,304,128]{2,1,0:T(8,128)(2,1)} %pad_maximum_fusion.rest_2_), calls=%async_computation.1 | async-start | bytes 1245184 | tf_op jit(solution)/shard_map/all_to_all | solution.py:586
  40.6 0.0 copy-start.13
  40.6 0.0 copy-start.14
  40.6 6.5 %pair_forward.5 = (f32[8,256,2048]{2,1,0:T(8,128)}, bf16[128,256,128]{2,1,0:T(8,128)(2,1)}) custom-call(bf16[128,256,128]{2,1,0:T(8,128)(2,1)} %x_ref.5, f32[128]{0:T(128)} %gain_ref.9, bf16[16,128]{1,0:T(8,128)(2,1)} %bitcast.4, f32[8,256,2048]{2,1,0:T(8,128)} %get-tuple-element.24.rest_0_, ...), custom_call_target="tpu_custom_call", output_to_operand_aliasing={{0}: (3, {}), {1}: (4, {})} | custom-call | flops 7864320000 | bytes 7864320 | tf_op jit(solution)/shard_map/pair_forward/pallas_call | solution.py:112
  47.2 4.8 %all-to-all-done.1.gathered_ref = bf16[8,304,128]{2,1,0:T(8,128)(2,1)S(1)} async-done(((bf16[8,304,128]{2,1,0:T(8,128)(2,1)}), bf16[8,304,128]{2,1,0:T(8,128)(2,1)S(1)}, u32[]{:S(2)}, u32[]{:S(2)}) %all-to-all-start.1) | async-done | bytes 622624 | tf_op jit(solution)/shard_map/all_to_all | solution.py:586
  51.9 0.0 copy-done.13
  51.9 0.0 copy-done.14
  51.9 0.0 copy-start
  51.9 0.0 copy-start.6
  51.9 0.0 copy-start.9
  52.0 8.1 %attend_stage.1 = (bf16[256,2048]{1,0:T(8,128)(2,1)S(1)}, f32[256,2048]{1,0:T(8,128)S(1)}, bf16[256,2048]{1,0:T(8,128)(2,1)S(1)}, bf16[8,176,128]{2,1,0:T(8,128)(2,1)S(1)}) custom-call(bf16[8,304,128]{2,1,0:T(8,128)(2,1)S(1)} %all-to-all-done.1.gathered_ref, bf16[768,128]{1,0:T(8,128)(2,1)S(1)} %copy-done.14, bf16[768,2304]{1,0:T(8,128)(2,1)} %project_hbm.1, ...), custom_call_target="tpu_custom_call" | custom-call | flops 8388608000 | bytes 12582912 | tf_op jit(solution)/shard_map/attend_stage/pallas_call | solution.py:358
  60.1 12.7 %all_to_all.15.received_ref = bf16[8,176,128]{2,1,0:T(8,128)(2,1)S(1)} all-to-all(bf16[8,176,128]{2,1,0:T(8,128)(2,1)S(1)} %get-tuple-element.31.own_ref), channel_id=1, replica_groups=mesh['row'=16,'col'=8] {'col'}, dimensions={0} | all-to-all | bytes 720896 | tf_op jit(solution)/shard_map/all_to_all | solution.py:593
  72.7 0.0 copy-done
  72.7 0.0 copy-done.6
  72.7 0.0 copy-done.9
  72.7 7.9 %gradient_stage.1 = (bf16[128,256,128]{2,1,0:T(8,128)(2,1)}, f32[3,256]{1,0:T(4,128)}, bf16[16,768]{1,0:T(8,128)(2,1)}) custom-call(bf16[256,2048]{1,0:T(8,128)(2,1)S(1)} %get-tuple-element.27.weight_ref, f32[256,2048]{1,0:T(8,128)S(1)} %get-tuple-element.28.grad_ref, bf16[256,2048]{1,0:T(8,128)(2,1)S(1)} %get-tuple-element.29.small_ref, ...), custom_call_target="tpu_custom_call" | custom-call | flops 16777216000 | bytes 23068672 | tf_op jit(solution)/shard_map/gradient_stage/pallas_call | solution.py:543
  (1 shorter events, 0.0 us)
Async XLA Ops:
  0.6 11.5 %collective-permute-start = (bf16[256,128]{1,0:T(8,128)(2,1)}, bf16[256,128]{1,0:T(8,128)(2,1)S(1)}, u32[]{:S(2)}, u32[]{:S(2)}) collective-permute-start(bf16[256,128]{1,0:T(8,128)(2,1)} %own_ref.1), channel_id=1, source_target_pairs={{0,1},{1,2},{2,3},{3,4},{4,5},{5,6},{6,7},{7,8},{8,9},{9,10},{10,1... | collective-permute-start | bytes 196616 | tf_op jit(solution)/shard_map/ppermute | solution.py:572
  5.8 7.9 %collective-permute-start.1 = (bf16[256,128]{1,0:T(8,128)(2,1)}, bf16[256,128]{1,0:T(8,128)(2,1)S(1)}, u32[]{:S(2)}, u32[]{:S(2)}) collective-permute-start(bf16[256,128]{1,0:T(8,128)(2,1)} %own_ref.1), channel_id=1, source_target_pairs={{1,0},{2,1},{3,2},{4,3},{5,4},{6,5},{7,6},{8,7},{9,8},{10,9},{11,1... | collective-permute-start | bytes 196616 | tf_op jit(solution)/shard_map/ppermute | solution.py:571
  7.1 6.6 %copy-start.1 = (bf16[128,768]{1,0:T(8,128)(2,1)S(1)}, bf16[128,768]{1,0:T(8,128)(2,1)}, u32[]{:S(2)}) copy-start(bf16[128,768]{1,0:T(8,128)(2,1)} %up_ref.1) | copy-start | bytes 589828
  7.1 6.6 %copy-start.2 = (bf16[128,384]{1,0:T(8,128)(2,1)S(1)}, bf16[128,384]{1,0:T(8,128)(2,1)}, u32[]{:S(2)}) copy-start(bf16[128,384]{1,0:T(8,128)(2,1)} %project_ref.1) | copy-start | bytes 294916
  7.1 6.6 %copy-start.3 = (bf16[256,128]{1,0:T(8,128)(2,1)S(1)}, bf16[256,128]{1,0:T(8,128)(2,1)}, u32[]{:S(2)}) copy-start(bf16[256,128]{1,0:T(8,128)(2,1)} %own_ref.1) | copy-start | bytes 196612
  7.2 6.6 %copy-start.4 = (bf16[128,128]{1,0:T(8,128)(2,1)S(1)}, bf16[128,128]{1,0:T(8,128)(2,1)}, u32[]{:S(2)}) copy-start(bf16[128,128]{1,0:T(8,128)(2,1)} %merge_ref.2) | copy-start | bytes 98308
  7.2 6.6 %copy-start.5 = (bf16[16,768]{1,0:T(8,128)(2,1)S(1)}, bf16[16,768]{1,0:T(8,128)(2,1)}, u32[]{:S(2)}) copy-start(bf16[16,768]{1,0:T(8,128)(2,1)} %single_ref.1) | copy-start | bytes 73732
  7.2 6.6 %copy-start.7 = (f32[768]{0:T(1024)S(1)}, f32[768]{0:T(1024)}, u32[]{:S(2)}) copy-start(f32[768]{0:T(1024)} %token_gain_ref.1) | copy-start | bytes 9220
  7.2 6.6 %copy-start.8 = (f32[3,256]{1,0:T(4,128)S(1)}, f32[3,256]{1,0:T(4,128)}, u32[]{:S(2)}) copy-start(f32[3,256]{1,0:T(4,128)} %cotangent_ref.1) | copy-start | bytes 9220
  7.2 6.6 %copy-start.10 = (bf16[3,128]{1,0:T(4,128)(2,1)S(1)}, bf16[3,128]{1,0:T(4,128)(2,1)}, u32[]{:S(2)}) copy-start(bf16[3,128]{1,0:T(4,128)(2,1)} %position_ref.1) | copy-start | bytes 2308
  7.2 6.6 %copy-start.11 = (f32[128]{0:T(128)S(1)}, f32[128]{0:T(128)}, u32[]{:S(2)}) copy-start(f32[128]{0:T(128)} %gain_ref.6) | copy-start | bytes 1540
  7.2 6.6 %copy-start.12 = (s32[1,16]{1,0:T(1,128)S(1)}, s32[1,16]{1,0:T(1,128)}, u32[]{:S(2)}) copy-start(s32[1,16]{1,0:T(1,128)} %counts_ref.3) | copy-start | bytes 196
  17.4 16.8 %all-to-all-start = ((bf16[16,96,128]{2,1,0:T(8,128)(2,1)}), bf16[16,96,128]{2,1,0:T(8,128)(2,1)S(1)}, u32[]{:S(2)}, u32[]{:S(2)}) async-start(bf16[16,96,128]{2,1,0:T(8,128)(2,1)} %get-tuple-element.21.rest_2_), calls=%async_computation | async-start | bytes 786432 | tf_op jit(solution)/shard_map/all_to_all | solution.py:583
  35.1 16.8 %all-to-all-start.1 = ((bf16[8,304,128]{2,1,0:T(8,128)(2,1)}), bf16[8,304,128]{2,1,0:T(8,128)(2,1)S(1)}, u32[]{:S(2)}, u32[]{:S(2)}) async-start(bf16[8,304,128]{2,1,0:T(8,128)(2,1)} %pad_maximum_fusion.rest_2_), calls=%async_computation.1 | async-start | bytes 1245184 | tf_op jit(solution)/shard_map/all_to_all | solution.py:586
  40.6 11.3 %copy-start.13 = (bf16[768,768]{1,0:T(8,128)(2,1)S(1)}, bf16[768,768]{1,0:T(8,128)(2,1)}, u32[]{:S(2)}) copy-start(bf16[768,768]{1,0:T(8,128)(2,1)} %merge_ref.3) | copy-start | bytes 3538948
  40.6 11.3 %copy-start.14 = (bf16[768,128]{1,0:T(8,128)(2,1)S(1)}, bf16[768,128]{1,0:T(8,128)(2,1)}, u32[]{:S(2)}) copy-start(bf16[768,128]{1,0:T(8,128)(2,1)} %down_ref.3) | copy-start | bytes 589828
  51.9 20.8 %copy-start = (bf16[128,256,128]{2,1,0:T(8,128)(2,1)S(1)}, bf16[128,256,128]{2,1,0:T(8,128)(2,1)}, u32[]{:S(2)}) copy-start(bf16[128,256,128]{2,1,0:T(8,128)(2,1)} %get-tuple-element.30.standard_ref) | copy-start | bytes 25165828
  51.9 20.8 %copy-start.6 = (bf16[128,16]{0,1:T(8,128)(2,1)S(1)}, bf16[128,16]{0,1:T(8,128)(2,1)}, u32[]{:S(2)}) copy-start(bf16[128,16]{0,1:T(8,128)(2,1)} %param.28) | copy-start | bytes 12292
  51.9 20.8 %copy-start.9 = (f32[128]{0:T(128)S(1)}, f32[128]{0:T(128)}, u32[]{:S(2)}) copy-start(f32[128]{0:T(128)} %gain_ref.9) | copy-start | bytes 1540

commit v6 on v5

--- a/solution.py
+++ b/solution.py
@@ -573,7 +573,7 @@
     gain = pair_gain
     bias_turned = bias_weight.T
     groups = pair_state.shape[0] // GROUP
-    cuts = (0, groups // 4, groups * 5 // 8, groups)
+    cuts = (0, groups // 4, groups // 2, groups)
     pair_part = pair_forward(pair_state, gain, bias_turned, 0, cuts[1])
     hidden, state, packed, send = atom_stage(
         left, atom_feats, right, atom_gain, atom_project, atom_merge, atom_up,

time: 81.1 us -> 81.2 us (level)
    all_to_all x1, waiting for transfers between devices: 2.95 us -> 4.62 us  [per_device(): shared = lax.all_to_all(send, 'row', 0, 0)]
    all_to_all x1, waiting for transfers between devices: 4.76 us -> 3.52 us  [per_device(): gathered = lax.all_to_all(mixed, 'col', 0, 0)]
where the time goes in v6:
time: 81.2 us; the launch traced here: 80.7 us
  Pallas kernels  37.1 us (46%)
  starting transfers between devices  19.3 us (24%)
  blocking collectives  12.8 us (16%)
  waiting for transfers between devices  9.67 us (12%)
  other arithmetic  0.89 us (1%)
  between operations  0.84 us (1%)
    pallas_call x3, Pallas kernels, pair_forward(): pl.pallas_call(pair_kernel, grid=(count // PAIR_STACK,), in_specs=[pl.Blo...  17.6 us
    all_to_all x1, blocking collectives, per_device(): received = lax.all_to_all(payload, 'col', 0, 0)  12.8 us
    pallas_call x1, Pallas kernels, attend_stage(): pl.pallas_call(attend_kernel, grid=(steps,), in_specs=[whole(a) for a in...  8.1 us
    pallas_call x1, Pallas kernels, gradient_stage(): pl.pallas_call(gradient_kernel, grid=(rows // GROUP // STACK,), in_specs=...  7.86 us
    all_to_all x1, starting transfers between devices, per_device(): shared = lax.all_to_all(send, 'row', 0, 0)  7.29 us
    all_to_all x1, starting transfers between devices, per_device(): gathered = lax.all_to_all(mixed, 'col', 0, 0)  5.52 us
    ppermute x1, starting transfers between devices, per_device(): lax.ppermute(atom_feats, both, [(i, i + 1) for i in range(devices - 1)])  5.18 us
    all_to_all x1, waiting for transfers between devices, per_device(): shared = lax.all_to_all(send, 'row', 0, 0)  4.62 us
  transfers between devices with their start and end apart: 4, of which 3 were waited for; matrix products, arithmetic and copies ran while one was open for 0% of the time, Pallas kernels for 22%

profile of v6, /device:TPU:0, one launch (start us, length us, event | category | flops | bytes accessed | tf_op | source)
XLA Modules:
  0.0 80.7 jit_solution(6661807945505651412)
XLA Ops:
  0.6 5.2 %collective-permute-start = (bf16[256,128]{1,0:T(8,128)(2,1)}, bf16[256,128]{1,0:T(8,128)(2,1)S(1)}, u32[]{:S(2)}, u32[]{:S(2)}) collective-permute-start(bf16[256,128]{1,0:T(8,128)(2,1)} %own_ref.1), channel_id=1, source_target_pairs={{0,1},{1,2},{2,3},{3,4},{4,5},{5,6},{6,7},{7,8},{8,9},{9,10},{10,1... | collective-permute-start | bytes 196616 | tf_op jit(solution)/shard_map/ppermute | solution.py:572
  5.8 1.3 %collective-permute-start.1 = (bf16[256,128]{1,0:T(8,128)(2,1)}, bf16[256,128]{1,0:T(8,128)(2,1)S(1)}, u32[]{:S(2)}, u32[]{:S(2)}) collective-permute-start(bf16[256,128]{1,0:T(8,128)(2,1)} %own_ref.1), channel_id=1, source_target_pairs={{1,0},{2,1},{3,2},{4,3},{5,4},{6,5},{7,6},{8,7},{9,8},{10,9},{11,1... | collective-permute-start | bytes 196616 | tf_op jit(solution)/shard_map/ppermute | solution.py:571
  7.1 0.0 copy-start.1
  7.1 0.0 copy-start.2
  7.1 0.0 copy-start.3
  7.2 0.0 copy-start.4
  7.2 0.0 copy-start.5
  7.2 0.0 copy-start.6
  7.2 0.0 copy-start.7
  7.2 0.0 copy-start.9
  7.2 0.0 copy-start.10
  7.2 0.0 copy-start.11
  7.2 4.9 %pair_forward.3 = (f32[8,256,2048]{2,1,0:T(8,128)}, bf16[128,256,128]{2,1,0:T(8,128)(2,1)}) custom-call(bf16[128,256,128]{2,1,0:T(8,128)(2,1)} %x_ref.5, f32[128]{0:T(128)} %gain_ref.9, bf16[16,128]{1,0:T(8,128)(2,1)} %bitcast.2), custom_call_target="tpu_custom_call" | custom-call | flops 5242880000 | bytes 5242880 | tf_op jit(solution)/shard_map/pair_forward/pallas_call | solution.py:112
  12.2 0.0 collective-permute-done.left_ref
  12.2 1.5 %collective-permute-done.1.right_ref = bf16[256,128]{1,0:T(8,128)(2,1)S(1)} collective-permute-done((bf16[256,128]{1,0:T(8,128)(2,1)}, bf16[256,128]{1,0:T(8,128)(2,1)S(1)}, u32[]{:S(2)}, u32[]{:S(2)}) %collective-permute-start.1) | collective-permute-done | bytes 65568 | tf_op jit(solution)/shard_map/ppermute | solution.py:571
  13.7 0.0 copy-done.1
  13.7 0.0 copy-done.2
  13.7 0.0 copy-done.3
  13.7 0.0 copy-done.4
  13.7 0.0 copy-done.5
  13.7 0.0 copy-done.6
  13.7 0.0 copy-done.7
  13.7 0.0 copy-done.9
  13.8 0.0 copy-done.10
  13.8 0.0 copy-done.11
  13.8 3.6 %atom_stage.1 = (bf16[256,128]{1,0:T(8,128)(2,1)S(1)}, f32[16,768]{1,0:T(8,128)S(1)}, bf16[112,128]{1,0:T(8,128)(2,1)S(1)}, bf16[16,96,128]{2,1,0:T(8,128)(2,1)}) custom-call(bf16[256,128]{1,0:T(8,128)(2,1)S(1)} %collective-permute-done.left_ref, bf16[256,128]{1,0:T(8,128)(2,1)S(1)} %copy-done.3, bf16[256,128]{1,0:T(8,128)(2,1)S(1)} %collective-permute-done.1.right_ref, ...), custom_call_target="tpu_custom_call" | custom-call | flops 419430400 | bytes 2097152 | tf_op jit(solution)/shard_map/atom_stage/pallas_call | solution.py:223
  17.4 7.3 %all-to-all-start = ((bf16[16,96,128]{2,1,0:T(8,128)(2,1)}), bf16[16,96,128]{2,1,0:T(8,128)(2,1)S(1)}, u32[]{:S(2)}, u32[]{:S(2)}) async-start(bf16[16,96,128]{2,1,0:T(8,128)(2,1)} %get-tuple-element.21.rest_2_), calls=%async_computation | async-start | bytes 786432 | tf_op jit(solution)/shard_map/all_to_all | solution.py:583
  24.7 4.8 %pair_forward.4 = (f32[8,256,2048]{2,1,0:T(8,128)}, bf16[128,256,128]{2,1,0:T(8,128)(2,1)}) custom-call(bf16[128,256,128]{2,1,0:T(8,128)(2,1)} %x_ref.5, f32[128]{0:T(128)} %gain_ref.9, bf16[16,128]{1,0:T(8,128)(2,1)} %bitcast.3, f32[8,256,2048]{2,1,0:T(8,128)} %get-tuple-element.20._.rest_0_, ...), custom_call_target="tpu_custom_call", output_to_operand_aliasing={{0}: (3, {}), {1}: (4, {})} | custom-call | flops 5242880000 | bytes 5242880 | tf_op jit(solution)/shard_map/pair_forward/pallas_call | solution.py:112
  29.5 4.6 %all-to-all-done = bf16[16,96,128]{2,1,0:T(8,128)(2,1)S(1)} async-done(((bf16[16,96,128]{2,1,0:T(8,128)(2,1)}), bf16[16,96,128]{2,1,0:T(8,128)(2,1)S(1)}, u32[]{:S(2)}, u32[]{:S(2)}) %all-to-all-start) | async-done | bytes 393248 | tf_op jit(solution)/shard_map/all_to_all | solution.py:583
  34.2 0.9 %pad_maximum_fusion.rest_2_ = bf16[8,304,128]{2,1,0:T(8,128)(2,1)} fusion(bf16[8,112,128]{2,1,0:T(8,128)(2,1)S(1)} %broadcast_in_dim.2, bf16[8,192,128]{2,1,0:T(8,128)(2,1)S(1)} %bitcast.6), kind=kLoop, calls=%fused_computation | loop fusion | flops 1245184 | bytes 1245184 | tf_op jit(solution)/shard_map/concatenate | solution.py:585
  35.1 5.5 %all-to-all-start.1 = ((bf16[8,304,128]{2,1,0:T(8,128)(2,1)}), bf16[8,304,128]{2,1,0:T(8,128)(2,1)S(1)}, u32[]{:S(2)}, u32[]{:S(2)}) async-start(bf16[8,304,128]{2,1,0:T(8,128)(2,1)} %pad_maximum_fusion.rest_2_), calls=%async_computation.1 | async-start | bytes 1245184 | tf_op jit(solution)/shard_map/all_to_all | solution.py:586
  40.6 0.0 copy-start.13
  40.6 0.0 copy-start.14
  40.6 7.8 %pair_forward.5 = (f32[8,256,2048]{2,1,0:T(8,128)}, bf16[128,256,128]{2,1,0:T(8,128)(2,1)}) custom-call(bf16[128,256,128]{2,1,0:T(8,128)(2,1)} %x_ref.5, f32[128]{0:T(128)} %gain_ref.9, bf16[16,128]{1,0:T(8,128)(2,1)} %bitcast.4, f32[8,256,2048]{2,1,0:T(8,128)} %get-tuple-element.24.rest_0_, ...), custom_call_target="tpu_custom_call", output_to_operand_aliasing={{0}: (3, {}), {1}: (4, {})} | custom-call | flops 10485760000 | bytes 10485760 | tf_op jit(solution)/shard_map/pair_forward/pallas_call | solution.py:112
  48.4 3.5 %all-to-all-done.1.gathered_ref = bf16[8,304,128]{2,1,0:T(8,128)(2,1)S(1)} async-done(((bf16[8,304,128]{2,1,0:T(8,128)(2,1)}), bf16[8,304,128]{2,1,0:T(8,128)(2,1)S(1)}, u32[]{:S(2)}, u32[]{:S(2)}) %all-to-all-start.1) | async-done | bytes 622624 | tf_op jit(solution)/shard_map/all_to_all | solution.py:586
  51.9 0.0 copy-done.13
  51.9 0.0 copy-done.14
  51.9 0.0 copy-start
  51.9 0.0 copy-start.8
  51.9 0.0 copy-start.12
  52.0 8.1 %attend_stage.1 = (bf16[256,2048]{1,0:T(8,128)(2,1)S(1)}, f32[256,2048]{1,0:T(8,128)S(1)}, bf16[256,2048]{1,0:T(8,128)(2,1)S(1)}, bf16[8,176,128]{2,1,0:T(8,128)(2,1)S(1)}) custom-call(bf16[8,304,128]{2,1,0:T(8,128)(2,1)S(1)} %all-to-all-done.1.gathered_ref, bf16[768,128]{1,0:T(8,128)(2,1)S(1)} %copy-done.14, bf16[768,2304]{1,0:T(8,128)(2,1)} %project_hbm.1, ...), custom_call_target="tpu_custom_call" | custom-call | flops 8388608000 | bytes 12582912 | tf_op jit(solution)/shard_map/attend_stage/pallas_call | solution.py:358
  60.1 12.8 %all_to_all.15.received_ref = bf16[8,176,128]{2,1,0:T(8,128)(2,1)S(1)} all-to-all(bf16[8,176,128]{2,1,0:T(8,128)(2,1)S(1)} %get-tuple-element.31.own_ref), channel_id=1, replica_groups=mesh['row'=16,'col'=8] {'col'}, dimensions={0} | all-to-all | bytes 720896 | tf_op jit(solution)/shard_map/all_to_all | solution.py:593
  72.9 0.0 copy-done
  72.9 0.0 copy-done.8
  72.9 0.0 copy-done.12
  72.9 7.9 %gradient_stage.1 = (bf16[128,256,128]{2,1,0:T(8,128)(2,1)}, f32[3,256]{1,0:T(4,128)}, bf16[16,768]{1,0:T(8,128)(2,1)}) custom-call(bf16[256,2048]{1,0:T(8,128)(2,1)S(1)} %get-tuple-element.27.weight_ref, f32[256,2048]{1,0:T(8,128)S(1)} %get-tuple-element.28.grad_ref, bf16[256,2048]{1,0:T(8,128)(2,1)S(1)} %get-tuple-element.29.small_ref, ...), custom_call_target="tpu_custom_call" | custom-call | flops 16777216000 | bytes 23068672 | tf_op jit(solution)/shard_map/gradient_stage/pallas_call | solution.py:543
  (1 shorter events, 0.0 us)
Async XLA Ops:
  0.6 11.5 %collective-permute-start = (bf16[256,128]{1,0:T(8,128)(2,1)}, bf16[256,128]{1,0:T(8,128)(2,1)S(1)}, u32[]{:S(2)}, u32[]{:S(2)}) collective-permute-start(bf16[256,128]{1,0:T(8,128)(2,1)} %own_ref.1), channel_id=1, source_target_pairs={{0,1},{1,2},{2,3},{3,4},{4,5},{5,6},{6,7},{7,8},{8,9},{9,10},{10,1... | collective-permute-start | bytes 196616 | tf_op jit(solution)/shard_map/ppermute | solution.py:572
  5.8 7.9 %collective-permute-start.1 = (bf16[256,128]{1,0:T(8,128)(2,1)}, bf16[256,128]{1,0:T(8,128)(2,1)S(1)}, u32[]{:S(2)}, u32[]{:S(2)}) collective-permute-start(bf16[256,128]{1,0:T(8,128)(2,1)} %own_ref.1), channel_id=1, source_target_pairs={{1,0},{2,1},{3,2},{4,3},{5,4},{6,5},{7,6},{8,7},{9,8},{10,9},{11,1... | collective-permute-start | bytes 196616 | tf_op jit(solution)/shard_map/ppermute | solution.py:571
  7.1 6.6 %copy-start.1 = (bf16[128,768]{1,0:T(8,128)(2,1)S(1)}, bf16[128,768]{1,0:T(8,128)(2,1)}, u32[]{:S(2)}) copy-start(bf16[128,768]{1,0:T(8,128)(2,1)} %up_ref.1) | copy-start | bytes 589828
  7.1 6.6 %copy-start.2 = (bf16[128,384]{1,0:T(8,128)(2,1)S(1)}, bf16[128,384]{1,0:T(8,128)(2,1)}, u32[]{:S(2)}) copy-start(bf16[128,384]{1,0:T(8,128)(2,1)} %project_ref.1) | copy-start | bytes 294916
  7.1 6.6 %copy-start.3 = (bf16[256,128]{1,0:T(8,128)(2,1)S(1)}, bf16[256,128]{1,0:T(8,128)(2,1)}, u32[]{:S(2)}) copy-start(bf16[256,128]{1,0:T(8,128)(2,1)} %own_ref.1) | copy-start | bytes 196612
  7.2 6.6 %copy-start.4 = (bf16[128,128]{1,0:T(8,128)(2,1)S(1)}, bf16[128,128]{1,0:T(8,128)(2,1)}, u32[]{:S(2)}) copy-start(bf16[128,128]{1,0:T(8,128)(2,1)} %merge_ref.2) | copy-start | bytes 98308
  7.2 6.6 %copy-start.5 = (bf16[16,768]{1,0:T(8,128)(2,1)S(1)}, bf16[16,768]{1,0:T(8,128)(2,1)}, u32[]{:S(2)}) copy-start(bf16[16,768]{1,0:T(8,128)(2,1)} %single_ref.1) | copy-start | bytes 73732
  7.2 6.6 %copy-start.6 = (f32[768]{0:T(1024)S(1)}, f32[768]{0:T(1024)}, u32[]{:S(2)}) copy-start(f32[768]{0:T(1024)} %token_gain_ref.1) | copy-start | bytes 9220
  7.2 6.6 %copy-start.7 = (f32[3,256]{1,0:T(4,128)S(1)}, f32[3,256]{1,0:T(4,128)}, u32[]{:S(2)}) copy-start(f32[3,256]{1,0:T(4,128)} %cotangent_ref.1) | copy-start | bytes 9220
  7.2 6.6 %copy-start.9 = (bf16[3,128]{1,0:T(4,128)(2,1)S(1)}, bf16[3,128]{1,0:T(4,128)(2,1)}, u32[]{:S(2)}) copy-start(bf16[3,128]{1,0:T(4,128)(2,1)} %position_ref.1) | copy-start | bytes 2308
  7.2 6.6 %copy-start.10 = (f32[128]{0:T(128)S(1)}, f32[128]{0:T(128)}, u32[]{:S(2)}) copy-start(f32[128]{0:T(128)} %gain_ref.6) | copy-start | bytes 1540
  7.2 6.6 %copy-start.11 = (s32[1,16]{1,0:T(1,128)S(1)}, s32[1,16]{1,0:T(1,128)}, u32[]{:S(2)}) copy-start(s32[1,16]{1,0:T(1,128)} %counts_ref.3) | copy-start | bytes 196
  17.4 16.8 %all-to-all-start = ((bf16[16,96,128]{2,1,0:T(8,128)(2,1)}), bf16[16,96,128]{2,1,0:T(8,128)(2,1)S(1)}, u32[]{:S(2)}, u32[]{:S(2)}) async-start(bf16[16,96,128]{2,1,0:T(8,128)(2,1)} %get-tuple-element.21.rest_2_), calls=%async_computation | async-start | bytes 786432 | tf_op jit(solution)/shard_map/all_to_all | solution.py:583
  35.1 16.8 %all-to-all-start.1 = ((bf16[8,304,128]{2,1,0:T(8,128)(2,1)}), bf16[8,304,128]{2,1,0:T(8,128)(2,1)S(1)}, u32[]{:S(2)}, u32[]{:S(2)}) async-start(bf16[8,304,128]{2,1,0:T(8,128)(2,1)} %pad_maximum_fusion.rest_2_), calls=%async_computation.1 | async-start | bytes 1245184 | tf_op jit(solution)/shard_map/all_to_all | solution.py:586
  40.6 11.3 %copy-start.13 = (bf16[768,768]{1,0:T(8,128)(2,1)S(1)}, bf16[768,768]{1,0:T(8,128)(2,1)}, u32[]{:S(2)}) copy-start(bf16[768,768]{1,0:T(8,128)(2,1)} %merge_ref.3) | copy-start | bytes 3538948
  40.6 11.3 %copy-start.14 = (bf16[768,128]{1,0:T(8,128)(2,1)S(1)}, bf16[768,128]{1,0:T(8,128)(2,1)}, u32[]{:S(2)}) copy-start(bf16[768,128]{1,0:T(8,128)(2,1)} %down_ref.3) | copy-start | bytes 589828
  51.9 20.9 %copy-start = (bf16[128,256,128]{2,1,0:T(8,128)(2,1)S(1)}, bf16[128,256,128]{2,1,0:T(8,128)(2,1)}, u32[]{:S(2)}) copy-start(bf16[128,256,128]{2,1,0:T(8,128)(2,1)} %get-tuple-element.30.standard_ref) | copy-start | bytes 25165828
  51.9 20.9 %copy-start.8 = (bf16[128,16]{0,1:T(8,128)(2,1)S(1)}, bf16[128,16]{0,1:T(8,128)(2,1)}, u32[]{:S(2)}) copy-start(bf16[128,16]{0,1:T(8,128)(2,1)} %param.28) | copy-start | bytes 12292
  51.9 20.9 %copy-start.12 = (f32[128]{0:T(128)S(1)}, f32[128]{0:T(128)}, u32[]{:S(2)}) copy-start(f32[128]{0:T(128)} %gain_ref.9) | copy-start | bytes 1540
